TPU v7x, 256 devices: a whole 4x4x8 slice. The times are simulated.
256 devices in a mesh: liq: 4 (over x), ill: 8 (over y, core), dur: 8 (over z).
Axes of the slice: x: 4, y: 4, z: 8, core: 2. Of those that a mesh axis runs over, the one named last changes fastest.
Arguments:
- marginal_value: float32 [32, 16, 16, 512], P(None, 'dur', 'ill', 'liq'), may hold values from 0.5 to 2
- transition: float32 [32, 32], replicated, may hold values from 0 to 1, as said below
- discount_shock: float32 [32], replicated, may hold values from 0.5 to 2
- illiquid_drift: float32 [16], P('ill'), may hold values from 0.2 to 0.8
- durable_keep: float32 [16], P('dur'), may hold values from 0.3 to 0.9
- bracket_index: int32 [32, 16, 16, 512], P(None, 'dur', 'ill', 'liq'), may hold values from 0 to 510
- bracket_weight: float32 [32, 16, 16, 512], P(None, 'dur', 'ill', 'liq'), may hold values from 0 to 1
- steady_consumption: float32 [32, 16, 16, 512], P(None, 'dur', 'ill', 'liq'), may hold values from 0.8 to 1.6
- lottery_weight: float32 [32, 16, 16, 512], P(None, 'dur', 'ill', 'liq'), may hold values from 0 to 1
- liquid_target: int32 [32, 16, 16, 512], P(None, 'dur', 'ill', 'liq'), may hold values from 0 to 510
- illiquid_target: int32 [32, 16, 16], P(None, 'dur', 'ill'), may hold values from 0 to 15
- population: float32 [32, 16, 16, 512], P(None, 'dur', 'ill', 'liq'), may hold values from 0.5 to 2
Outputs:
- consumption: float32 [32, 16, 16, 512], P(None, 'dur', 'ill', 'liq')
- population_next: float32 [32, 16, 16, 512], P(None, 'dur', 'ill', 'liq')
Inputs may be any that keep to these rules, and one draw needn't show every extreme that they name: `bracket_index`: global liquid index; the upper bracket point is index + 1. `liquid_target`: global liquid index; the upper target is index + 1. `illiquid_target`: global illiquid index. `transition`: entries positive, every row sums to one.
All inputs are finite; a program needn't handle non-finite values.
Results may differ from a plain program's by a relative error of at most 0.000065.
Values sent between devices are 32-bit elements; how exact they have to be, the bound alone decides.
No kernel may reach another device: no remote copies, remote signals or barrier semaphores. Data moves between devices by JAX's collectives and lax.ppermute only.
A program may use at most 64 MiB of HBM per device.

v0:
```python
import jax
import jax.numpy as jnp
from jax import lax
from jax.sharding import PartitionSpec as P

DISCOUNT = 0.96
GROSS_RATE = 1.01
SLOPE_GAIN = 0.5
HIGHEST_PREC = lax.Precision.HIGHEST


def passed_along(block, axis, distance):
    devices = range(lax.axis_size(axis))
    route = [(i - distance, i) for i in devices if i - distance in devices]
    return lax.ppermute(block, axis, route)


def copy_for_each(x, axis):
    peers = lax.axis_size(axis)
    return lax.all_to_all(jnp.broadcast_to(x[None], (peers, *x.shape)), axis, 0, 0, tiled=True)


def in_order(pieces, dim):
    pieces = jnp.moveaxis(pieces, 0, dim)
    lengths = pieces.shape
    return pieces.reshape(*lengths[:dim], lengths[dim] * lengths[dim + 1], *lengths[dim + 2 :])


def collect(x, axis, dim):
    pieces = copy_for_each(x, axis)
    return in_order(pieces, dim)


def cut_along(x, dim, peers):
    lengths = x.shape
    pieces = x.reshape(*lengths[:dim], peers, lengths[dim] // peers, *lengths[dim + 1 :])
    return jnp.moveaxis(pieces, dim, 0)


def sum_at_owner(x, axis, dim):
    peers = lax.axis_size(axis)
    pieces = lax.all_to_all(cut_along(x, dim, peers), axis, 0, 0, tiled=True)
    return jnp.sum(pieces, axis=0)


def expect_upper(values, transition, drift_rate):
    expected = jnp.einsum("zy,ydab->zdab", transition, values, precision=HIGHEST_PREC)
    above_plane = passed_along(expected[:, :, :1, :], "ill", -1)
    is_last = lax.axis_index("ill") == lax.axis_size("ill") - 1
    above_plane = jnp.where(is_last, expected[:, :, -1:, :], above_plane)
    upper_plane = jnp.concatenate([expected[:, :, 1:, :], above_plane], axis=2)
    drift_full = drift_rate[None, None, :, None]
    return drift_full * expected + (1.0 - drift_full) * upper_plane


def backward_step(values, transition, drift_rate, shock_scale, both_index, bracket_weight):
    drifted = expect_upper(values, transition, drift_rate)
    endogenous = lax.rsqrt(DISCOUNT * GROSS_RATE * shock_scale[:, None, None, None] * drifted)
    pencil = collect(endogenous, "liq", 3)
    liq_rows = bracket_weight.shape[3]
    picked = jnp.take_along_axis(pencil, both_index, axis=3)
    lower_value = picked[:, :, :, :liq_rows]
    upper_value = picked[:, :, :, liq_rows:]
    return bracket_weight * lower_value + (1.0 - bracket_weight) * upper_value


def scatter_pair(size, index_low, index_high, mass_low, mass_high):
    flat_index = jnp.concatenate([index_low.reshape(-1), index_high.reshape(-1)])
    flat_value = jnp.concatenate([mass_low.reshape(-1), mass_high.reshape(-1)])
    return jnp.zeros((size,), jnp.float32).at[flat_index].add(flat_value)


def joint_terms(population, share, liquid_target, illiquid_target, liq_count, ill_count):
    incomes, durables, ill_rows, liq_rows = population.shape
    inc_idx = lax.broadcasted_iota(jnp.int32, population.shape, 0)
    dur_idx = lax.broadcasted_iota(jnp.int32, population.shape, 1)
    ill_dest = jnp.broadcast_to(illiquid_target[:, :, :, None], population.shape)
    owner_ill = ill_dest // ill_rows
    local_ill = ill_dest % ill_rows

    def flat_index(target):
        owner_block = target // liq_rows * ill_count + owner_ill
        return (
            ((owner_block * incomes + inc_idx) * durables + dur_idx) * ill_rows + local_ill
        ) * liq_rows + target % liq_rows

    total = liq_count * ill_count * incomes * durables * ill_rows * liq_rows
    flat_mass = scatter_pair(
        total,
        flat_index(liquid_target),
        flat_index(liquid_target + 1),
        population * share,
        population * (1.0 - share),
    )
    return flat_mass.reshape(liq_count * ill_count * incomes, durables, ill_rows, liq_rows)


def body(
    marginal_value,
    transition,
    discount_shock,
    illiquid_drift,
    durable_keep,
    bracket_index,
    bracket_weight,
    steady_consumption,
    lottery_weight,
    liquid_target,
    illiquid_target,
    population,
):
    both_index = jnp.concatenate([bracket_index, bracket_index + 1], axis=3)
    policy_one = backward_step(
        marginal_value, transition, illiquid_drift, discount_shock, both_index, bracket_weight
    )
    value_two = GROSS_RATE / (policy_one * policy_one)
    consumption = backward_step(
        value_two,
        transition,
        illiquid_drift,
        jnp.ones_like(discount_shock),
        both_index,
        bracket_weight,
    )
    share = jnp.clip(lottery_weight + SLOPE_GAIN * (policy_one - steady_consumption), 0.0, 1.0)
    liq_count = lax.axis_size("liq")
    ill_count = lax.axis_size("ill")
    income_half = population.shape[0] // 2
    halves = []
    for half_idx in range(2):
        picked = slice(half_idx * income_half, (half_idx + 1) * income_half)
        terms = joint_terms(
            population[picked],
            share[picked],
            liquid_target[picked],
            illiquid_target[picked],
            liq_count,
            ill_count,
        )
        halves.append(sum_at_owner(terms, ("liq", "ill"), 0))
    lottery_mass = jnp.concatenate(halves, axis=0)
    durables = population.shape[1]
    dur_plane = lax.axis_index("dur") * durables + lax.broadcasted_iota(jnp.int32, (durables,), 0)
    stay_share = jnp.where(dur_plane == 0, 1.0, durable_keep)[None, :, None, None]
    depart = (1.0 - stay_share) * lottery_mass
    incoming = passed_along(depart[:, :1], "dur", -1)
    settled = stay_share * lottery_mass + jnp.concatenate([depart[:, 1:], incoming], axis=1)
    population_next = jnp.einsum("zy,zdab->ydab", transition, settled, precision=HIGHEST_PREC)
    return (consumption, population_next)


def solution(mesh):
    in_specs = (
        P(None, "dur", "ill", "liq"),
        P(),
        P(),
        P("ill"),
        P("dur"),
        P(None, "dur", "ill", "liq"),
        P(None, "dur", "ill", "liq"),
        P(None, "dur", "ill", "liq"),
        P(None, "dur", "ill", "liq"),
        P(None, "dur", "ill", "liq"),
        P(None, "dur", "ill"),
        P(None, "dur", "ill", "liq"),
    )
    out_specs = (P(None, "dur", "ill", "liq"), P(None, "dur", "ill", "liq"))
    return jax.shard_map(body, mesh=mesh, in_specs=in_specs, out_specs=out_specs, check_vma=False)
```

profile of v0, /device:TPU:96, one launch (start us, length us, event | category | flops | bytes accessed | tf_op | source)
XLA Modules:
  0.0 962.6 jit_solution(2422771263683891310)
XLA Ops:
  0.6 0.0 copy-start
  0.6 0.0 copy-start.7
  0.7 0.8 copy-done
  1.5 0.9 fusion.15
  2.4 1.3 collective-permute-start
  3.7 0.8 broadcast_add_fusion.3
  4.5 0.1 copy.118
  4.6 0.8 compare_and_fusion.2
  5.5 0.1 copy.111
  5.6 0.7 broadcast_subtract_fusion.1
  6.2 0.1 copy.116
  6.3 0.1 copy.113
  6.5 0.1 copy.117
  6.5 0.1 copy.115
  6.6 0.1 copy.114
  6.7 0.1 copy.110
  6.8 0.1 copy.109
  6.9 0.1 copy.108
  7.0 0.1 copy.107
  7.1 0.1 copy.106
  7.3 1.5 fusion.39
  8.8 0.1 compare_select_fusion.2
  8.8 0.7 broadcast_multiply_fusion.1
  9.5 0.0 collective-permute-done
  9.5 0.1 fusion.8
  9.6 0.7 broadcast_in_dim.55
  10.4 4.3 all-to-all-start
  14.7 0.2 bitcast_or_fusion
  14.9 0.1 copy.129
  14.9 7.7 all-to-all-done
  22.6 0.0 copy-start.2
  22.6 0.0 copy-start.4
  22.7 0.0 copy-start.5
  22.7 366.2 %gather_fusion = f32[32768]{0:T(1024)S(1)} fusion(f32[32,2,2,512]{3,0,2,1:T(8,128)S(1)} %copy_bitcast_fusion.1, s32[32768]{0:T(1024)S(1)} %bitcast.44), kind=kCustom, calls=%fused_computation.clone | custom fusion | bytes 786432 | tf_op jit(solution)/shard_map/jit(take_along_axis)/gather | solution.py:61
  388.9 0.0 copy-start.3
  388.9 0.0 copy-start.6
  388.9 0.1 reshape.265
  389.0 0.2 broadcast_select_fusion.1
  389.2 0.1 add_clamp_fusion
  389.4 0.2 copy-done.3
  389.6 0.2 convolution_bitcast_fusion.1
  389.8 1.3 collective-permute-start.1
  391.1 0.1 slice_multiply_fusion.4
  391.2 1.7 collective-permute-done.1
  392.9 0.1 fusion.11
  393.0 0.7 broadcast_in_dim.56
  393.8 3.4 all-to-all-start.1
  397.2 86.8 %scatter_custom_fusion = f32[262144]{0:T(1024)} fusion(s32[16384]{0:T(1024)S(1)} %bitcast.55, f32[16384]{0:T(1024)S(1)} %pad_maximum_fusion, f32[]{:T(128)} %constant.136.clone.1), kind=kCustom, calls=%fused_computation.8 | custom fusion | flops 16384 | bytes 1048580 | tf_op jit(solution)/shard_map/scatter-add | solution.py:70
  484.0 8.9 all-to-all-start.2
  492.9 0.1 compare_select_fusion.1
  493.0 86.8 %scatter_custom_fusion.1 = f32[262144]{0:T(1024)} fusion(s32[16384]{0:T(1024)S(1)} %bitcast.56, f32[16384]{0:T(1024)S(1)} %pad_maximum_fusion.1, f32[]{:T(128)} %constant.136.clone.1), kind=kCustom, calls=%fused_computation.6 | custom fusion | flops 16384 | bytes 1048580 | tf_op jit(solution)/shard_map/scatter-add | solution.py:70
  579.8 0.0 all-to-all-done.2
  579.9 7.5 all-to-all-start.3
  587.4 366.2 %gather_fusion.1 = f32[32768]{0:T(1024)S(1)} fusion(f32[32,2,2,512]{3,0,2,1:T(8,128)S(1)} %copy_bitcast_fusion, s32[32768]{0:T(1024)S(1)} %bitcast.45), kind=kCustom, calls=%fused_computation.1.clone | custom fusion | bytes 786432 | tf_op jit(solution)/shard_map/jit(take_along_axis)/gather | solution.py:61
  953.7 0.1 reshape.270
  953.7 0.1 broadcast_select_fusion
  953.9 0.3 reduce_sum.18
  954.2 0.3 reduce_sum.19
  954.6 0.1 broadcast_multiply_fusion
  954.6 2.0 collective-permute-start.2
  956.7 0.7 fusion.4
  957.4 4.3 collective-permute-done.2
  961.7 0.3 convolution_bitcast_fusion
  961.9 0.7 copy.121
  (25 shorter events, 0.2 us)
Async XLA Ops:
  0.6 0.8 copy-start
  0.6 8.9 copy-start.7
  0.7 14.0 %copy-start.1 = (s32[32,2,2,128]{3,2,1,0:T(2,128)S(1)}, s32[32,2,2,128]{3,2,1,0:T(2,128)}, u32[]{:S(2)}) copy-start(s32[32,2,2,128]{3,2,1,0:T(2,128)} %param.19) | copy-start | bytes 196612
  2.4 7.1 collective-permute-start
  10.4 12.3 %all-to-all-start = ((f32[4,32,2,2,128]{4,1,3,2,0:T(8,128)}), f32[4,32,2,2,128]{4,1,3,2,0:T(8,128)S(1)}, u32[]{:S(2)}, u32[]{:S(2)}) async-start(f32[4,32,2,2,128]{4,1,3,2,0:T(8,128)} %broadcast_in_dim.55), calls=%async_computation | async-start | bytes 524288 | tf_op jit(solution)/shard_map/all_to_all | solution.py:20
  22.6 366.6 %copy-start.2 = (f32[32,2,2,128]{3,2,1,0:T(2,128)S(1)}, f32[32,2,2,128]{3,2,1,0:T(2,128)}, u32[]{:S(2)}) copy-start(f32[32,2,2,128]{3,2,1,0:T(2,128)} %param.20) | copy-start | bytes 196612
  22.6 366.6 %copy-start.4 = (f32[32,2,2,128]{3,2,1,0:T(2,128)S(1)}, f32[32,2,2,128]{3,2,1,0:T(2,128)}, u32[]{:S(2)}) copy-start(f32[32,2,2,128]{3,2,1,0:T(2,128)} %param.22) | copy-start | bytes 196612
  22.7 366.5 %copy-start.5 = (f32[32,2,2,128]{3,2,1,0:T(2,128)S(1)}, f32[32,2,2,128]{3,2,1,0:T(2,128)}, u32[]{:S(2)}) copy-start(f32[32,2,2,128]{3,2,1,0:T(2,128)} %param.21) | copy-start | bytes 196612
  388.9 0.7 copy-start.3
  388.9 2.2 copy-start.6
  389.8 3.1 collective-permute-start.1
  393.8 90.3 %all-to-all-start.1 = ((f32[4,32,2,2,128]{4,1,3,2,0:T(8,128)}), f32[4,32,2,2,128]{4,1,3,2,0:T(8,128)S(1)}, u32[]{:S(2)}, u32[]{:S(2)}) async-start(f32[4,32,2,2,128]{4,1,3,2,0:T(8,128)} %broadcast_in_dim.56), calls=%async_computation.1 | async-start | bytes 524288 | tf_op jit(solution)/shard_map/all_to_all | solution.py:20
  484.0 95.8 %all-to-all-start.2 = ((f32[32,16,2,2,128]{4,3,2,1,0:T(2,128)}), f32[32,16,2,2,128]{4,3,2,1,0:T(2,128)S(1)}, u32[]{:S(2)}, u32[]{:S(2)}) async-start(f32[32,16,2,2,128]{4,3,2,1,0:T(2,128)} %bitcast.12), calls=%async_computation.2 | async-start | bytes 2097152 | tf_op jit(solution)/shard_map/all_to_all | solution.py:42
  579.9 7.5 copy-start.8
  579.9 374.4 %all-to-all-start.3 = ((f32[32,16,2,2,128]{4,3,2,1,0:T(2,128)}), f32[32,16,2,2,128]{4,3,2,1,0:T(2,128)S(1)}, u32[]{:S(2)}, u32[]{:S(2)}) async-start(f32[32,16,2,2,128]{4,3,2,1,0:T(2,128)} %bitcast.18), calls=%async_computation.3 | async-start | bytes 2097152 | tf_op jit(solution)/shard_map/all_to_all | solution.py:42
  954.6 7.0 collective-permute-start.2
where the time goes:
time: 964 us; the launch traced here: 963 us
  local copies, waits for them, and re-layouts  737 us (76%)
  other arithmetic  181 us (19%)
  starting transfers between devices  28.7 us (3%)
  waiting for transfers between devices  13.7 us (1%)
    gather x4, local copies, waits for them, and re-layouts, backward_step(): picked = jnp.take_along_axis(pencil, both_index, axis=3)  733 us
    scatter-add x2, other arithmetic, scatter_pair(): return jnp.zeros((size,), jnp.float32).at[flat_index].add(flat_value)  174 us
  transfers between devices with their start and end apart: 7, of which 3 were waited for; matrix products, arithmetic and copies ran while one was open for 57% of the time, Pallas kernels for 0%

commit v1 on v0

v1 whole, which is shorter than its diff:
```python
import functools

import jax
import jax.numpy as jnp
from jax import lax
from jax.experimental import pallas as pl
from jax.experimental.pallas import tpu as pltpu
from jax.sharding import PartitionSpec as P

DISCOUNT = 0.96
GROSS_RATE = 1.01
SLOPE_GAIN = 0.5
HIGHEST_PREC = lax.Precision.HIGHEST

Z = 32
LANES = 128
PLANE_ROWS = 4 * Z
HALF_ROWS = 2 * Z
VMEM = pltpu.VMEM
SMEM = pltpu.SMEM


def plane_of(ref, a, d):
    return ref[pl.ds(2 * d + a, Z, stride=4), :]


def dot_full(left, right):
    return jnp.dot(left, right, precision=HIGHEST_PREC, preferred_element_type=jnp.float32)


def split_lanes(wide, count):
    return [wide[:, i * LANES : (i + 1) * LANES] for i in range(count)]


def expect_kernel(value_ref, transition_ref, shock_ref, expected_ref):
    rows = lax.broadcasted_iota(jnp.int32, (Z, Z), 0)
    cols = lax.broadcasted_iota(jnp.int32, (Z, Z), 1)
    scale = jnp.where(rows == cols, shock_ref[...] * (DISCOUNT * GROSS_RATE), 0.0)
    scaled = dot_full(scale, transition_ref[...])
    planes = [plane_of(value_ref, p // 2, p % 2) for p in range(4)]
    expected = dot_full(scaled, jnp.concatenate(planes, axis=1))
    for p, plane in enumerate(split_lanes(expected, 4)):
        expected_ref[p * Z : (p + 1) * Z, :] = plane


def interpolate(pieces, index, weight, me):
    upper_index = index + 1
    quarter = ((index >> 7) - me) & 3
    upper_quarter = ((upper_index >> 7) - me) & 3
    lane = index & 127
    upper_lane = upper_index & 127
    lower = upper = None
    for q, piece in enumerate(pieces):
        low = jnp.take_along_axis(piece, lane, axis=1, mode="promise_in_bounds")
        high = jnp.take_along_axis(piece, upper_lane, axis=1, mode="promise_in_bounds")
        lower = low if lower is None else jnp.where(quarter == q, low, lower)
        upper = high if upper is None else jnp.where(upper_quarter == q, high, upper)
    return weight * lower + (1.0 - weight) * upper


def policy_plane(own, above, drift, index, weight, me):
    endogenous = [lax.rsqrt(drift * o + (1.0 - drift) * u) for o, u in zip(own, above)]
    return interpolate(endogenous, index, weight, me)


def forward_half(
    a, own, above, drift, me, transition_ref,
    index_ref, weight_ref, steady_ref, lottery_ref, target_ref, population_ref,
    mass_scr, row_scr,
):
    values = []
    for d in range(2):
        index = plane_of(index_ref, a, d)
        weight = plane_of(weight_ref, a, d)
        policy = policy_plane(own[d], above[d], drift, index, weight, me)
        values.append(GROSS_RATE / (policy * policy))
        share = plane_of(lottery_ref, a, d) + SLOPE_GAIN * (policy - plane_of(steady_ref, a, d))
        share = jnp.clip(share, 0.0, 1.0)
        population = plane_of(population_ref, a, d)
        rows = slice(d * Z, (d + 1) * Z)
        mass_scr[0, rows, :] = population * share
        mass_scr[1, rows, :] = population * (1.0 - share)
    scaled = transition_ref[...] * (DISCOUNT * GROSS_RATE)
    expected = split_lanes(dot_full(scaled, jnp.concatenate(values, axis=1)), 2)

    sub8 = lax.broadcasted_iota(jnp.int32, (8, LANES), 0)
    is_low = sub8 < 4
    sub_quarter = sub8 & 3
    sub128 = lax.broadcasted_iota(jnp.int32, (LANES, LANES), 0)
    for d in range(2):
        for z in range(Z):
            row = d * Z + z
            target = target_ref[pl.ds(4 * z + 2 * d + a, 1), :]
            quarter = ((target >> 7) - me) & 3
            hot = jnp.where(sub128 == (target & 127), 1.0, 0.0).astype(jnp.bfloat16)
            mass = jnp.where(is_low, mass_scr[0, row : row + 1, :], mass_scr[1, row : row + 1, :])
            mass = jnp.where(quarter == sub_quarter, mass, 0.0)
            first = mass.astype(jnp.bfloat16)
            rest = mass - first.astype(jnp.float32)
            both = jnp.concatenate([mass, rest], axis=0).astype(jnp.bfloat16)
            out = lax.dot_general(both, hot, (((1,), (1,)), ((), ())), preferred_element_type=jnp.float32)
            row_scr[row * 8 : row * 8 + 8, :] = out[:8] + out[8:]
    lane = lax.broadcasted_iota(jnp.int32, (HALF_ROWS, LANES), 1)
    low = [row_scr[pl.ds(q, HALF_ROWS, stride=8), :] for q in range(4)]
    high = [pltpu.roll(row_scr[pl.ds(4 + q, HALF_ROWS, stride=8), :], 1, 1) for q in range(4)]
    rows_by_quarter = [low[q] + jnp.where(lane == 0, high[(q + 3) % 4], high[q]) for q in range(4)]
    return expected, rows_by_quarter


def rows_of(refs, p):
    return [ref[p * Z : (p + 1) * Z, :] for ref in refs]


def first_half_kernel(
    ints_ref, floats_ref, e0, e1, e2, e3, transition_ref, index_ref, weight_ref, steady_ref, lottery_ref, target_ref,
    population_ref, out_ref, mass_scr, row_scr,
):
    pieces = (e0, e1, e2, e3)
    expected, by_quarter = forward_half(
        0, [rows_of(pieces, 0), rows_of(pieces, 1)], [rows_of(pieces, 2), rows_of(pieces, 3)], floats_ref[0],
        ints_ref[0], transition_ref, index_ref, weight_ref, steady_ref, lottery_ref, target_ref, population_ref,
        mass_scr, row_scr,
    )
    for q in range(4):
        out_ref[q * HALF_ROWS : (q + 1) * HALF_ROWS, :] = by_quarter[q]
    for d in range(2):
        out_ref[4 * HALF_ROWS + d * Z : 4 * HALF_ROWS + (d + 1) * Z, :] = expected[d]


def second_half_kernel(
    ints_ref, floats_ref, e0, e1, e2, e3, halo_ref, first_ref, transition_ref, index_ref, weight_ref, steady_ref,
    lottery_ref, target_ref, population_ref, p0, p1, p2, p3, mass_scr, row_scr,
):
    pieces = (e0, e1, e2, e3)
    above = [[halo_ref[q * HALF_ROWS + d * Z : q * HALF_ROWS + (d + 1) * Z, :] for q in range(4)] for d in range(2)]
    expected, by_quarter = forward_half(
        1, [rows_of(pieces, 2), rows_of(pieces, 3)], above, floats_ref[1],
        ints_ref[0], transition_ref, index_ref, weight_ref, steady_ref, lottery_ref, target_ref, population_ref,
        mass_scr, row_scr,
    )
    for q, out in enumerate((p0, p1, p2, p3)):
        out[:HALF_ROWS, :] = first_ref[q * HALF_ROWS : (q + 1) * HALF_ROWS, :]
        out[HALF_ROWS : 2 * HALF_ROWS, :] = by_quarter[q]
        out[2 * HALF_ROWS : 3 * HALF_ROWS, :] = first_ref[4 * HALF_ROWS :, :]
        for d in range(2):
            out[3 * HALF_ROWS + d * Z : 3 * HALF_ROWS + (d + 1) * Z, :] = expected[d]


def consume_kernel(ints_ref, floats_ref, e0, e1, e2, e3, halo_ref, index_ref, weight_ref, out_ref):
    pieces = (e0, e1, e2, e3)
    for a in range(2):
        for d in range(2):
            own = [ref[PLANE_ROWS + (2 * a + d) * Z : PLANE_ROWS + (2 * a + d + 1) * Z, :] for ref in pieces]
            if a == 0:
                above = [ref[PLANE_ROWS + (2 + d) * Z : PLANE_ROWS + (3 + d) * Z, :] for ref in pieces]
            else:
                above = [halo_ref[q * HALF_ROWS + d * Z : q * HALF_ROWS + (d + 1) * Z, :] for q in range(4)]
            policy = policy_plane(
                own, above, floats_ref[a], plane_of(index_ref, a, d), plane_of(weight_ref, a, d), ints_ref[0]
            )
            out_ref[pl.ds(2 * d + a, Z, stride=4), :] = policy


def gather_mass_kernel(floats_ref, p0, p1, p2, p3, ill_ref, core_out, dur_out):
    total = p0[:PLANE_ROWS, :] + p1[:PLANE_ROWS, :] + p2[:PLANE_ROWS, :] + p3[:PLANE_ROWS, :]
    target = jnp.broadcast_to(ill_ref[...].astype(jnp.float32), (8, LANES))
    core_out[:PLANE_ROWS, :] = total
    core_out[PLANE_ROWS:, :] = target
    leave = floats_ref[4]
    dur_out[:Z, :] = leave * total[:Z]
    dur_out[Z : 2 * Z, :] = leave * total[2 * Z : 3 * Z]
    dur_out[2 * Z :, :] = target


def spread_targets(target_row, planes):
    z = lax.broadcasted_iota(jnp.int32, (Z, LANES), 0)
    lane = lax.broadcasted_iota(jnp.int32, (Z, LANES), 1)
    picked = [jnp.where(lane == 4 * z + 2 * d + a, target_row, 0.0) for a, d in planes]
    picked = jnp.concatenate(picked, axis=0).astype(jnp.bfloat16)
    ones = jnp.ones((LANES, LANES), jnp.bfloat16)
    return jnp.dot(picked, ones, preferred_element_type=jnp.float32)


def settle_kernel(ints_ref, floats_ref, own_ref, core_ref, dur_ref, dur_core_ref, o0, o1, o2, o3):
    whole = ((0, 0), (0, 1), (1, 0), (1, 1))
    lowest = ((0, 0), (1, 0))
    sources = ([], [])
    for ref in (own_ref, core_ref):
        targets = spread_targets(ref[PLANE_ROWS : PLANE_ROWS + 1, :], whole)
        for p, (_, d) in enumerate(whole):
            sources[d].append((targets[p * Z : (p + 1) * Z], ref[p * Z : (p + 1) * Z, :]))
    arriving = []
    for ref in (dur_ref, dur_core_ref):
        targets = spread_targets(ref[2 * Z : 2 * Z + 1, :], lowest)
        for p in range(2):
            arriving.append((targets[p * Z : (p + 1) * Z], ref[p * Z : (p + 1) * Z, :]))
    y, core = ints_ref[1], ints_ref[2]
    stay_low, stay_high, leave_high = floats_ref[2], floats_ref[3], floats_ref[5]
    for k, out in enumerate((o0, o1, o2, o3)):
        for a in range(2):
            point = (4 * ((y + k) & 3) + 2 * core + a).astype(jnp.float32)

            def gathered(pairs):
                parts = [jnp.where(target == point, mass, 0.0) for target, mass in pairs]
                return (parts[0] + parts[1]) + (parts[2] + parts[3])

            low, high = gathered(sources[0]), gathered(sources[1])
            out[2 * a * Z : (2 * a + 1) * Z, :] = stay_low * low + leave_high * high
            out[(2 * a + 1) * Z : (2 * a + 2) * Z, :] = stay_high * high + gathered(arriving)


def population_kernel(transition_ref, s0, s1, s2, s3, out_ref):
    settled = (s0[...] + s1[...]) + (s2[...] + s3[...])
    wide = jnp.concatenate([settled[p * Z : (p + 1) * Z] for p in range(4)], axis=1)
    moved = lax.dot_general(
        transition_ref[...], wide, (((0,), (0,)), ((), ())), precision=HIGHEST_PREC, preferred_element_type=jnp.float32
    )
    for p, plane in enumerate(split_lanes(moved, 4)):
        a, d = p // 2, p % 2
        out_ref[pl.ds(2 * d + a, Z, stride=4), :] = plane


def call(kernel, out_rows, spaces, scratch=()):
    shapes = [jax.ShapeDtypeStruct((rows, LANES), jnp.float32) for rows in out_rows]
    specs = [pl.BlockSpec(memory_space=VMEM) for _ in out_rows]
    single = len(out_rows) == 1
    return pl.pallas_call(
        kernel,
        out_shape=shapes[0] if single else shapes,
        in_specs=[pl.BlockSpec(memory_space=SMEM if s == "s" else VMEM) for s in spaces],
        out_specs=specs[0] if single else specs,
        scratch_shapes=list(scratch),
    )


def turned(axis, distance):
    count = lax.axis_size(axis)
    return [(i, (i + distance) % count) for i in range(count)]


def from_other_liq(pieces):
    got = [lax.ppermute(pieces[k], "liq", turned("liq", k)) for k in range(1, 4)]
    return [got[3 - k] for k in range(1, 4)]


def from_above_ill(x):
    return lax.ppermute(x, "ill", turned("ill", -1))


def body(
    marginal_value, transition, discount_shock, illiquid_drift, durable_keep, bracket_index, bracket_weight,
    steady_consumption, lottery_weight, liquid_target, illiquid_target, population,
):
    flat = lambda x: x.reshape(PLANE_ROWS, LANES)
    liq, ill, dur = lax.axis_index("liq"), lax.axis_index("ill"), lax.axis_index("dur")
    ill_count, dur_count = lax.axis_size("ill"), lax.axis_size("dur")
    ints = jnp.stack([liq, ill // 2, ill % 2]).astype(jnp.int32)
    last = ill == ill_count - 1
    stay_low = jnp.where(dur == 0, 1.0, durable_keep[0])
    stay_high = durable_keep[1]
    floats = jnp.stack(
        [
            illiquid_drift[0],
            jnp.where(last, 1.0, illiquid_drift[1]),
            stay_low,
            stay_high,
            1.0 - stay_low,
            1.0 - stay_high,
        ]
    )
    index, weight = flat(bracket_index), flat(bracket_weight)
    states = [index, weight] + [flat(x) for x in (steady_consumption, lottery_weight, liquid_target, population)]
    scratch = [pltpu.VMEM((2, HALF_ROWS, LANES), jnp.float32), pltpu.VMEM((8 * HALF_ROWS, LANES), jnp.float32)]

    with jax.named_scope("expect"):
        expected = call(expect_kernel, [PLANE_ROWS], "vvv")(
            flat(marginal_value), transition, discount_shock.reshape(1, Z)
        )
    with jax.named_scope("expected_over_liq"):
        pieces = [expected] + from_other_liq([expected] * 4)
    with jax.named_scope("expected_over_ill"):
        halo = from_above_ill(jnp.concatenate([x[:HALF_ROWS] for x in pieces], axis=0))
    with jax.named_scope("first_half"):
        first = call(first_half_kernel, [5 * HALF_ROWS], "ss" + "v" * 11, scratch)(
            ints, floats, *pieces, transition, *states
        )
    with jax.named_scope("second_half"):
        sends = call(second_half_kernel, [4 * HALF_ROWS] * 4, "ss" + "v" * 13, scratch)(
            ints, floats, *pieces, halo, first, transition, *states
        )
    with jax.named_scope("mass_over_liq"):
        got = [sends[0]] + from_other_liq(sends)
    with jax.named_scope("gather_mass"):
        to_core, to_dur = call(gather_mass_kernel, [PLANE_ROWS + 8, HALF_ROWS + 8], "s" + "v" * 5)(
            floats, *got, illiquid_target.reshape(1, PLANE_ROWS)
        )
    with jax.named_scope("mass_over_core_and_dur"):
        other_core = [(i, i ^ 1) for i in range(ill_count)]
        both = [
            (i * dur_count + d, (i ^ 1) * dur_count + (d - 1) % dur_count)
            for i in range(ill_count)
            for d in range(dur_count)
        ]
        from_core = lax.ppermute(to_core, "ill", other_core)
        from_dur = lax.ppermute(to_dur, "dur", turned("dur", -1))
        from_dur_core = lax.ppermute(to_dur, ("ill", "dur"), both)
    with jax.named_scope("expected_over_ill"):
        halo = from_above_ill(
            jnp.concatenate([x[PLANE_ROWS : PLANE_ROWS + HALF_ROWS] for x in got], axis=0)
        )
    with jax.named_scope("settle"):
        parts = call(settle_kernel, [PLANE_ROWS] * 4, "ssvvvv")(
            ints, floats, to_core, from_core, from_dur, from_dur_core
        )
    with jax.named_scope("mass_over_ill"):
        arrived = [lax.ppermute(parts[k], "ill", turned("ill", 2 * k)) for k in range(1, 4)]
    with jax.named_scope("consume"):
        consumption = call(consume_kernel, [PLANE_ROWS], "ss" + "v" * 7)(ints, floats, *got, halo, index, weight)
    with jax.named_scope("population"):
        population_next = call(population_kernel, [PLANE_ROWS], "vvvvv")(transition, parts[0], *arrived)
    shape = population.shape
    return consumption.reshape(shape), population_next.reshape(shape)


def solution(mesh):
    state = P(None, "dur", "ill", "liq")
    in_specs = (
        state, P(), P(), P("ill"), P("dur"), state, state, state, state, state, P(None, "dur", "ill"), state,
    )
    return jax.shard_map(body, mesh=mesh, in_specs=in_specs, out_specs=(state, state), check_vma=False)
```

time: 964 us -> 65.4 us (0.07)
  the two profiles are of different devices: /device:TPU:96 before, /device:TPU:1 now
where the time goes in v1:
time: 65.4 us; the launch traced here: 64.6 us
  starting transfers between devices  19.6 us (30%)
  Pallas kernels  16.6 us (25%)
  waiting for transfers between devices  14.2 us (22%)
  local copies, waits for them, and re-layouts  11 us (17%)
  between operations  2.65 us (4%)
    ppermute x6, waiting for transfers between devices, from_other_liq(): lax.ppermute(pieces[k], 'liq', turned('liq', k))  11.1 us
    ppermute x1, starting transfers between devices, body(): from_dur_core = lax.ppermute(to_dur, ('ill', 'dur'), both)  6.94 us
    ppermute x6, starting transfers between devices, from_other_liq(): lax.ppermute(pieces[k], 'liq', turned('liq', k))  6.41 us
    unnamed x37, local copies, waits for them, and re-layouts  4.71 us
    pallas_call x1, Pallas kernels, body(): call(second_half_kernel, [4 * HALF_ROWS] * 4, 'ss' + 'v' * 13, scratch)  3.58 us
    pallas_call x1, Pallas kernels, body(): call(first_half_kernel, [5 * HALF_ROWS], 'ss' + 'v' * 11, scratch)  3.39 us
    ppermute x3, starting transfers between devices, body(): lax.ppermute(parts[k], 'ill', turned('ill', 2 * k))  2.68 us
    pallas_call x1, Pallas kernels, body(): call(consume_kernel, [PLANE_ROWS], 'ss' + 'v' * 7)  2.27 us
  transfers between devices with their start and end apart: 14, of which 8 were waited for; matrix products, arithmetic and copies ran while one was open for 8% of the time, Pallas kernels for 12%

profile of v1, /device:TPU:1, one launch (start us, length us, event | category | flops | bytes accessed | tf_op | source)
XLA Modules:
  0.0 64.6 jit_solution(9871687221452174801)
XLA Ops:
  0.6 1.8 %expect.1.e0 = f32[128,128]{1,0:T(8,128)} custom-call(f32[128,128]{1,0:T(8,128)} %bitcast.32, f32[32,32]{1,0:T(8,128)} %transition_ref.7, f32[1,32]{1,0:T(1,128)} %bitcast.35), custom_call_target="tpu_custom_call" | custom-call | tf_op jit(solution)/shard_map/expect/pallas_call | solution.py:276
  2.5 3.3 %collective-permute-start = (f32[128,128]{1,0:T(8,128)}, f32[128,128]{1,0:T(8,128)S(1)}, u32[]{:S(2)}, u32[]{:S(2)}) collective-permute-start(f32[128,128]{1,0:T(8,128)} %expect.1.e0), channel_id=1, source_target_pairs={{0,192},{64,0},{128,64},{192,128},{1,193},{65,1},{129,65},{193,129... | collective-permute-start | bytes 196616 | tf_op jit(solution)/shard_map/expected_over_liq/ppermute | solution.py:242
  5.8 0.5 collective-permute-start.1
  6.3 0.6 collective-permute-start.2
  6.9 0.8 %slice.48 = f32[64,128]{1,0:T(8,128)S(1)} slice(f32[128,128]{1,0:T(8,128)} %expect.1.e0), slice={[0:64], [0:128]} | slice | bytes 65536 | tf_op jit(solution)/shard_map/expected_over_ill/slice | solution.py:282
  7.7 0.0 collective-permute-done.e1
  7.7 3.0 %collective-permute-done.1.e2 = f32[128,128]{1,0:T(8,128)S(1)} collective-permute-done((f32[128,128]{1,0:T(8,128)}, f32[128,128]{1,0:T(8,128)S(1)}, u32[]{:S(2)}, u32[]{:S(2)}) %collective-permute-start.1) | collective-permute-done | bytes 65568 | tf_op jit(solution)/shard_map/expected_over_liq/ppermute | solution.py:242
  10.7 0.0 copy-done.3
  10.7 0.6 collective-permute-done.2.e3
  11.3 0.8 %slice-done.3 = f32[64,128]{1,0:T(8,128)S(1)} async-done(((f32[128,128]{1,0:T(8,128)}), f32[64,128]{1,0:T(8,128)S(1)}, s32[]{:S(2)}) %slice-start.3) | async-done | bytes 32792 | tf_op jit(solution)/shard_map/expected_over_ill/slice | solution.py:282
  12.1 0.0 copy-done.4
  12.1 0.0 copy-done.5
  12.1 2.1 %collective-permute-start.3 = (f32[256,128]{1,0:T(8,128)S(1)}, f32[256,128]{1,0:T(8,128)S(1)}, u32[]{:S(2)}, u32[]{:S(2)}) collective-permute-start(f32[256,128]{1,0:T(8,128)S(1)} %pad_maximum_fusion), channel_id=1, source_target_pairs={{0,56},{8,0},{16,8},{24,16},{32,24},{40,32},{48,40},{56,48},{1,57}... | collective-permute-start | bytes 393224 | tf_op jit(solution)/shard_map/expected_over_ill/ppermute | solution.py:247
  14.2 0.0 copy-done.15
  14.2 0.0 copy-done.16
  14.2 0.6 fusion
  16.8 1.9 %stack.32.floats_ref = f32[6]{0:T(128)} concatenate(f32[1]{0:T(128)} %get-tuple-element.26, f32[1]{0:T(128)} %bitcast.4, f32[1]{0:T(128)} %bitcast.6, f32[1]{0:T(128)} %get-tuple-element.22, f32[1]{0:T(128)} %bitcast.7, f32[1]{0:T(128)S(6)} %sub.13), dimensions={0} | concatenate | bytes 48 | tf_op jit(solution)/shard_map/stack | solution.py:261
  18.7 0.6 pad_add_fusion.ints_ref
  19.3 3.4 %first_half.1.first_ref = f32[320,128]{1,0:T(8,128)} custom-call(s32[3]{0:T(128)} %pad_add_fusion.ints_ref, f32[6]{0:T(128)} %stack.32.floats_ref, f32[128,128]{1,0:T(8,128)} %expect.1.e0, f32[128,128]{1,0:T(8,128)} %copy-done.3, f32[128,128]{1,0:T(8,128)} %copy-done.4, f32[128,128]{1,0:T(8,128)} %copy-done.5, f32[32,32]{1,0:T(8,128)} %transition_ref.7, ...), custom_call_target="tpu_custom_call" | custom-call | tf_op jit(solution)/shard_map/first_half/pallas_call | solution.py:284
  22.7 0.0 collective-permute-done.3.halo_ref
  22.7 0.6 %copy-done.6 = f32[256,128]{1,0:T(8,128)} copy-done((f32[256,128]{1,0:T(8,128)}, f32[256,128]{1,0:T(8,128)S(1)}, u32[]{:S(2)}) %copy-start.6) | copy-done | bytes 131096
  23.3 3.6 %second_half.1 = (f32[256,128]{1,0:T(8,128)}, f32[256,128]{1,0:T(8,128)}, f32[256,128]{1,0:T(8,128)}, f32[256,128]{1,0:T(8,128)}) custom-call(s32[3]{0:T(128)} %pad_add_fusion.ints_ref, f32[6]{0:T(128)} %stack.32.floats_ref, f32[128,128]{1,0:T(8,128)} %expect.1.e0, f32[128,128]{1,0:T(8,128)} %copy-done.3, f32[128,128]{1,0:T(8,128)} %copy-done.4, ...), custom_call_target="tpu_custom_call" | custom-call | tf_op jit(solution)/shard_map/second_half/pallas_call | solution.py:288
  26.9 1.3 %collective-permute-start.4 = (f32[256,128]{1,0:T(8,128)}, f32[256,128]{1,0:T(8,128)S(1)}, u32[]{:S(2)}, u32[]{:S(2)}) collective-permute-start(f32[256,128]{1,0:T(8,128)} %get-tuple-element.13), channel_id=1, source_target_pairs={{0,192},{64,0},{128,64},{192,128},{1,193},{65,1},{129,65},{193,129... | collective-permute-start | bytes 393224 | tf_op jit(solution)/shard_map/mass_over_liq/ppermute | solution.py:242
  28.2 0.7 %collective-permute-start.5 = (f32[256,128]{1,0:T(8,128)}, f32[256,128]{1,0:T(8,128)S(1)}, u32[]{:S(2)}, u32[]{:S(2)}) collective-permute-start(f32[256,128]{1,0:T(8,128)} %get-tuple-element.14), channel_id=1, source_target_pairs={{0,128},{64,192},{128,0},{192,64},{1,129},{65,193},{129,1},{193,65... | collective-permute-start | bytes 393224 | tf_op jit(solution)/shard_map/mass_over_liq/ppermute | solution.py:242
  28.9 0.0 collective-permute-start.6
  28.9 0.0 copy-done.14
  28.9 0.1 copy.15
  29.0 0.7 %reshape.49.ill_ref = s32[1,128]{1,0:T(1,128)} reshape(s32[32,2,2]{2,1,0:T(2,128)S(1)} %copy.15) | data formatting | bytes 1024 | tf_op jit(solution)/shard_map/gather_mass/reshape | solution.py:295
  29.7 0.8 %slice.44 = f32[64,128]{1,0:T(8,128)S(1)} slice(f32[256,128]{1,0:T(8,128)} %get-tuple-element.12.e0.p0), slice={[128:192], [0:128]} | slice | bytes 65536 | tf_op jit(solution)/shard_map/expected_over_ill/slice | solution.py:309
  30.4 0.6 collective-permute-done.4.e1.p1
  31.0 2.8 %collective-permute-done.5.e2.p2 = f32[256,128]{1,0:T(8,128)S(1)} collective-permute-done((f32[256,128]{1,0:T(8,128)}, f32[256,128]{1,0:T(8,128)S(1)}, u32[]{:S(2)}, u32[]{:S(2)}) %collective-permute-start.5) | collective-permute-done | bytes 131104 | tf_op jit(solution)/shard_map/mass_over_liq/ppermute | solution.py:242
  33.8 4.1 %collective-permute-done.6.e3.p3 = f32[256,128]{1,0:T(8,128)S(1)} collective-permute-done((f32[256,128]{1,0:T(8,128)}, f32[256,128]{1,0:T(8,128)S(1)}, u32[]{:S(2)}, u32[]{:S(2)}) %collective-permute-start.6) | collective-permute-done | bytes 131104 | tf_op jit(solution)/shard_map/mass_over_liq/ppermute | solution.py:242
  37.9 0.0 copy-done
  37.9 0.0 copy-done.1
  37.9 0.7 %copy-done.2 = f32[256,128]{1,0:T(8,128)} copy-done((f32[256,128]{1,0:T(8,128)}, f32[256,128]{1,0:T(8,128)S(1)}, u32[]{:S(2)}) %copy-start.2) | copy-done | bytes 131096
  38.6 1.8 %gather_mass.1 = (f32[136,128]{1,0:T(8,128)}, f32[72,128]{1,0:T(8,128)}) custom-call(f32[6]{0:T(128)} %stack.32.floats_ref, f32[256,128]{1,0:T(8,128)} %get-tuple-element.12.e0.p0, f32[256,128]{1,0:T(8,128)} %copy-done, f32[256,128]{1,0:T(8,128)} %copy-done.1, f32[256,128]{1,0:T(8,128)} %copy-done.2, s32[1,128]{1,0:T(1,128)} %reshape.49.ill_ref), custom_call_target="tpu_custom_call" | custom-call | tf_op jit(solution)/shard_map/gather_mass/pallas_call | solution.py:294
  40.3 0.7 %collective-permute-start.8 = (f32[136,128]{1,0:T(8,128)}, f32[136,128]{1,0:T(8,128)S(1)}, u32[]{:S(2)}, u32[]{:S(2)}) collective-permute-start(f32[136,128]{1,0:T(8,128)} %get-tuple-element.16.own_ref), channel_id=1, source_target_pairs={{0,8},{8,0},{16,24},{24,16},{32,40},{40,32},{48,56},{56,48},{1,9},... | collective-permute-start | bytes 208904 | tf_op jit(solution)/shard_map/mass_over_core_and_dur/ppermute | solution.py:304
  41.0 0.8 %slice-done.2 = f32[64,128]{1,0:T(8,128)S(1)} async-done(((f32[256,128]{1,0:T(8,128)}), f32[64,128]{1,0:T(8,128)S(1)}, s32[]{:S(2)}) %slice-start.2) | async-done | bytes 32792 | tf_op jit(solution)/shard_map/expected_over_ill/slice | solution.py:309
  41.8 0.0 slice-done
  41.8 0.0 slice-done.1
  41.8 0.0 collective-permute-start.7
  41.9 0.7 %copy-done.17 = f32[72,128]{1,0:T(8,128)S(1)} copy-done((f32[72,128]{1,0:T(8,128)S(1)}, f32[72,128]{1,0:T(8,128)}, u32[]{:S(2)}) %copy-start.17) | copy-done | bytes 36888
  42.6 6.9 %collective-permute-start.10 = (f32[72,128]{1,0:T(8,128)S(1)}, f32[72,128]{1,0:T(8,128)S(1)}, u32[]{:S(2)}, u32[]{:S(2)}) collective-permute-start(f32[72,128]{1,0:T(8,128)S(1)} %copy-done.17), channel_id=1, source_target_pairs={{0,15},{1,8},{2,9},{3,10},{4,11},{5,12},{6,13},{7,14},{8,7},{9,0},... | collective-permute-start | bytes 110600 | tf_op jit(solution)/shard_map/mass_over_core_and_dur/ppermute | solution.py:306
  49.5 0.7 %collective-permute-start.9 = (f32[72,128]{1,0:T(8,128)S(1)}, f32[72,128]{1,0:T(8,128)S(1)}, u32[]{:S(2)}, u32[]{:S(2)}) collective-permute-start(f32[72,128]{1,0:T(8,128)S(1)} %copy-done.17), channel_id=1, source_target_pairs={{0,7},{1,0},{2,1},{3,2},{4,3},{5,4},{6,5},{7,6},{8,15},{9,8},{10,9... | collective-permute-start | bytes 110600 | tf_op jit(solution)/shard_map/mass_over_core_and_dur/ppermute | solution.py:305
  50.3 0.3 collective-permute-done.10.dur_core_ref
  50.6 1.7 %collective-permute-done.9.dur_ref = f32[72,128]{1,0:T(8,128)S(1)} collective-permute-done((f32[72,128]{1,0:T(8,128)S(1)}, f32[72,128]{1,0:T(8,128)S(1)}, u32[]{:S(2)}, u32[]{:S(2)}) %collective-permute-start.9) | collective-permute-done | bytes 36896 | tf_op jit(solution)/shard_map/mass_over_core_and_dur/ppermute | solution.py:305
  52.4 0.0 collective-permute-done.8.core_ref
  52.4 0.6 copy-done.13
  53.0 0.6 copy-done.8
  53.6 1.9 %settle.1 = (f32[128,128]{1,0:T(8,128)}, f32[128,128]{1,0:T(8,128)}, f32[128,128]{1,0:T(8,128)}, f32[128,128]{1,0:T(8,128)}) custom-call(s32[3]{0:T(128)} %pad_add_fusion.ints_ref, f32[6]{0:T(128)} %stack.32.floats_ref, f32[136,128]{1,0:T(8,128)} %get-tuple-element.16.own_ref, f32[136,128]{1,0:T(8,128)} %copy-done.8, f32[72,128]{1,0:T(8,128)} %copy-done.13, ...), custom_call_target="tpu_custom_call" | custom-call | tf_op jit(solution)/shard_map/settle/pallas_call | solution.py:312
  55.5 0.0 collective-permute-start.11
  55.5 1.7 %collective-permute-start.12 = (f32[128,128]{1,0:T(8,128)}, f32[128,128]{1,0:T(8,128)S(1)}, u32[]{:S(2)}, u32[]{:S(2)}) collective-permute-start(f32[128,128]{1,0:T(8,128)} %get-tuple-element.20), channel_id=1, source_target_pairs={{0,32},{8,40},{16,48},{24,56},{32,0},{40,8},{48,16},{56,24},{1,33}... | collective-permute-start | bytes 196616 | tf_op jit(solution)/shard_map/mass_over_ill/ppermute | solution.py:316
  57.2 1.0 %collective-permute-start.13 = (f32[128,128]{1,0:T(8,128)}, f32[128,128]{1,0:T(8,128)S(1)}, u32[]{:S(2)}, u32[]{:S(2)}) collective-permute-start(f32[128,128]{1,0:T(8,128)} %get-tuple-element.21), channel_id=1, source_target_pairs={{0,48},{8,56},{16,0},{24,8},{32,16},{40,24},{48,32},{56,40},{1,49}... | collective-permute-start | bytes 196616 | tf_op jit(solution)/shard_map/mass_over_ill/ppermute | solution.py:316
  58.2 0.0 collective-permute-done.7.halo_ref
  58.2 0.6 %copy-done.7 = f32[256,128]{1,0:T(8,128)} copy-done((f32[256,128]{1,0:T(8,128)}, f32[256,128]{1,0:T(8,128)S(1)}, u32[]{:S(2)}) %copy-start.7) | copy-done | bytes 131096
  58.8 2.3 %consume.1 = f32[128,128]{1,0:T(8,128)} custom-call(s32[3]{0:T(128)} %pad_add_fusion.ints_ref, f32[6]{0:T(128)} %stack.32.floats_ref, f32[256,128]{1,0:T(8,128)} %get-tuple-element.12.e0.p0, f32[256,128]{1,0:T(8,128)} %copy-done, f32[256,128]{1,0:T(8,128)} %copy-done.1, f32[256,128]{1,0:T(8,128)} %copy-done.2, f32[256,128]{1,0:T(8,128)} %copy-done.7, ...), custom_call_target="tpu_custom_call" | custom-call | tf_op jit(solution)/shard_map/consume/pallas_call | solution.py:318
  61.1 1.0 %collective-permute-done.11.s1 = f32[128,128]{1,0:T(8,128)S(1)} collective-permute-done((f32[128,128]{1,0:T(8,128)}, f32[128,128]{1,0:T(8,128)S(1)}, u32[]{:S(2)}, u32[]{:S(2)}) %collective-permute-start.11) | collective-permute-done | bytes 65568 | tf_op jit(solution)/shard_map/mass_over_ill/ppermute | solution.py:316
  62.1 0.0 collective-permute-done.12.s2
  62.1 0.0 collective-permute-done.13.s3
  62.1 0.0 copy-start.11
  62.1 0.6 copy-done.9
  62.7 0.0 copy-done.10
  62.8 0.0 copy-done.11
  62.8 1.8 %population.1 = f32[128,128]{1,0:T(8,128)} custom-call(f32[32,32]{1,0:T(8,128)} %transition_ref.7, f32[128,128]{1,0:T(8,128)} %get-tuple-element.18.s0, f32[128,128]{1,0:T(8,128)} %copy-done.9, f32[128,128]{1,0:T(8,128)} %copy-done.10, f32[128,128]{1,0:T(8,128)} %copy-done.11), custom_call_target="tpu_custom_call" | custom-call | tf_op jit(solution)/shard_map/population/pallas_call | solution.py:320
  (26 shorter events, 0.1 us)
Async XLA Ops:
  2.5 5.2 %collective-permute-start = (f32[128,128]{1,0:T(8,128)}, f32[128,128]{1,0:T(8,128)S(1)}, u32[]{:S(2)}, u32[]{:S(2)}) collective-permute-start(f32[128,128]{1,0:T(8,128)} %expect.1.e0), channel_id=1, source_target_pairs={{0,192},{64,0},{128,64},{192,128},{1,193},{65,1},{129,65},{193,129... | collective-permute-start | bytes 196616 | tf_op jit(solution)/shard_map/expected_over_liq/ppermute | solution.py:242
  5.8 4.9 %collective-permute-start.1 = (f32[128,128]{1,0:T(8,128)}, f32[128,128]{1,0:T(8,128)S(1)}, u32[]{:S(2)}, u32[]{:S(2)}) collective-permute-start(f32[128,128]{1,0:T(8,128)} %expect.1.e0), channel_id=1, source_target_pairs={{0,128},{64,192},{128,0},{192,64},{1,129},{65,193},{129,1},{193,65... | collective-permute-start | bytes 196616 | tf_op jit(solution)/shard_map/expected_over_liq/ppermute | solution.py:242
  6.3 5.0 %collective-permute-start.2 = (f32[128,128]{1,0:T(8,128)}, f32[128,128]{1,0:T(8,128)S(1)}, u32[]{:S(2)}, u32[]{:S(2)}) collective-permute-start(f32[128,128]{1,0:T(8,128)} %expect.1.e0), channel_id=1, source_target_pairs={{0,64},{64,128},{128,192},{192,0},{1,65},{65,129},{129,193},{193,1... | collective-permute-start | bytes 196616 | tf_op jit(solution)/shard_map/expected_over_liq/ppermute | solution.py:242
  7.7 3.0 %copy-start.3 = (f32[128,128]{1,0:T(8,128)}, f32[128,128]{1,0:T(8,128)S(1)}, u32[]{:S(2)}) copy-start(f32[128,128]{1,0:T(8,128)S(1)} %collective-permute-done.e1) | copy-start | bytes 196612
  10.7 1.4 %copy-start.4 = (f32[128,128]{1,0:T(8,128)}, f32[128,128]{1,0:T(8,128)S(1)}, u32[]{:S(2)}) copy-start(f32[128,128]{1,0:T(8,128)S(1)} %collective-permute-done.1.e2) | copy-start | bytes 196612
  11.3 0.8 %copy-start.5 = (f32[128,128]{1,0:T(8,128)}, f32[128,128]{1,0:T(8,128)S(1)}, u32[]{:S(2)}) copy-start(f32[128,128]{1,0:T(8,128)S(1)} %collective-permute-done.2.e3) | copy-start | bytes 196612
  11.3 0.8 %slice-start.3 = ((f32[128,128]{1,0:T(8,128)}), f32[64,128]{1,0:T(8,128)S(1)}, s32[]{:S(2)}) async-start(f32[128,128]{1,0:T(8,128)} %copy-done.3), calls=%async_computation.3 | async-start | bytes 65536 | tf_op jit(solution)/shard_map/expected_over_ill/slice | solution.py:282
  12.1 2.2 %copy-start.15 = (f32[2]{0:T(128)S(1)}, f32[2]{0:T(128)}, u32[]{:S(2)}) copy-start(f32[2]{0:T(128)} %param.16) | copy-start | bytes 28
  12.1 2.2 %copy-start.16 = (f32[2]{0:T(128)S(1)}, f32[2]{0:T(128)}, u32[]{:S(2)}) copy-start(f32[2]{0:T(128)} %param.15) | copy-start | bytes 28
  12.1 10.6 %collective-permute-start.3 = (f32[256,128]{1,0:T(8,128)S(1)}, f32[256,128]{1,0:T(8,128)S(1)}, u32[]{:S(2)}, u32[]{:S(2)}) collective-permute-start(f32[256,128]{1,0:T(8,128)S(1)} %pad_maximum_fusion), channel_id=1, source_target_pairs={{0,56},{8,0},{16,8},{24,16},{32,24},{40,32},{48,40},{56,48},{1,57}... | collective-permute-start | bytes 393224 | tf_op jit(solution)/shard_map/expected_over_ill/ppermute | solution.py:247
  22.7 0.7 %copy-start.6 = (f32[256,128]{1,0:T(8,128)}, f32[256,128]{1,0:T(8,128)S(1)}, u32[]{:S(2)}) copy-start(f32[256,128]{1,0:T(8,128)S(1)} %collective-permute-done.3.halo_ref) | copy-start | bytes 393220
  26.9 2.0 %copy-start.14 = (s32[32,2,2]{0,2,1:T(2,128)S(1)}, s32[32,2,2]{0,2,1:T(2,128)}, u32[]{:S(2)}) copy-start(s32[32,2,2]{0,2,1:T(2,128)} %param.22) | copy-start | bytes 1540
  26.9 4.1 %collective-permute-start.4 = (f32[256,128]{1,0:T(8,128)}, f32[256,128]{1,0:T(8,128)S(1)}, u32[]{:S(2)}, u32[]{:S(2)}) collective-permute-start(f32[256,128]{1,0:T(8,128)} %get-tuple-element.13), channel_id=1, source_target_pairs={{0,192},{64,0},{128,64},{192,128},{1,193},{65,1},{129,65},{193,129... | collective-permute-start | bytes 393224 | tf_op jit(solution)/shard_map/mass_over_liq/ppermute | solution.py:242
  28.2 5.6 %collective-permute-start.5 = (f32[256,128]{1,0:T(8,128)}, f32[256,128]{1,0:T(8,128)S(1)}, u32[]{:S(2)}, u32[]{:S(2)}) collective-permute-start(f32[256,128]{1,0:T(8,128)} %get-tuple-element.14), channel_id=1, source_target_pairs={{0,128},{64,192},{128,0},{192,64},{1,129},{65,193},{129,1},{193,65... | collective-permute-start | bytes 393224 | tf_op jit(solution)/shard_map/mass_over_liq/ppermute | solution.py:242
  28.9 9.0 %collective-permute-start.6 = (f32[256,128]{1,0:T(8,128)}, f32[256,128]{1,0:T(8,128)S(1)}, u32[]{:S(2)}, u32[]{:S(2)}) collective-permute-start(f32[256,128]{1,0:T(8,128)} %get-tuple-element.15), channel_id=1, source_target_pairs={{0,64},{64,128},{128,192},{192,0},{1,65},{65,129},{129,193},{193,1... | collective-permute-start | bytes 393224 | tf_op jit(solution)/shard_map/mass_over_liq/ppermute | solution.py:242
  31.0 6.9 %copy-start = (f32[256,128]{1,0:T(8,128)}, f32[256,128]{1,0:T(8,128)S(1)}, u32[]{:S(2)}) copy-start(f32[256,128]{1,0:T(8,128)S(1)} %collective-permute-done.4.e1.p1) | copy-start | bytes 393220
  33.8 4.1 %copy-start.1 = (f32[256,128]{1,0:T(8,128)}, f32[256,128]{1,0:T(8,128)S(1)}, u32[]{:S(2)}) copy-start(f32[256,128]{1,0:T(8,128)S(1)} %collective-permute-done.5.e2.p2) | copy-start | bytes 393220
  37.9 0.7 %copy-start.2 = (f32[256,128]{1,0:T(8,128)}, f32[256,128]{1,0:T(8,128)S(1)}, u32[]{:S(2)}) copy-start(f32[256,128]{1,0:T(8,128)S(1)} %collective-permute-done.6.e3.p3) | copy-start | bytes 393220
  40.3 12.0 %collective-permute-start.8 = (f32[136,128]{1,0:T(8,128)}, f32[136,128]{1,0:T(8,128)S(1)}, u32[]{:S(2)}, u32[]{:S(2)}) collective-permute-start(f32[136,128]{1,0:T(8,128)} %get-tuple-element.16.own_ref), channel_id=1, source_target_pairs={{0,8},{8,0},{16,24},{24,16},{32,40},{40,32},{48,56},{56,48},{1,9},... | collective-permute-start | bytes 208904 | tf_op jit(solution)/shard_map/mass_over_core_and_dur/ppermute | solution.py:304
  41.0 0.8 %slice-start.2 = ((f32[256,128]{1,0:T(8,128)}), f32[64,128]{1,0:T(8,128)S(1)}, s32[]{:S(2)}) async-start(f32[256,128]{1,0:T(8,128)} %copy-done.2), calls=%async_computation.2 | async-start | bytes 65536 | tf_op jit(solution)/shard_map/expected_over_ill/slice | solution.py:309
  41.0 0.8 %slice-start = ((f32[256,128]{1,0:T(8,128)}), f32[64,128]{1,0:T(8,128)S(1)}, s32[]{:S(2)}) async-start(f32[256,128]{1,0:T(8,128)} %copy-done), calls=%async_computation | async-start | bytes 65536 | tf_op jit(solution)/shard_map/expected_over_ill/slice | solution.py:309
  41.0 0.8 %slice-start.1 = ((f32[256,128]{1,0:T(8,128)}), f32[64,128]{1,0:T(8,128)S(1)}, s32[]{:S(2)}) async-start(f32[256,128]{1,0:T(8,128)} %copy-done.1), calls=%async_computation.1 | async-start | bytes 65536 | tf_op jit(solution)/shard_map/expected_over_ill/slice | solution.py:309
  41.8 0.8 %copy-start.17 = (f32[72,128]{1,0:T(8,128)S(1)}, f32[72,128]{1,0:T(8,128)}, u32[]{:S(2)}) copy-start(f32[72,128]{1,0:T(8,128)} %get-tuple-element.17) | copy-start | bytes 110596
  41.8 16.3 %collective-permute-start.7 = (f32[256,128]{1,0:T(8,128)S(1)}, f32[256,128]{1,0:T(8,128)S(1)}, u32[]{:S(2)}, u32[]{:S(2)}) collective-permute-start(f32[256,128]{1,0:T(8,128)S(1)} %pad_maximum_fusion.1), channel_id=1, source_target_pairs={{0,56},{8,0},{16,8},{24,16},{32,24},{40,32},{48,40},{56,48},{1,57}... | collective-permute-start | bytes 393224 | tf_op jit(solution)/shard_map/expected_over_ill/ppermute | solution.py:247
  42.6 8.0 %collective-permute-start.10 = (f32[72,128]{1,0:T(8,128)S(1)}, f32[72,128]{1,0:T(8,128)S(1)}, u32[]{:S(2)}, u32[]{:S(2)}) collective-permute-start(f32[72,128]{1,0:T(8,128)S(1)} %copy-done.17), channel_id=1, source_target_pairs={{0,15},{1,8},{2,9},{3,10},{4,11},{5,12},{6,13},{7,14},{8,7},{9,0},... | collective-permute-start | bytes 110600 | tf_op jit(solution)/shard_map/mass_over_core_and_dur/ppermute | solution.py:306
  49.5 2.8 %collective-permute-start.9 = (f32[72,128]{1,0:T(8,128)S(1)}, f32[72,128]{1,0:T(8,128)S(1)}, u32[]{:S(2)}, u32[]{:S(2)}) collective-permute-start(f32[72,128]{1,0:T(8,128)S(1)} %copy-done.17), channel_id=1, source_target_pairs={{0,7},{1,0},{2,1},{3,2},{4,3},{5,4},{6,5},{7,6},{8,15},{9,8},{10,9... | collective-permute-start | bytes 110600 | tf_op jit(solution)/shard_map/mass_over_core_and_dur/ppermute | solution.py:305
  50.6 1.8 %copy-start.12 = (f32[72,128]{1,0:T(8,128)}, f32[72,128]{1,0:T(8,128)S(1)}, u32[]{:S(2)}) copy-start(f32[72,128]{1,0:T(8,128)S(1)} %collective-permute-done.10.dur_core_ref) | copy-start | bytes 110596
  52.4 0.6 copy-start.13
  53.0 0.6 copy-start.8
  55.5 6.6 %collective-permute-start.11 = (f32[128,128]{1,0:T(8,128)}, f32[128,128]{1,0:T(8,128)S(1)}, u32[]{:S(2)}, u32[]{:S(2)}) collective-permute-start(f32[128,128]{1,0:T(8,128)} %get-tuple-element.19), channel_id=1, source_target_pairs={{0,16},{8,24},{16,32},{24,40},{32,48},{40,56},{48,0},{56,8},{1,17}... | collective-permute-start | bytes 196616 | tf_op jit(solution)/shard_map/mass_over_ill/ppermute | solution.py:316
  55.5 6.6 %collective-permute-start.12 = (f32[128,128]{1,0:T(8,128)}, f32[128,128]{1,0:T(8,128)S(1)}, u32[]{:S(2)}, u32[]{:S(2)}) collective-permute-start(f32[128,128]{1,0:T(8,128)} %get-tuple-element.20), channel_id=1, source_target_pairs={{0,32},{8,40},{16,48},{24,56},{32,0},{40,8},{48,16},{56,24},{1,33}... | collective-permute-start | bytes 196616 | tf_op jit(solution)/shard_map/mass_over_ill/ppermute | solution.py:316
  57.2 4.9 %collective-permute-start.13 = (f32[128,128]{1,0:T(8,128)}, f32[128,128]{1,0:T(8,128)S(1)}, u32[]{:S(2)}, u32[]{:S(2)}) collective-permute-start(f32[128,128]{1,0:T(8,128)} %get-tuple-element.21), channel_id=1, source_target_pairs={{0,48},{8,56},{16,0},{24,8},{32,16},{40,24},{48,32},{56,40},{1,49}... | collective-permute-start | bytes 196616 | tf_op jit(solution)/shard_map/mass_over_ill/ppermute | solution.py:316
  58.2 0.6 %copy-start.7 = (f32[256,128]{1,0:T(8,128)}, f32[256,128]{1,0:T(8,128)S(1)}, u32[]{:S(2)}) copy-start(f32[256,128]{1,0:T(8,128)S(1)} %collective-permute-done.7.halo_ref) | copy-start | bytes 393220
  62.1 0.6 copy-start.9
  62.1 0.7 %copy-start.10 = (f32[128,128]{1,0:T(8,128)}, f32[128,128]{1,0:T(8,128)S(1)}, u32[]{:S(2)}) copy-start(f32[128,128]{1,0:T(8,128)S(1)} %collective-permute-done.12.s2) | copy-start | bytes 196612
  62.1 0.7 %copy-start.11 = (f32[128,128]{1,0:T(8,128)}, f32[128,128]{1,0:T(8,128)S(1)}, u32[]{:S(2)}) copy-start(f32[128,128]{1,0:T(8,128)S(1)} %collective-permute-done.13.s3) | copy-start | bytes 196612

commit v2 on v1

v2 whole, which is shorter than its diff:
```python
import functools

import jax
import jax.numpy as jnp
from jax import lax
from jax.experimental import pallas as pl
from jax.experimental.pallas import tpu as pltpu
from jax.sharding import PartitionSpec as P

DISCOUNT = 0.96
GROSS_RATE = 1.01
SLOPE_GAIN = 0.5
HIGHEST_PREC = lax.Precision.HIGHEST

Z = 32
LANES = 128
PLANE_ROWS = 4 * Z
HALF_ROWS = 2 * Z
KERNEL_VMEM = 4 << 20
VMEM = pltpu.VMEM
SMEM = pltpu.SMEM


def plane_of(ref, a, d):
    return ref[pl.ds(2 * d + a, Z, stride=4), :]


def dot_full(left, right):
    return jnp.dot(left, right, precision=HIGHEST_PREC, preferred_element_type=jnp.float32)


def split_lanes(wide, count):
    return [wide[:, i * LANES : (i + 1) * LANES] for i in range(count)]


def pack_kernel(v0, v1, v2, v3, out_ref):
    for q, ref in enumerate((v1, v2, v3)):
        for d in range(2):
            out_ref[(q + 1) * HALF_ROWS + d * Z : (q + 1) * HALF_ROWS + (d + 1) * Z, :] = plane_of(ref, 0, d)
    out_ref[:HALF_ROWS, :] = v0[:HALF_ROWS, :]


def interpolate(pieces, index, weight, me):
    upper_index = index + 1
    quarter = ((index >> 7) - me) & 3
    upper_quarter = ((upper_index >> 7) - me) & 3
    lane = index & 127
    upper_lane = upper_index & 127
    lower = upper = None
    for q, piece in enumerate(pieces):
        low = jnp.take_along_axis(piece, lane, axis=1, mode="promise_in_bounds")
        high = jnp.take_along_axis(piece, upper_lane, axis=1, mode="promise_in_bounds")
        lower = low if lower is None else jnp.where(quarter == q, low, lower)
        upper = high if upper is None else jnp.where(upper_quarter == q, high, upper)
    return weight * lower + (1.0 - weight) * upper


def policy_plane(own, above, drift, index, weight, me):
    endogenous = [lax.rsqrt(drift * o + (1.0 - drift) * u) for o, u in zip(own, above)]
    return interpolate(endogenous, index, weight, me)


def forward_half(
    a, own, above, drift, me, transition_ref,
    index_ref, weight_ref, steady_ref, lottery_ref, target_ref, population_ref,
    mass_scr, row_scr,
):
    values = []
    for d in range(2):
        index = plane_of(index_ref, a, d)
        weight = plane_of(weight_ref, a, d)
        policy = policy_plane(own[d], above[d], drift, index, weight, me)
        values.append(GROSS_RATE / (policy * policy))
        share = plane_of(lottery_ref, a, d) + SLOPE_GAIN * (policy - plane_of(steady_ref, a, d))
        share = jnp.clip(share, 0.0, 1.0)
        population = plane_of(population_ref, a, d)
        rows = slice(d * Z, (d + 1) * Z)
        mass_scr[0, rows, :] = population * share
        mass_scr[1, rows, :] = population * (1.0 - share)
    scaled = transition_ref[...] * (DISCOUNT * GROSS_RATE)
    expected = split_lanes(dot_full(scaled, jnp.concatenate(values, axis=1)), 2)

    sub8 = lax.broadcasted_iota(jnp.int32, (8, LANES), 0)
    is_low = sub8 < 4
    sub_quarter = sub8 & 3
    sub128 = lax.broadcasted_iota(jnp.int32, (LANES, LANES), 0)
    for d in range(2):
        for z in range(Z):
            row = d * Z + z
            target = target_ref[pl.ds(4 * z + 2 * d + a, 1), :]
            quarter = ((target >> 7) - me) & 3
            hot = jnp.where(sub128 == (target & 127), 1.0, 0.0).astype(jnp.bfloat16)
            mass = jnp.where(is_low, mass_scr[0, row : row + 1, :], mass_scr[1, row : row + 1, :])
            mass = jnp.where(quarter == sub_quarter, mass, 0.0)
            first = mass.astype(jnp.bfloat16)
            rest = mass - first.astype(jnp.float32)
            both = jnp.concatenate([mass, rest], axis=0).astype(jnp.bfloat16)
            out = lax.dot_general(both, hot, (((1,), (1,)), ((), ())), preferred_element_type=jnp.float32)
            row_scr[row * 8 : row * 8 + 8, :] = out[:8] + out[8:]
    lane = lax.broadcasted_iota(jnp.int32, (HALF_ROWS, LANES), 1)
    low = [row_scr[pl.ds(q, HALF_ROWS, stride=8), :] for q in range(4)]
    high = [pltpu.roll(row_scr[pl.ds(4 + q, HALF_ROWS, stride=8), :], 1, 1) for q in range(4)]
    rows_by_quarter = [low[q] + jnp.where(lane == 0, high[(q + 3) % 4], high[q]) for q in range(4)]
    return expected, rows_by_quarter


def last_drift(drift_ref):
    is_last = lax.axis_index("ill") == lax.axis_size("ill") - 1
    return jnp.where(is_last, 1.0, drift_ref[1])


def stay_of(keep_ref):
    return jnp.where(lax.axis_index("dur") == 0, 1.0, keep_ref[0]), keep_ref[1]


def rows_of(refs, p):
    return [ref[p * Z : (p + 1) * Z, :] for ref in refs]


def rows_of(refs, p):
    return [ref[p * Z : (p + 1) * Z, :] for ref in refs]


def first_half_kernel(
    small_ref, v0, v1, v2, v3, scaled_ref, transition_ref, index_ref, weight_ref, steady_ref, lottery_ref, target_ref,
    population_ref, mass_ref, expected_ref, upper_ref, mass_scr, row_scr,
):
    values = []
    for p in range(4):
        values += [v0[p * Z : (p + 1) * Z, :]] + [plane_of(ref, p // 2, p % 2) for ref in (v1, v2, v3)]
    planes = split_lanes(dot_full(scaled_ref[...], jnp.concatenate(values, axis=1)), 16)
    for i in range(8):
        upper_ref[i * Z : (i + 1) * Z, :] = planes[8 + i]
    expected, by_quarter = forward_half(
        0, [planes[0:4], planes[4:8]], [planes[8:12], planes[12:16]], small_ref[0:1, :],
        lax.axis_index("liq"), transition_ref, index_ref, weight_ref, steady_ref, lottery_ref, target_ref,
        population_ref, mass_scr, row_scr,
    )
    for q in range(4):
        mass_ref[q * HALF_ROWS : (q + 1) * HALF_ROWS, :] = by_quarter[q]
    for d in range(2):
        expected_ref[d * Z : (d + 1) * Z, :] = expected[d]


def second_half_kernel(
    small_ref, upper_ref, halo_ref, first_ref, scaled_ref, transition_ref, index_ref, weight_ref, steady_ref,
    lottery_ref, target_ref, population_ref, p0, p1, p2, p3, expected_ref, mass_scr, row_scr,
):
    own = [[upper_ref[(4 * d + q) * Z : (4 * d + q + 1) * Z, :] for q in range(4)] for d in range(2)]
    values = [halo_ref[q * HALF_ROWS + d * Z : q * HALF_ROWS + (d + 1) * Z, :] for d in range(2) for q in range(4)]
    planes = split_lanes(dot_full(scaled_ref[...], jnp.concatenate(values, axis=1)), 8)
    expected, by_quarter = forward_half(
        1, own, [planes[0:4], planes[4:8]], small_ref[1:2, :],
        lax.axis_index("liq"), transition_ref, index_ref, weight_ref, steady_ref, lottery_ref, target_ref,
        population_ref, mass_scr, row_scr,
    )
    for q, out in enumerate((p0, p1, p2, p3)):
        out[:HALF_ROWS, :] = first_ref[q * HALF_ROWS : (q + 1) * HALF_ROWS, :]
        out[HALF_ROWS:, :] = by_quarter[q]
    for d in range(2):
        expected_ref[d * Z : (d + 1) * Z, :] = expected[d]


def consume_kernel(small_ref, e0, e1, e2, e3, index_ref, weight_ref, out_ref):
    pieces = (e0, e1, e2, e3)
    for a in range(2):
        for d in range(2):
            policy = policy_plane(
                rows_of(pieces, 2 * a + d), rows_of(pieces, 2 * a + 2 + d), small_ref[a : a + 1, :],
                plane_of(index_ref, a, d), plane_of(weight_ref, a, d), lax.axis_index("liq"),
            )
            out_ref[pl.ds(2 * d + a, Z, stride=4), :] = policy


def gather_mass_kernel(small_ref, p0, p1, p2, p3, lower_ref, upper_ref, halo_ref, core_out, expected_out):
    core_out[:PLANE_ROWS, :] = (p0[...] + p1[...]) + (p2[...] + p3[...])
    core_out[PLANE_ROWS:, :] = small_ref[...]
    for i, ref in enumerate((lower_ref, upper_ref, halo_ref)):
        expected_out[i * HALF_ROWS : (i + 1) * HALF_ROWS, :] = ref[...]


def leave_kernel(own_ref, core_ref, dur_out):
    for i, ref in enumerate((own_ref, core_ref)):
        leave = 1.0 - ref[PLANE_ROWS + 2 : PLANE_ROWS + 3, :]
        for a in range(2):
            row = i * HALF_ROWS + a * Z
            dur_out[row : row + Z, :] = leave * ref[2 * a * Z : (2 * a + 1) * Z, :]
        dur_out[PLANE_ROWS + 8 * i : PLANE_ROWS + 8 * i + 8, :] = ref[PLANE_ROWS:, :]


def spread_targets(small):
    rows = lax.broadcasted_iota(jnp.int32, (Z, LANES), 0)
    lane = lax.broadcasted_iota(jnp.int32, (Z, LANES), 1)
    picked = [jnp.where(lane == rows, row, 0.0) for row in small]
    picked = jnp.concatenate(picked, axis=0).astype(jnp.bfloat16)
    ones = jnp.ones((LANES, LANES), jnp.bfloat16)
    return jnp.dot(picked, ones, preferred_element_type=jnp.float32)


def settle_kernel(own_ref, core_ref, dur_ref, o0, o1, o2, o3):
    sources = ([], [])
    for ref in (own_ref, core_ref):
        targets = spread_targets([ref[PLANE_ROWS + 4 + p : PLANE_ROWS + 5 + p, :] for p in range(4)])
        for p in range(4):
            sources[p % 2].append((targets[p * Z : (p + 1) * Z], ref[p * Z : (p + 1) * Z, :]))
    arriving = []
    targets = spread_targets(
        [dur_ref[PLANE_ROWS + i + p : PLANE_ROWS + i + p + 1, :] for i in (4, 12) for p in (0, 2)]
    )
    for i in range(4):
        arriving.append((targets[i * Z : (i + 1) * Z], dur_ref[i * Z : (i + 1) * Z, :]))
    ill = lax.axis_index("ill")
    y, core = ill >> 1, ill & 1
    stay_low, stay_high = own_ref[PLANE_ROWS + 2 : PLANE_ROWS + 3, :], own_ref[PLANE_ROWS + 3 : PLANE_ROWS + 4, :]
    leave_high = 1.0 - stay_high
    for k, out in enumerate((o0, o1, o2, o3)):
        for a in range(2):
            point = (4 * ((y + k) & 3) + 2 * core + a).astype(jnp.float32)

            def gathered(pairs):
                parts = [jnp.where(target == point, mass, 0.0) for target, mass in pairs]
                return (parts[0] + parts[1]) + (parts[2] + parts[3])

            low, high = gathered(sources[0]), gathered(sources[1])
            out[2 * a * Z : (2 * a + 1) * Z, :] = stay_low * low + leave_high * high
            out[(2 * a + 1) * Z : (2 * a + 2) * Z, :] = stay_high * high + gathered(arriving)


def population_kernel(transition_ref, s0, s1, s2, s3, out_ref):
    settled = (s0[...] + s1[...]) + (s2[...] + s3[...])
    wide = jnp.concatenate([settled[p * Z : (p + 1) * Z] for p in range(4)], axis=1)
    moved = lax.dot_general(
        transition_ref[...], wide, (((0,), (0,)), ((), ())), precision=HIGHEST_PREC, preferred_element_type=jnp.float32
    )
    for p, plane in enumerate(split_lanes(moved, 4)):
        a, d = p // 2, p % 2
        out_ref[pl.ds(2 * d + a, Z, stride=4), :] = plane


def call(kernel, out_rows, inputs, scratch=(), work=0):
    shapes = [jax.ShapeDtypeStruct(rows if isinstance(rows, tuple) else (rows, LANES), jnp.float32) for rows in out_rows]
    specs = [pl.BlockSpec(memory_space=VMEM) for _ in out_rows]
    single = len(out_rows) == 1
    return pl.pallas_call(
        kernel,
        out_shape=shapes[0] if single else shapes,
        in_specs=[pl.BlockSpec(memory_space=VMEM)] * len(inputs),
        out_specs=specs[0] if single else specs,
        scratch_shapes=list(scratch),
        compiler_params=pltpu.CompilerParams(vmem_limit_bytes=KERNEL_VMEM),
        cost_estimate=pl.CostEstimate(flops=0, transcendentals=0, bytes_accessed=work) if work else None,
    )(*inputs)


def turned(axis, distance):
    count = lax.axis_size(axis)
    return [(i, (i + distance) % count) for i in range(count)]


def from_other_liq(pieces):
    got = [lax.ppermute(pieces[k], "liq", turned("liq", k)) for k in range(1, 4)]
    return [got[3 - k] for k in range(1, 4)]


def from_above_ill(x):
    return lax.ppermute(x, "ill", turned("ill", -1))


def body(
    marginal_value, transition, discount_shock, illiquid_drift, durable_keep, bracket_index, bracket_weight,
    steady_consumption, lottery_weight, liquid_target, illiquid_target, population,
):
    flat = lambda x: x.reshape(PLANE_ROWS, LANES)
    ill_count, dur_count = lax.axis_size("ill"), lax.axis_size("dur")
    index, weight = flat(bracket_index), flat(bracket_weight)
    states = [index, weight] + [flat(x) for x in (steady_consumption, lottery_weight, liquid_target, population)]
    scratch = [pltpu.VMEM((2, HALF_ROWS, LANES), jnp.float32), pltpu.VMEM((8 * HALF_ROWS, LANES), jnp.float32)]
    below_dur = [(d, d - 1) for d in range(1, dur_count)]
    other_core = [(i, i ^ 1) for i in range(ill_count)]

    with jax.named_scope("value_over_liq"):
        value = flat(marginal_value)
        pieces = [marginal_value.transpose(2, 1, 0, 3).reshape(PLANE_ROWS, LANES)] + from_other_liq([value] * 4)
    with jax.named_scope("prepare"):
        scaled = transition * (discount_shock * (DISCOUNT * GROSS_RATE))[:, None]
        is_last = lax.axis_index("ill") == ill_count - 1
        is_lowest = lax.axis_index("dur") == 0
        row = lax.broadcasted_iota(jnp.int32, (8, LANES), 0)
        drift = jnp.where(row[:2] == 0, illiquid_drift[:, None], jnp.where(is_last, 1.0, illiquid_drift[:, None]))
        stay = jnp.where((row[:2] == 0) & is_lowest, 1.0, durable_keep[:, None])
        target = illiquid_target.transpose(2, 1, 0).reshape(4, Z).astype(jnp.float32)
        small = jnp.concatenate([drift, stay, jnp.pad(target, ((0, 0), (0, LANES - Z)))], axis=0)
    with jax.named_scope("value_over_ill"):
        halo = from_above_ill(call(pack_kernel, [4 * HALF_ROWS], pieces))
    with jax.named_scope("first_half"):
        mass, lower, upper = call(
            first_half_kernel,
            [4 * HALF_ROWS, HALF_ROWS, 4 * HALF_ROWS],
            [small, *pieces, scaled, transition, *states],
            scratch,
        )
    with jax.named_scope("expected_over_ill"):
        next_halo = from_above_ill(lower)
    with jax.named_scope("second_half"):
        *sends, higher = call(
            second_half_kernel,
            [PLANE_ROWS] * 4 + [HALF_ROWS],
            [small, upper, halo, mass, scaled, transition, *states],
            scratch,
            30000000,
        )
    with jax.named_scope("mass_over_liq"):
        got = [sends[0]] + from_other_liq(sends)
    with jax.named_scope("gather_mass"):
        to_core, expected = call(
            gather_mass_kernel, [PLANE_ROWS + 8, 3 * HALF_ROWS], [small, *got, lower, higher, next_halo]
        )
    with jax.named_scope("mass_over_core"):
        from_core = lax.ppermute(to_core, "ill", other_core)
    with jax.named_scope("leave"):
        to_dur = call(leave_kernel, [PLANE_ROWS + 16], [to_core, from_core])
    with jax.named_scope("mass_over_dur"):
        from_dur = lax.ppermute(to_dur, "dur", below_dur)
    with jax.named_scope("expected_over_liq"):
        expected_pieces = [expected] + from_other_liq([expected] * 4)
    with jax.named_scope("settle"):
        parts = call(settle_kernel, [PLANE_ROWS] * 4, [to_core, from_core, from_dur])
    with jax.named_scope("mass_over_ill"):
        arrived = [lax.ppermute(parts[k], "ill", turned("ill", 2 * k)) for k in range(1, 4)]
    with jax.named_scope("consume"):
        consumption = call(consume_kernel, [PLANE_ROWS], [small, *expected_pieces, index, weight])
    with jax.named_scope("population"):
        population_next = call(population_kernel, [PLANE_ROWS], [transition, parts[0], *arrived])
    shape = population.shape
    return consumption.reshape(shape), population_next.reshape(shape)


def solution(mesh):
    state = P(None, "dur", "ill", "liq")
    in_specs = (
        state, P(), P(), P("ill"), P("dur"), state, state, state, state, state, P(None, "dur", "ill"), state,
    )
    return jax.shard_map(body, mesh=mesh, in_specs=in_specs, out_specs=(state, state), check_vma=False)
```

time: 65.4 us -> 42.5 us (0.65)
  the two profiles are of different devices: /device:TPU:1 before, /device:TPU:96 now
where the time goes in v2:
time: 42.5 us; the launch traced here: 42.2 us
  starting transfers between devices  21.9 us (52%)
  waiting for transfers between devices  10.6 us (25%)
  Pallas kernels  5.89 us (14%)
  local copies, waits for them, and re-layouts  2.21 us (5%)
  other arithmetic  0.82 us (2%)
  between operations  0.77 us (2%)
    ppermute x9, starting transfers between devices, from_other_liq(): lax.ppermute(pieces[k], 'liq', turned('liq', k))  11 us
    pallas_call x8, Pallas kernels, call(): pl.pallas_call(kernel, out_shape=shapes[0] if single else shapes, in_spec...  5.89 us
    ppermute x3, starting transfers between devices, body(): lax.ppermute(parts[k], 'ill', turned('ill', 2 * k))  5.53 us
    ppermute x2, starting transfers between devices, from_above_ill(): return lax.ppermute(x, 'ill', turned('ill', -1))  3.28 us
    ppermute x9, waiting for transfers between devices, from_other_liq(): lax.ppermute(pieces[k], 'liq', turned('liq', k))  3.01 us
    ppermute x1, waiting for transfers between devices, body(): from_dur = lax.ppermute(to_dur, 'dur', below_dur)  2.7 us
    ppermute x2, waiting for transfers between devices, from_above_ill(): return lax.ppermute(x, 'ill', turned('ill', -1))  2.19 us
    ppermute x1, starting transfers between devices, body(): from_dur = lax.ppermute(to_dur, 'dur', below_dur)  2.01 us
  transfers between devices with their start and end apart: 16, of which 9 were waited for; matrix products, arithmetic and copies ran while one was open for 4% of the time, Pallas kernels for 8%

profile of v2, /device:TPU:96, one launch (start us, length us, event | category | flops | bytes accessed | tf_op | source)
XLA Modules:
  0.0 42.2 jit_solution(18243523372067334973)
XLA Ops:
  0.6 0.0 copy-start.6
  0.6 2.8 %collective-permute-start = (f32[128,128]{1,0:T(8,128)}, f32[128,128]{1,0:T(8,128)S(1)}, u32[]{:S(2)}, u32[]{:S(2)}) collective-permute-start(f32[128,128]{1,0:T(8,128)} %bitcast.31), channel_id=1, source_target_pairs={{0,192},{64,0},{128,64},{192,128},{1,193},{65,1},{129,65},{193,129... | collective-permute-start | bytes 196616 | tf_op jit(solution)/shard_map/value_over_liq/ppermute | solution.py:261
  3.5 0.8 %collective-permute-start.1 = (f32[128,128]{1,0:T(8,128)}, f32[128,128]{1,0:T(8,128)S(1)}, u32[]{:S(2)}, u32[]{:S(2)}) collective-permute-start(f32[128,128]{1,0:T(8,128)} %bitcast.32), channel_id=1, source_target_pairs={{0,128},{64,192},{128,0},{192,64},{1,129},{65,193},{129,1},{193,65... | collective-permute-start | bytes 196616 | tf_op jit(solution)/shard_map/value_over_liq/ppermute | solution.py:261
  4.3 0.9 %collective-permute-start.2 = (f32[128,128]{1,0:T(8,128)}, f32[128,128]{1,0:T(8,128)S(1)}, u32[]{:S(2)}, u32[]{:S(2)}) collective-permute-start(f32[128,128]{1,0:T(8,128)} %bitcast.33), channel_id=1, source_target_pairs={{0,64},{64,128},{128,192},{192,0},{1,65},{65,129},{129,193},{193,1... | collective-permute-start | bytes 196616 | tf_op jit(solution)/shard_map/value_over_liq/ppermute | solution.py:261
  5.2 0.7 %broadcast_multiply_fusion.1 = f32[32]{0:T(128)S(1)} fusion(f32[32]{0:T(128)} %param.14), kind=kLoop, calls=%fused_computation.8 | loop fusion | flops 32 | bytes 256 | tf_op jit(solution)/shard_map/prepare/mul | solution.py:285
  5.8 0.0 copy-start.8
  5.8 0.7 %copy-done.8 = f32[2]{0:T(128)S(1)} copy-done((f32[2]{0:T(128)S(1)}, f32[2]{0:T(128)}, u32[]{:S(2)}) %copy-start.8) | copy-done | bytes 32
  6.5 0.0 copy-done.6
  6.5 0.1 broadcast_multiply_fusion.scaled_ref
  6.6 0.0 copy-start.9
  6.6 0.7 %copy-done.9 = f32[2]{0:T(128)S(1)} copy-done((f32[2]{0:T(128)S(1)}, f32[2]{0:T(128)}, u32[]{:S(2)}) %copy-start.9) | copy-done | bytes 32
  7.2 0.1 broadcast_select_fusion.1
  7.3 0.0 copy-start.7
  7.3 0.9 %copy.15 = f32[2,2,32,128]{3,2,1,0:T(8,128)S(1)} copy(f32[2,2,32,128]{3,0,1,2:T(2,128)} %bitcast.34) | data formatting | bytes 131072 | tf_op jit(solution)/shard_map/value_over_liq/transpose | solution.py:283
  8.1 0.0 collective-permute-done.v1
  8.1 1.3 %collective-permute-done.1.v2 = f32[128,128]{1,0:T(8,128)S(1)} collective-permute-done((f32[128,128]{1,0:T(8,128)}, f32[128,128]{1,0:T(8,128)S(1)}, u32[]{:S(2)}, u32[]{:S(2)}) %collective-permute-start.1) | collective-permute-done | bytes 65568 | tf_op jit(solution)/shard_map/value_over_liq/ppermute | solution.py:261
  9.5 0.7 %collective-permute-done.2.v3 = f32[128,128]{1,0:T(8,128)S(1)} collective-permute-done((f32[128,128]{1,0:T(8,128)}, f32[128,128]{1,0:T(8,128)S(1)}, u32[]{:S(2)}, u32[]{:S(2)}) %collective-permute-start.2) | collective-permute-done | bytes 65568 | tf_op jit(solution)/shard_map/value_over_liq/ppermute | solution.py:261
  10.2 0.0 copy-start
  10.2 0.0 copy-start.1
  10.2 0.0 copy-start.2
  10.2 0.0 copy-start.3
  10.2 0.0 copy-start.4
  10.2 0.0 copy-start.5
  10.2 1.0 %collective-permute-start.3 = (f32[256,128]{1,0:T(8,128)S(1)}, f32[256,128]{1,0:T(8,128)S(1)}, u32[]{:S(2)}, u32[]{:S(2)}) collective-permute-start(f32[256,128]{1,0:T(8,128)S(1)} %value_over_ill.1), channel_id=1, source_target_pairs={{0,56},{8,0},{16,8},{24,16},{32,24},{40,32},{48,40},{56,48},{1,57}... | collective-permute-start | bytes 393224 | tf_op jit(solution)/shard_map/value_over_ill/ppermute | solution.py:266
  11.2 0.0 copy-done.7
  11.3 0.0 copy-done
  11.3 0.0 copy-done.1
  11.3 0.0 copy-done.2
  11.3 0.0 copy-done.3
  11.3 0.0 copy-done.4
  11.3 0.0 copy-done.5
  11.3 1.8 %first_half.1 = (f32[256,128]{1,0:T(8,128)S(1)}, f32[64,128]{1,0:T(8,128)S(1)}, f32[256,128]{1,0:T(8,128)S(1)}) custom-call(f32[8,128]{1,0:T(8,128)S(1)} %select_maximum_fusion.small_ref, f32[128,128]{1,0:T(8,128)S(1)} %bitcast.21, f32[128,128]{1,0:T(8,128)S(1)} %collective-permute-done.v1, f32[128,128]{1,0:T(8,128)S(1)} %collective-permute-done.1.v2, ...), custom_call_target="tpu_custom_call" | custom-call | tf_op jit(solution)/shard_map/first_half/pallas_call | solution.py:244
  13.2 0.6 %collective-permute-done.3.halo_ref = f32[256,128]{1,0:T(8,128)S(1)} collective-permute-done((f32[256,128]{1,0:T(8,128)S(1)}, f32[256,128]{1,0:T(8,128)S(1)}, u32[]{:S(2)}, u32[]{:S(2)}) %collective-permute-start.3) | collective-permute-done | bytes 131104 | tf_op jit(solution)/shard_map/value_over_ill/ppermute | solution.py:266
  13.8 1.7 %second_half.1 = (f32[128,128]{1,0:T(8,128)S(1)}, f32[128,128]{1,0:T(8,128)S(1)}, f32[128,128]{1,0:T(8,128)S(1)}, f32[128,128]{1,0:T(8,128)S(1)}, f32[64,128]{1,0:T(8,128)S(1)}) custom-call(f32[8,128]{1,0:T(8,128)S(1)} %select_maximum_fusion.small_ref, f32[256,128]{1,0:T(8,128)S(1)} %get-tuple-element.16.upper_ref, ...), custom_call_target="tpu_custom_call" | custom-call | bytes 30000000 | tf_op jit(solution)/shard_map/second_half/pallas_call | solution.py:244
  15.5 1.0 %collective-permute-start.4 = (f32[128,128]{1,0:T(8,128)S(1)}, f32[128,128]{1,0:T(8,128)S(1)}, u32[]{:S(2)}, u32[]{:S(2)}) collective-permute-start(f32[128,128]{1,0:T(8,128)S(1)} %get-tuple-element.19), channel_id=1, source_target_pairs={{0,192},{64,0},{128,64},{192,128},{1,193},{65,1},{129,65},{193,129... | collective-permute-start | bytes 196616 | tf_op jit(solution)/shard_map/mass_over_liq/ppermute | solution.py:261
  16.5 1.5 %collective-permute-start.5 = (f32[128,128]{1,0:T(8,128)S(1)}, f32[128,128]{1,0:T(8,128)S(1)}, u32[]{:S(2)}, u32[]{:S(2)}) collective-permute-start(f32[128,128]{1,0:T(8,128)S(1)} %get-tuple-element.20), channel_id=1, source_target_pairs={{0,128},{64,192},{128,0},{192,64},{1,129},{65,193},{129,1},{193,65... | collective-permute-start | bytes 196616 | tf_op jit(solution)/shard_map/mass_over_liq/ppermute | solution.py:261
  18.0 0.7 %collective-permute-start.6 = (f32[128,128]{1,0:T(8,128)S(1)}, f32[128,128]{1,0:T(8,128)S(1)}, u32[]{:S(2)}, u32[]{:S(2)}) collective-permute-start(f32[128,128]{1,0:T(8,128)S(1)} %get-tuple-element.21), channel_id=1, source_target_pairs={{0,64},{64,128},{128,192},{192,0},{1,65},{65,129},{129,193},{193,1... | collective-permute-start | bytes 196616 | tf_op jit(solution)/shard_map/mass_over_liq/ppermute | solution.py:261
  18.8 2.2 %collective-permute-start.7 = (f32[64,128]{1,0:T(8,128)S(1)}, f32[64,128]{1,0:T(8,128)S(1)}, u32[]{:S(2)}, u32[]{:S(2)}) collective-permute-start(f32[64,128]{1,0:T(8,128)S(1)} %get-tuple-element.22.lower_ref), channel_id=1, source_target_pairs={{0,56},{8,0},{16,8},{24,16},{32,24},{40,32},{48,40},{56,48},{1,57}... | collective-permute-start | bytes 98312 | tf_op jit(solution)/shard_map/expected_over_ill/ppermute | solution.py:266
  21.0 1.6 %collective-permute-done.7.halo_ref = f32[64,128]{1,0:T(8,128)S(1)} collective-permute-done((f32[64,128]{1,0:T(8,128)S(1)}, f32[64,128]{1,0:T(8,128)S(1)}, u32[]{:S(2)}, u32[]{:S(2)}) %collective-permute-start.7) | collective-permute-done | bytes 32800 | tf_op jit(solution)/shard_map/expected_over_ill/ppermute | solution.py:266
  22.6 0.0 collective-permute-done.4.p1
  22.6 0.0 collective-permute-done.5.p2
  22.6 1.0 %collective-permute-done.6.p3 = f32[128,128]{1,0:T(8,128)S(1)} collective-permute-done((f32[128,128]{1,0:T(8,128)S(1)}, f32[128,128]{1,0:T(8,128)S(1)}, u32[]{:S(2)}, u32[]{:S(2)}) %collective-permute-start.6) | collective-permute-done | bytes 65568 | tf_op jit(solution)/shard_map/mass_over_liq/ppermute | solution.py:261
  23.6 0.1 collective-permute-start.11
  23.7 0.3 collective-permute-start.10
  24.1 0.9 %collective-permute-done.11.core_ref = f32[136,128]{1,0:T(8,128)S(1)} collective-permute-done((f32[136,128]{1,0:T(8,128)S(1)}, f32[136,128]{1,0:T(8,128)S(1)}, u32[]{:S(2)}, u32[]{:S(2)}) %collective-permute-start.11) | collective-permute-done | bytes 69664 | tf_op jit(solution)/shard_map/mass_over_core/ppermute | solution.py:319
  25.0 2.0 %collective-permute-start.12 = (f32[144,128]{1,0:T(8,128)S(1)}, f32[144,128]{1,0:T(8,128)S(1)}, u32[]{:S(2)}, u32[]{:S(2)}) collective-permute-start(f32[144,128]{1,0:T(8,128)S(1)} %leave.1), channel_id=1, source_target_pairs={{1,0},{2,1},{3,2},{4,3},{5,4},{6,5},{7,6},{9,8},{10,9},{11,10},{12... | collective-permute-start | bytes 221192 | tf_op jit(solution)/shard_map/mass_over_dur/ppermute | solution.py:323
  27.0 2.1 %collective-permute-start.8 = (f32[192,128]{1,0:T(8,128)S(1)}, f32[192,128]{1,0:T(8,128)S(1)}, u32[]{:S(2)}, u32[]{:S(2)}) collective-permute-start(f32[192,128]{1,0:T(8,128)S(1)} %get-tuple-element.24.e0), channel_id=1, source_target_pairs={{0,192},{64,0},{128,64},{192,128},{1,193},{65,1},{129,65},{193,129... | collective-permute-start | bytes 294920 | tf_op jit(solution)/shard_map/expected_over_liq/ppermute | solution.py:261
  29.2 0.7 %collective-permute-start.9 = (f32[192,128]{1,0:T(8,128)S(1)}, f32[192,128]{1,0:T(8,128)S(1)}, u32[]{:S(2)}, u32[]{:S(2)}) collective-permute-start(f32[192,128]{1,0:T(8,128)S(1)} %get-tuple-element.24.e0), channel_id=1, source_target_pairs={{0,128},{64,192},{128,0},{192,64},{1,129},{65,193},{129,1},{193,65... | collective-permute-start | bytes 294920 | tf_op jit(solution)/shard_map/expected_over_liq/ppermute | solution.py:261
  29.9 2.7 %collective-permute-done.12.dur_ref = f32[144,128]{1,0:T(8,128)S(1)} collective-permute-done((f32[144,128]{1,0:T(8,128)S(1)}, f32[144,128]{1,0:T(8,128)S(1)}, u32[]{:S(2)}, u32[]{:S(2)}) %collective-permute-start.12) | collective-permute-done | bytes 73760 | tf_op jit(solution)/shard_map/mass_over_dur/ppermute | solution.py:323
  32.6 0.3 settle.1
  32.9 1.3 %collective-permute-start.13 = (f32[128,128]{1,0:T(8,128)S(1)}, f32[128,128]{1,0:T(8,128)S(1)}, u32[]{:S(2)}, u32[]{:S(2)}) collective-permute-start(f32[128,128]{1,0:T(8,128)S(1)} %get-tuple-element.27), channel_id=1, source_target_pairs={{0,16},{8,24},{16,32},{24,40},{32,48},{40,56},{48,0},{56,8},{1,17}... | collective-permute-start | bytes 196616 | tf_op jit(solution)/shard_map/mass_over_ill/ppermute | solution.py:329
  34.2 2.9 %collective-permute-start.14 = (f32[128,128]{1,0:T(8,128)S(1)}, f32[128,128]{1,0:T(8,128)S(1)}, u32[]{:S(2)}, u32[]{:S(2)}) collective-permute-start(f32[128,128]{1,0:T(8,128)S(1)} %get-tuple-element.28), channel_id=1, source_target_pairs={{0,32},{8,40},{16,48},{24,56},{32,0},{40,8},{48,16},{56,24},{1,33}... | collective-permute-start | bytes 196616 | tf_op jit(solution)/shard_map/mass_over_ill/ppermute | solution.py:329
  37.1 0.0 collective-permute-done.10.e3
  37.1 1.4 %collective-permute-start.15 = (f32[128,128]{1,0:T(8,128)S(1)}, f32[128,128]{1,0:T(8,128)S(1)}, u32[]{:S(2)}, u32[]{:S(2)}) collective-permute-start(f32[128,128]{1,0:T(8,128)S(1)} %get-tuple-element.29), channel_id=1, source_target_pairs={{0,48},{8,56},{16,0},{24,8},{32,16},{40,24},{48,32},{56,40},{1,49}... | collective-permute-start | bytes 196616 | tf_op jit(solution)/shard_map/mass_over_ill/ppermute | solution.py:329
  38.5 0.0 collective-permute-done.8.e1
  38.5 0.0 collective-permute-done.9.e2
  38.5 1.1 %consume.1 = f32[128,128]{1,0:T(8,128)} custom-call(f32[8,128]{1,0:T(8,128)S(1)} %select_maximum_fusion.small_ref, f32[192,128]{1,0:T(8,128)S(1)} %get-tuple-element.24.e0, f32[192,128]{1,0:T(8,128)S(1)} %collective-permute-done.8.e1, f32[192,128]{1,0:T(8,128)S(1)} %collective-permute-done.9.e2, f32[192,128]{1,0:T(8,128)S(1)} %collective-permute-done.10.e3, ...), custom_call_target="tpu_custom_call" | custom-call | tf_op jit(solution)/shard_map/consume/pallas_call | solution.py:244
  39.5 0.0 collective-permute-done.13.s1
  39.5 0.5 %collective-permute-done.14.s2 = f32[128,128]{1,0:T(8,128)S(1)} collective-permute-done((f32[128,128]{1,0:T(8,128)S(1)}, f32[128,128]{1,0:T(8,128)S(1)}, u32[]{:S(2)}, u32[]{:S(2)}) %collective-permute-start.14) | collective-permute-done | bytes 65568 | tf_op jit(solution)/shard_map/mass_over_ill/ppermute | solution.py:329
  40.0 1.3 %collective-permute-done.15.s3 = f32[128,128]{1,0:T(8,128)S(1)} collective-permute-done((f32[128,128]{1,0:T(8,128)S(1)}, f32[128,128]{1,0:T(8,128)S(1)}, u32[]{:S(2)}, u32[]{:S(2)}) %collective-permute-start.15) | collective-permute-done | bytes 65568 | tf_op jit(solution)/shard_map/mass_over_ill/ppermute | solution.py:329
  41.4 0.9 %population.1 = f32[128,128]{1,0:T(8,128)} custom-call(f32[32,32]{1,0:T(8,128)S(1)} %copy-done.6, f32[128,128]{1,0:T(8,128)S(1)} %get-tuple-element.26.s0, f32[128,128]{1,0:T(8,128)S(1)} %collective-permute-done.13.s1, f32[128,128]{1,0:T(8,128)S(1)} %collective-permute-done.14.s2, f32[128,128]{1,0:T(8,128)S(1)} %collective-permute-done.15.s3), custom_call_target="tpu_custom_call" | custom-call | tf_op jit(solution)/shard_map/population/pallas_call | solution.py:244
  (8 shorter events, 0.1 us)
Async XLA Ops:
  0.6 5.9 %copy-start.6 = (f32[32,32]{1,0:T(8,128)S(1)}, f32[32,32]{1,0:T(8,128)}, u32[]{:S(2)}) copy-start(f32[32,32]{1,0:T(8,128)} %transition_ref.5) | copy-start | bytes 12292
  0.6 7.5 %collective-permute-start = (f32[128,128]{1,0:T(8,128)}, f32[128,128]{1,0:T(8,128)S(1)}, u32[]{:S(2)}, u32[]{:S(2)}) collective-permute-start(f32[128,128]{1,0:T(8,128)} %bitcast.31), channel_id=1, source_target_pairs={{0,192},{64,0},{128,64},{192,128},{1,193},{65,1},{129,65},{193,129... | collective-permute-start | bytes 196616 | tf_op jit(solution)/shard_map/value_over_liq/ppermute | solution.py:261
  3.5 6.0 %collective-permute-start.1 = (f32[128,128]{1,0:T(8,128)}, f32[128,128]{1,0:T(8,128)S(1)}, u32[]{:S(2)}, u32[]{:S(2)}) collective-permute-start(f32[128,128]{1,0:T(8,128)} %bitcast.32), channel_id=1, source_target_pairs={{0,128},{64,192},{128,0},{192,64},{1,129},{65,193},{129,1},{193,65... | collective-permute-start | bytes 196616 | tf_op jit(solution)/shard_map/value_over_liq/ppermute | solution.py:261
  4.3 5.9 %collective-permute-start.2 = (f32[128,128]{1,0:T(8,128)}, f32[128,128]{1,0:T(8,128)S(1)}, u32[]{:S(2)}, u32[]{:S(2)}) collective-permute-start(f32[128,128]{1,0:T(8,128)} %bitcast.33), channel_id=1, source_target_pairs={{0,64},{64,128},{128,192},{192,0},{1,65},{65,129},{129,193},{193,1... | collective-permute-start | bytes 196616 | tf_op jit(solution)/shard_map/value_over_liq/ppermute | solution.py:261
  5.8 0.7 %copy-start.8 = (f32[2]{0:T(128)S(1)}, f32[2]{0:T(128)}, u32[]{:S(2)}) copy-start(f32[2]{0:T(128)} %param.15) | copy-start | bytes 28
  6.6 0.7 %copy-start.9 = (f32[2]{0:T(128)S(1)}, f32[2]{0:T(128)}, u32[]{:S(2)}) copy-start(f32[2]{0:T(128)} %param.16) | copy-start | bytes 28
  7.3 4.0 %copy-start.7 = (s32[32,2,2]{0,2,1:T(2,128)S(1)}, s32[32,2,2]{0,2,1:T(2,128)}, u32[]{:S(2)}) copy-start(s32[32,2,2]{0,2,1:T(2,128)} %param.22) | copy-start | bytes 1540
  10.2 1.1 %copy-start = (s32[32,2,2,128]{3,2,1,0:T(2,128)S(1)}, s32[32,2,2,128]{3,2,1,0:T(2,128)}, u32[]{:S(2)}) copy-start(s32[32,2,2,128]{3,2,1,0:T(2,128)} %param.17) | copy-start | bytes 196612
  10.2 1.1 %copy-start.1 = (f32[32,2,2,128]{3,2,1,0:T(2,128)S(1)}, f32[32,2,2,128]{3,2,1,0:T(2,128)}, u32[]{:S(2)}) copy-start(f32[32,2,2,128]{3,2,1,0:T(2,128)} %param.18) | copy-start | bytes 196612
  10.2 1.1 %copy-start.2 = (f32[32,2,2,128]{3,2,1,0:T(2,128)S(1)}, f32[32,2,2,128]{3,2,1,0:T(2,128)}, u32[]{:S(2)}) copy-start(f32[32,2,2,128]{3,2,1,0:T(2,128)} %param.19) | copy-start | bytes 196612
  10.2 1.1 %copy-start.3 = (f32[32,2,2,128]{3,2,1,0:T(2,128)S(1)}, f32[32,2,2,128]{3,2,1,0:T(2,128)}, u32[]{:S(2)}) copy-start(f32[32,2,2,128]{3,2,1,0:T(2,128)} %param.20) | copy-start | bytes 196612
  10.2 1.1 %copy-start.4 = (s32[32,2,2,128]{3,2,1,0:T(2,128)S(1)}, s32[32,2,2,128]{3,2,1,0:T(2,128)}, u32[]{:S(2)}) copy-start(s32[32,2,2,128]{3,2,1,0:T(2,128)} %param.21) | copy-start | bytes 196612
  10.2 1.1 %copy-start.5 = (f32[32,2,2,128]{3,2,1,0:T(2,128)S(1)}, f32[32,2,2,128]{3,2,1,0:T(2,128)}, u32[]{:S(2)}) copy-start(f32[32,2,2,128]{3,2,1,0:T(2,128)} %param.23) | copy-start | bytes 196612
  10.2 3.6 %collective-permute-start.3 = (f32[256,128]{1,0:T(8,128)S(1)}, f32[256,128]{1,0:T(8,128)S(1)}, u32[]{:S(2)}, u32[]{:S(2)}) collective-permute-start(f32[256,128]{1,0:T(8,128)S(1)} %value_over_ill.1), channel_id=1, source_target_pairs={{0,56},{8,0},{16,8},{24,16},{32,24},{40,32},{48,40},{56,48},{1,57}... | collective-permute-start | bytes 393224 | tf_op jit(solution)/shard_map/value_over_ill/ppermute | solution.py:266
  15.5 7.1 %collective-permute-start.4 = (f32[128,128]{1,0:T(8,128)S(1)}, f32[128,128]{1,0:T(8,128)S(1)}, u32[]{:S(2)}, u32[]{:S(2)}) collective-permute-start(f32[128,128]{1,0:T(8,128)S(1)} %get-tuple-element.19), channel_id=1, source_target_pairs={{0,192},{64,0},{128,64},{192,128},{1,193},{65,1},{129,65},{193,129... | collective-permute-start | bytes 196616 | tf_op jit(solution)/shard_map/mass_over_liq/ppermute | solution.py:261
  16.5 6.1 %collective-permute-start.5 = (f32[128,128]{1,0:T(8,128)S(1)}, f32[128,128]{1,0:T(8,128)S(1)}, u32[]{:S(2)}, u32[]{:S(2)}) collective-permute-start(f32[128,128]{1,0:T(8,128)S(1)} %get-tuple-element.20), channel_id=1, source_target_pairs={{0,128},{64,192},{128,0},{192,64},{1,129},{65,193},{129,1},{193,65... | collective-permute-start | bytes 196616 | tf_op jit(solution)/shard_map/mass_over_liq/ppermute | solution.py:261
  18.0 5.6 %collective-permute-start.6 = (f32[128,128]{1,0:T(8,128)S(1)}, f32[128,128]{1,0:T(8,128)S(1)}, u32[]{:S(2)}, u32[]{:S(2)}) collective-permute-start(f32[128,128]{1,0:T(8,128)S(1)} %get-tuple-element.21), channel_id=1, source_target_pairs={{0,64},{64,128},{128,192},{192,0},{1,65},{65,129},{129,193},{193,1... | collective-permute-start | bytes 196616 | tf_op jit(solution)/shard_map/mass_over_liq/ppermute | solution.py:261
  18.8 3.8 %collective-permute-start.7 = (f32[64,128]{1,0:T(8,128)S(1)}, f32[64,128]{1,0:T(8,128)S(1)}, u32[]{:S(2)}, u32[]{:S(2)}) collective-permute-start(f32[64,128]{1,0:T(8,128)S(1)} %get-tuple-element.22.lower_ref), channel_id=1, source_target_pairs={{0,56},{8,0},{16,8},{24,16},{32,24},{40,32},{48,40},{56,48},{1,57}... | collective-permute-start | bytes 98312 | tf_op jit(solution)/shard_map/expected_over_ill/ppermute | solution.py:266
  23.6 1.3 %collective-permute-start.11 = (f32[136,128]{1,0:T(8,128)S(1)}, f32[136,128]{1,0:T(8,128)S(1)}, u32[]{:S(2)}, u32[]{:S(2)}) collective-permute-start(f32[136,128]{1,0:T(8,128)S(1)} %get-tuple-element.25.own_ref), channel_id=1, source_target_pairs={{0,8},{8,0},{16,24},{24,16},{32,40},{40,32},{48,56},{56,48},{1,9},... | collective-permute-start | bytes 208904 | tf_op jit(solution)/shard_map/mass_over_core/ppermute | solution.py:319
  23.7 13.4 %collective-permute-start.10 = (f32[192,128]{1,0:T(8,128)S(1)}, f32[192,128]{1,0:T(8,128)S(1)}, u32[]{:S(2)}, u32[]{:S(2)}) collective-permute-start(f32[192,128]{1,0:T(8,128)S(1)} %get-tuple-element.24.e0), channel_id=1, source_target_pairs={{0,64},{64,128},{128,192},{192,0},{1,65},{65,129},{129,193},{193,1... | collective-permute-start | bytes 294920 | tf_op jit(solution)/shard_map/expected_over_liq/ppermute | solution.py:261
  25.0 7.6 %collective-permute-start.12 = (f32[144,128]{1,0:T(8,128)S(1)}, f32[144,128]{1,0:T(8,128)S(1)}, u32[]{:S(2)}, u32[]{:S(2)}) collective-permute-start(f32[144,128]{1,0:T(8,128)S(1)} %leave.1), channel_id=1, source_target_pairs={{1,0},{2,1},{3,2},{4,3},{5,4},{6,5},{7,6},{9,8},{10,9},{11,10},{12... | collective-permute-start | bytes 221192 | tf_op jit(solution)/shard_map/mass_over_dur/ppermute | solution.py:323
  27.0 11.4 %collective-permute-start.8 = (f32[192,128]{1,0:T(8,128)S(1)}, f32[192,128]{1,0:T(8,128)S(1)}, u32[]{:S(2)}, u32[]{:S(2)}) collective-permute-start(f32[192,128]{1,0:T(8,128)S(1)} %get-tuple-element.24.e0), channel_id=1, source_target_pairs={{0,192},{64,0},{128,64},{192,128},{1,193},{65,1},{129,65},{193,129... | collective-permute-start | bytes 294920 | tf_op jit(solution)/shard_map/expected_over_liq/ppermute | solution.py:261
  29.2 9.3 %collective-permute-start.9 = (f32[192,128]{1,0:T(8,128)S(1)}, f32[192,128]{1,0:T(8,128)S(1)}, u32[]{:S(2)}, u32[]{:S(2)}) collective-permute-start(f32[192,128]{1,0:T(8,128)S(1)} %get-tuple-element.24.e0), channel_id=1, source_target_pairs={{0,128},{64,192},{128,0},{192,64},{1,129},{65,193},{129,1},{193,65... | collective-permute-start | bytes 294920 | tf_op jit(solution)/shard_map/expected_over_liq/ppermute | solution.py:261
  32.9 6.6 %collective-permute-start.13 = (f32[128,128]{1,0:T(8,128)S(1)}, f32[128,128]{1,0:T(8,128)S(1)}, u32[]{:S(2)}, u32[]{:S(2)}) collective-permute-start(f32[128,128]{1,0:T(8,128)S(1)} %get-tuple-element.27), channel_id=1, source_target_pairs={{0,16},{8,24},{16,32},{24,40},{32,48},{40,56},{48,0},{56,8},{1,17}... | collective-permute-start | bytes 196616 | tf_op jit(solution)/shard_map/mass_over_ill/ppermute | solution.py:329
  34.2 5.8 %collective-permute-start.14 = (f32[128,128]{1,0:T(8,128)S(1)}, f32[128,128]{1,0:T(8,128)S(1)}, u32[]{:S(2)}, u32[]{:S(2)}) collective-permute-start(f32[128,128]{1,0:T(8,128)S(1)} %get-tuple-element.28), channel_id=1, source_target_pairs={{0,32},{8,40},{16,48},{24,56},{32,0},{40,8},{48,16},{56,24},{1,33}... | collective-permute-start | bytes 196616 | tf_op jit(solution)/shard_map/mass_over_ill/ppermute | solution.py:329
  37.1 4.3 %collective-permute-start.15 = (f32[128,128]{1,0:T(8,128)S(1)}, f32[128,128]{1,0:T(8,128)S(1)}, u32[]{:S(2)}, u32[]{:S(2)}) collective-permute-start(f32[128,128]{1,0:T(8,128)S(1)} %get-tuple-element.29), channel_id=1, source_target_pairs={{0,48},{8,56},{16,0},{24,8},{32,16},{40,24},{48,32},{56,40},{1,49}... | collective-permute-start | bytes 196616 | tf_op jit(solution)/shard_map/mass_over_ill/ppermute | solution.py:329

commit v3 on v2

--- a/solution.py
+++ b/solution.py
@@ -33,7 +33,8 @@
     return [wide[:, i * LANES : (i + 1) * LANES] for i in range(count)]
 
 
-def pack_kernel(v0, v1, v2, v3, out_ref):
+def pack_kernel(v0, v1, v2, v3, hot_ref, out_ref):
+    del hot_ref
     for q, ref in enumerate((v1, v2, v3)):
         for d in range(2):
             out_ref[(q + 1) * HALF_ROWS + d * Z : (q + 1) * HALF_ROWS + (d + 1) * Z, :] = plane_of(ref, 0, d)
@@ -61,9 +62,9 @@
 
 
 def forward_half(
-    a, own, above, drift, me, transition_ref,
+    a, own, above, drift, me, table_ref,
     index_ref, weight_ref, steady_ref, lottery_ref, target_ref, population_ref,
-    mass_scr, row_scr,
+    mass_scr, row_scr, hot_ref=None,
 ):
     values = []
     for d in range(2):
@@ -77,7 +78,7 @@
         rows = slice(d * Z, (d + 1) * Z)
         mass_scr[0, rows, :] = population * share
         mass_scr[1, rows, :] = population * (1.0 - share)
-    scaled = transition_ref[...] * (DISCOUNT * GROSS_RATE)
+    scaled = table_ref[8:, :Z] * (DISCOUNT * GROSS_RATE)
     expected = split_lanes(dot_full(scaled, jnp.concatenate(values, axis=1)), 2)
 
     sub8 = lax.broadcasted_iota(jnp.int32, (8, LANES), 0)
@@ -89,13 +90,16 @@
             row = d * Z + z
             target = target_ref[pl.ds(4 * z + 2 * d + a, 1), :]
             quarter = ((target >> 7) - me) & 3
-            hot = jnp.where(sub128 == (target & 127), 1.0, 0.0).astype(jnp.bfloat16)
+            if hot_ref is None:
+                hot, hot_lanes = jnp.where(sub128 == (target & 127), 1.0, 0.0).astype(jnp.bfloat16), 1
+            else:
+                hot, hot_lanes = hot_ref[row * LANES : (row + 1) * LANES, :], 0
             mass = jnp.where(is_low, mass_scr[0, row : row + 1, :], mass_scr[1, row : row + 1, :])
             mass = jnp.where(quarter == sub_quarter, mass, 0.0)
             first = mass.astype(jnp.bfloat16)
             rest = mass - first.astype(jnp.float32)
             both = jnp.concatenate([mass, rest], axis=0).astype(jnp.bfloat16)
-            out = lax.dot_general(both, hot, (((1,), (1,)), ((), ())), preferred_element_type=jnp.float32)
+            out = lax.dot_general(both, hot, (((1,), (hot_lanes,)), ((), ())), preferred_element_type=jnp.float32)
             row_scr[row * 8 : row * 8 + 8, :] = out[:8] + out[8:]
     lane = lax.broadcasted_iota(jnp.int32, (HALF_ROWS, LANES), 1)
     low = [row_scr[pl.ds(q, HALF_ROWS, stride=8), :] for q in range(4)]
@@ -121,19 +125,28 @@
     return [ref[p * Z : (p + 1) * Z, :] for ref in refs]
 
 
+def hot_kernel(target_ref, out_ref):
+    lanes = lax.broadcasted_iota(jnp.int32, (LANES, LANES), 1)
+    planes = [plane_of(target_ref, 1, d) & 127 for d in range(2)]
+    turned_target = jnp.concatenate(planes + [jnp.zeros((HALF_ROWS, LANES), jnp.int32)], axis=0).T
+    for row in range(HALF_ROWS):
+        hot = jnp.where(lanes == turned_target[:, row : row + 1], 1.0, 0.0)
+        out_ref[row * LANES : (row + 1) * LANES, :] = hot.astype(jnp.bfloat16)
+
+
 def first_half_kernel(
-    small_ref, v0, v1, v2, v3, scaled_ref, transition_ref, index_ref, weight_ref, steady_ref, lottery_ref, target_ref,
+    table_ref, v0, v1, v2, v3, index_ref, weight_ref, steady_ref, lottery_ref, target_ref,
     population_ref, mass_ref, expected_ref, upper_ref, mass_scr, row_scr,
 ):
     values = []
     for p in range(4):
         values += [v0[p * Z : (p + 1) * Z, :]] + [plane_of(ref, p // 2, p % 2) for ref in (v1, v2, v3)]
-    planes = split_lanes(dot_full(scaled_ref[...], jnp.concatenate(values, axis=1)), 16)
+    planes = split_lanes(dot_full(table_ref[8:, :Z] * (table_ref[8:, Z : Z + 1] * (DISCOUNT * GROSS_RATE)), jnp.concatenate(values, axis=1)), 16)
     for i in range(8):
         upper_ref[i * Z : (i + 1) * Z, :] = planes[8 + i]
     expected, by_quarter = forward_half(
-        0, [planes[0:4], planes[4:8]], [planes[8:12], planes[12:16]], small_ref[0:1, :],
-        lax.axis_index("liq"), transition_ref, index_ref, weight_ref, steady_ref, lottery_ref, target_ref,
+        0, [planes[0:4], planes[4:8]], [planes[8:12], planes[12:16]], table_ref[0:1, :],
+        lax.axis_index("liq"), table_ref, index_ref, weight_ref, steady_ref, lottery_ref, target_ref,
         population_ref, mass_scr, row_scr,
     )
     for q in range(4):
@@ -143,16 +156,16 @@
 
 
 def second_half_kernel(
-    small_ref, upper_ref, halo_ref, first_ref, scaled_ref, transition_ref, index_ref, weight_ref, steady_ref,
+    table_ref, upper_ref, halo_ref, first_ref, hot_ref, index_ref, weight_ref, steady_ref,
     lottery_ref, target_ref, population_ref, p0, p1, p2, p3, expected_ref, mass_scr, row_scr,
 ):
     own = [[upper_ref[(4 * d + q) * Z : (4 * d + q + 1) * Z, :] for q in range(4)] for d in range(2)]
     values = [halo_ref[q * HALF_ROWS + d * Z : q * HALF_ROWS + (d + 1) * Z, :] for d in range(2) for q in range(4)]
-    planes = split_lanes(dot_full(scaled_ref[...], jnp.concatenate(values, axis=1)), 8)
+    planes = split_lanes(dot_full(table_ref[8:, :Z] * (table_ref[8:, Z : Z + 1] * (DISCOUNT * GROSS_RATE)), jnp.concatenate(values, axis=1)), 8)
     expected, by_quarter = forward_half(
-        1, own, [planes[0:4], planes[4:8]], small_ref[1:2, :],
-        lax.axis_index("liq"), transition_ref, index_ref, weight_ref, steady_ref, lottery_ref, target_ref,
-        population_ref, mass_scr, row_scr,
+        1, own, [planes[0:4], planes[4:8]], table_ref[1:2, :],
+        lax.axis_index("liq"), table_ref, index_ref, weight_ref, steady_ref, lottery_ref, target_ref,
+        population_ref, mass_scr, row_scr, hot_ref,
     )
     for q, out in enumerate((p0, p1, p2, p3)):
         out[:HALF_ROWS, :] = first_ref[q * HALF_ROWS : (q + 1) * HALF_ROWS, :]
@@ -161,20 +174,20 @@
         expected_ref[d * Z : (d + 1) * Z, :] = expected[d]
 
 
-def consume_kernel(small_ref, e0, e1, e2, e3, index_ref, weight_ref, out_ref):
+def consume_kernel(table_ref, e0, e1, e2, e3, index_ref, weight_ref, out_ref):
     pieces = (e0, e1, e2, e3)
     for a in range(2):
         for d in range(2):
             policy = policy_plane(
-                rows_of(pieces, 2 * a + d), rows_of(pieces, 2 * a + 2 + d), small_ref[a : a + 1, :],
+                rows_of(pieces, 2 * a + d), rows_of(pieces, 2 * a + 2 + d), table_ref[a : a + 1, :],
                 plane_of(index_ref, a, d), plane_of(weight_ref, a, d), lax.axis_index("liq"),
             )
             out_ref[pl.ds(2 * d + a, Z, stride=4), :] = policy
 
 
-def gather_mass_kernel(small_ref, p0, p1, p2, p3, lower_ref, upper_ref, halo_ref, core_out, expected_out):
+def gather_mass_kernel(table_ref, p0, p1, p2, p3, lower_ref, upper_ref, halo_ref, core_out, expected_out):
     core_out[:PLANE_ROWS, :] = (p0[...] + p1[...]) + (p2[...] + p3[...])
-    core_out[PLANE_ROWS:, :] = small_ref[...]
+    core_out[PLANE_ROWS:, :] = table_ref[:8, :]
     for i, ref in enumerate((lower_ref, upper_ref, halo_ref)):
         expected_out[i * HALF_ROWS : (i + 1) * HALF_ROWS, :] = ref[...]
 
@@ -200,12 +213,12 @@
 def settle_kernel(own_ref, core_ref, dur_ref, o0, o1, o2, o3):
     sources = ([], [])
     for ref in (own_ref, core_ref):
-        targets = spread_targets([ref[PLANE_ROWS + 4 + p : PLANE_ROWS + 5 + p, :] for p in range(4)])
+        targets = spread_targets([ref[PLANE_ROWS + row : PLANE_ROWS + row + 1, :] for row in (4, 6, 5, 7)])
         for p in range(4):
             sources[p % 2].append((targets[p * Z : (p + 1) * Z], ref[p * Z : (p + 1) * Z, :]))
     arriving = []
     targets = spread_targets(
-        [dur_ref[PLANE_ROWS + i + p : PLANE_ROWS + i + p + 1, :] for i in (4, 12) for p in (0, 2)]
+        [dur_ref[PLANE_ROWS + row : PLANE_ROWS + row + 1, :] for row in (4, 5, 12, 13)]
     )
     for i in range(4):
         arriving.append((targets[i * Z : (i + 1) * Z], dur_ref[i * Z : (i + 1) * Z, :]))
@@ -226,25 +239,25 @@
             out[(2 * a + 1) * Z : (2 * a + 2) * Z, :] = stay_high * high + gathered(arriving)
 
 
-def population_kernel(transition_ref, s0, s1, s2, s3, out_ref):
+def population_kernel(table_ref, s0, s1, s2, s3, out_ref):
     settled = (s0[...] + s1[...]) + (s2[...] + s3[...])
     wide = jnp.concatenate([settled[p * Z : (p + 1) * Z] for p in range(4)], axis=1)
     moved = lax.dot_general(
-        transition_ref[...], wide, (((0,), (0,)), ((), ())), precision=HIGHEST_PREC, preferred_element_type=jnp.float32
+        table_ref[8:, :Z], wide, (((0,), (0,)), ((), ())), precision=HIGHEST_PREC, preferred_element_type=jnp.float32
     )
     for p, plane in enumerate(split_lanes(moved, 4)):
         a, d = p // 2, p % 2
         out_ref[pl.ds(2 * d + a, Z, stride=4), :] = plane
 
 
-def call(kernel, out_rows, inputs, scratch=(), work=0):
-    shapes = [jax.ShapeDtypeStruct(rows if isinstance(rows, tuple) else (rows, LANES), jnp.float32) for rows in out_rows]
+def call(kernel, out_rows, inputs, scratch=(), work=0, dtype=jnp.float32, spaces=None):
+    shapes = [jax.ShapeDtypeStruct((rows, LANES), dtype) for rows in out_rows]
     specs = [pl.BlockSpec(memory_space=VMEM) for _ in out_rows]
     single = len(out_rows) == 1
     return pl.pallas_call(
         kernel,
         out_shape=shapes[0] if single else shapes,
-        in_specs=[pl.BlockSpec(memory_space=VMEM)] * len(inputs),
+        in_specs=[pl.BlockSpec(memory_space=space) for space in spaces or [VMEM] * len(inputs)],
         out_specs=specs[0] if single else specs,
         scratch_shapes=list(scratch),
         compiler_params=pltpu.CompilerParams(vmem_limit_bytes=KERNEL_VMEM),
@@ -282,21 +295,26 @@
         value = flat(marginal_value)
         pieces = [marginal_value.transpose(2, 1, 0, 3).reshape(PLANE_ROWS, LANES)] + from_other_liq([value] * 4)
     with jax.named_scope("prepare"):
-        scaled = transition * (discount_shock * (DISCOUNT * GROSS_RATE))[:, None]
         is_last = lax.axis_index("ill") == ill_count - 1
         is_lowest = lax.axis_index("dur") == 0
-        row = lax.broadcasted_iota(jnp.int32, (8, LANES), 0)
-        drift = jnp.where(row[:2] == 0, illiquid_drift[:, None], jnp.where(is_last, 1.0, illiquid_drift[:, None]))
-        stay = jnp.where((row[:2] == 0) & is_lowest, 1.0, durable_keep[:, None])
-        target = illiquid_target.transpose(2, 1, 0).reshape(4, Z).astype(jnp.float32)
-        small = jnp.concatenate([drift, stay, jnp.pad(target, ((0, 0), (0, LANES - Z)))], axis=0)
+        row = lax.broadcasted_iota(jnp.int32, (2, LANES), 0)
+        drift = jnp.where((row == 1) & is_last, 1.0, illiquid_drift[:, None])
+        stay = jnp.where((row == 0) & is_lowest, 1.0, durable_keep[:, None])
+        target = illiquid_target.transpose(1, 2, 0).reshape(4, Z).astype(jnp.float32)
+        target = jnp.pad(target, ((0, 0), (0, LANES - Z)))
+        income = jnp.concatenate(
+            [transition, discount_shock[:, None], jnp.zeros((Z, LANES - Z - 1), jnp.float32)], axis=1
+        )
+        table = jnp.concatenate([drift, stay, target, income], axis=0)
+    with jax.named_scope("hot"):
+        hot = call(hot_kernel, [HALF_ROWS * LANES], [flat(liquid_target)], dtype=jnp.bfloat16)
     with jax.named_scope("value_over_ill"):
-        halo = from_above_ill(call(pack_kernel, [4 * HALF_ROWS], pieces))
+        halo = from_above_ill(call(pack_kernel, [4 * HALF_ROWS], [*pieces, hot], spaces=[VMEM] * 4 + [pl.ANY]))
     with jax.named_scope("first_half"):
         mass, lower, upper = call(
             first_half_kernel,
             [4 * HALF_ROWS, HALF_ROWS, 4 * HALF_ROWS],
-            [small, *pieces, scaled, transition, *states],
+            [table, *pieces, *states],
             scratch,
         )
     with jax.named_scope("expected_over_ill"):
@@ -305,7 +323,7 @@
         *sends, higher = call(
             second_half_kernel,
             [PLANE_ROWS] * 4 + [HALF_ROWS],
-            [small, upper, halo, mass, scaled, transition, *states],
+            [table, upper, halo, mass, hot, *states],
             scratch,
             30000000,
         )
@@ -313,7 +331,7 @@
         got = [sends[0]] + from_other_liq(sends)
     with jax.named_scope("gather_mass"):
         to_core, expected = call(
-            gather_mass_kernel, [PLANE_ROWS + 8, 3 * HALF_ROWS], [small, *got, lower, higher, next_halo]
+            gather_mass_kernel, [PLANE_ROWS + 8, 3 * HALF_ROWS], [table, *got, lower, higher, next_halo]
         )
     with jax.named_scope("mass_over_core"):
         from_core = lax.ppermute(to_core, "ill", other_core)
@@ -328,9 +346,9 @@
     with jax.named_scope("mass_over_ill"):
         arrived = [lax.ppermute(parts[k], "ill", turned("ill", 2 * k)) for k in range(1, 4)]
     with jax.named_scope("consume"):
-        consumption = call(consume_kernel, [PLANE_ROWS], [small, *expected_pieces, index, weight])
+        consumption = call(consume_kernel, [PLANE_ROWS], [table, *expected_pieces, index, weight])
     with jax.named_scope("population"):
-        population_next = call(population_kernel, [PLANE_ROWS], [transition, parts[0], *arrived])
+        population_next = call(population_kernel, [PLANE_ROWS], [table, parts[0], *arrived])
     shape = population.shape
     return consumption.reshape(shape), population_next.reshape(shape)
 

time: 42.5 us -> 41.7 us (0.981)
  Pallas kernels: 5.89 us -> 6.83 us
  other arithmetic: 0.82 us -> 0.17 us
  starting transfers between devices: 21.9 us -> 21.3 us
    pallas_call x8 -> x9, Pallas kernels: 5.89 us -> 6.83 us  [call(): pl.pallas_call(kernel, out_shape=shapes[0] if single else shapes, in_spec...]
    mul x2 -> x0, other arithmetic: 0.73 us -> none  [body(): scaled = transition * (discount_shock * (DISCOUNT * GROSS_RATE))[:, None]]
    ppermute x3, starting transfers between devices: 5.53 us -> 5.08 us  [body(): lax.ppermute(parts[k], 'ill', turned('ill', 2 * k))]
    unnamed x20 -> x24, local copies, waits for them, and re-layouts: 1.34 us -> 0.9 us
  transfers between devices with their start and end apart: 16 -> 16, of which waited for: 9 -> 9; matrix products, arithmetic and copies ran while one was open for 4% -> 3% of each run, Pallas kernels for 8% -> 11%
where the time goes in v3:
time: 41.7 us; the launch traced here: 41.5 us
  starting transfers between devices  21.3 us (51%)
  waiting for transfers between devices  10.5 us (25%)
  Pallas kernels  6.83 us (16%)
  local copies, waits for them, and re-layouts  1.86 us (4%)
  between operations  0.82 us (2%)
    ppermute x9, starting transfers between devices, from_other_liq(): lax.ppermute(pieces[k], 'liq', turned('liq', k))  10.8 us
    pallas_call x9, Pallas kernels, call(): pl.pallas_call(kernel, out_shape=shapes[0] if single else shapes, in_spec...  6.83 us
    ppermute x3, starting transfers between devices, body(): lax.ppermute(parts[k], 'ill', turned('ill', 2 * k))  5.08 us
    ppermute x2, starting transfers between devices, from_above_ill(): return lax.ppermute(x, 'ill', turned('ill', -1))  3.28 us
    ppermute x9, waiting for transfers between devices, from_other_liq(): lax.ppermute(pieces[k], 'liq', turned('liq', k))  2.99 us
    ppermute x1, waiting for transfers between devices, body(): from_dur = lax.ppermute(to_dur, 'dur', below_dur)  2.89 us
    ppermute x1, starting transfers between devices, body(): from_dur = lax.ppermute(to_dur, 'dur', below_dur)  2.02 us
    ppermute x2, waiting for transfers between devices, from_above_ill(): return lax.ppermute(x, 'ill', turned('ill', -1))  1.9 us
  transfers between devices with their start and end apart: 16, of which 9 were waited for; matrix products, arithmetic and copies ran while one was open for 3% of the time, Pallas kernels for 11%

profile of v3, /device:TPU:96, one launch (start us, length us, event | category | flops | bytes accessed | tf_op | source)
XLA Modules:
  0.0 41.5 jit_solution(14152436292931294344)
XLA Ops:
  0.6 2.8 %collective-permute-start = (f32[128,128]{1,0:T(8,128)}, f32[128,128]{1,0:T(8,128)S(1)}, u32[]{:S(2)}, u32[]{:S(2)}) collective-permute-start(f32[128,128]{1,0:T(8,128)} %bitcast.33), channel_id=1, source_target_pairs={{0,192},{64,0},{128,64},{192,128},{1,193},{65,1},{129,65},{193,129... | collective-permute-start | bytes 196616 | tf_op jit(solution)/shard_map/value_over_liq/ppermute | solution.py:274
  3.5 0.8 %collective-permute-start.1 = (f32[128,128]{1,0:T(8,128)}, f32[128,128]{1,0:T(8,128)S(1)}, u32[]{:S(2)}, u32[]{:S(2)}) collective-permute-start(f32[128,128]{1,0:T(8,128)} %bitcast.34), channel_id=1, source_target_pairs={{0,128},{64,192},{128,0},{192,64},{1,129},{65,193},{129,1},{193,65... | collective-permute-start | bytes 196616 | tf_op jit(solution)/shard_map/value_over_liq/ppermute | solution.py:274
  4.3 0.9 %collective-permute-start.2 = (f32[128,128]{1,0:T(8,128)}, f32[128,128]{1,0:T(8,128)S(1)}, u32[]{:S(2)}, u32[]{:S(2)}) collective-permute-start(f32[128,128]{1,0:T(8,128)} %bitcast.35), channel_id=1, source_target_pairs={{0,64},{64,128},{128,192},{192,0},{1,65},{65,129},{129,193},{193,1... | collective-permute-start | bytes 196616 | tf_op jit(solution)/shard_map/value_over_liq/ppermute | solution.py:274
  5.2 0.9 %copy.15 = f32[2,2,32,128]{3,2,1,0:T(8,128)S(1)} copy(f32[2,2,32,128]{3,0,1,2:T(2,128)} %bitcast.36) | data formatting | bytes 131072 | tf_op jit(solution)/shard_map/value_over_liq/transpose | solution.py:296
  6.0 0.0 copy-start
  6.0 0.8 %copy-done = s32[32,2,2,128]{3,2,1,0:T(2,128)S(1)} copy-done((s32[32,2,2,128]{3,2,1,0:T(2,128)S(1)}, s32[32,2,2,128]{3,2,1,0:T(2,128)}, u32[]{:S(2)}) %copy-start) | copy-done | bytes 65560
  6.9 0.0 copy-start.10
  6.9 0.0 copy-start.11
  6.9 0.0 copy-start.7
  6.9 0.0 copy-start.1
  6.9 0.0 copy-start.2
  6.9 0.0 copy-start.3
  6.9 0.0 copy-start.4
  6.9 0.0 copy-start.5
  7.0 0.0 copy-start.6
  7.0 1.4 %hot.1.hot_ref = bf16[8192,128]{1,0:T(8,128)(2,1)S(1)} custom-call(s32[128,128]{1,0:T(8,128)S(1)} %bitcast.15), custom_call_target="tpu_custom_call" | custom-call | tf_op jit(solution)/shard_map/hot/pallas_call | solution.py:257
  8.3 0.0 collective-permute-done.v1
  8.4 1.1 %collective-permute-done.1.v2 = f32[128,128]{1,0:T(8,128)S(1)} collective-permute-done((f32[128,128]{1,0:T(8,128)}, f32[128,128]{1,0:T(8,128)S(1)}, u32[]{:S(2)}, u32[]{:S(2)}) %collective-permute-start.1) | collective-permute-done | bytes 65568 | tf_op jit(solution)/shard_map/value_over_liq/ppermute | solution.py:274
  9.5 0.7 %collective-permute-done.2.v3 = f32[128,128]{1,0:T(8,128)S(1)} collective-permute-done((f32[128,128]{1,0:T(8,128)}, f32[128,128]{1,0:T(8,128)S(1)}, u32[]{:S(2)}, u32[]{:S(2)}) %collective-permute-start.2) | collective-permute-done | bytes 65568 | tf_op jit(solution)/shard_map/value_over_liq/ppermute | solution.py:274
  10.2 1.0 %collective-permute-start.3 = (f32[256,128]{1,0:T(8,128)S(1)}, f32[256,128]{1,0:T(8,128)S(1)}, u32[]{:S(2)}, u32[]{:S(2)}) collective-permute-start(f32[256,128]{1,0:T(8,128)S(1)} %value_over_ill.1), channel_id=1, source_target_pairs={{0,56},{8,0},{16,8},{24,16},{32,24},{40,32},{48,40},{56,48},{1,57}... | collective-permute-start | bytes 393224 | tf_op jit(solution)/shard_map/value_over_ill/ppermute | solution.py:279
  11.2 0.0 copy-done.10
  11.2 0.0 copy-done.11
  11.2 0.1 broadcast_select_fusion
  11.3 0.0 copy-done.9
  11.3 0.1 copy.14
  11.4 0.0 copy-done.8
  11.4 0.0 copy-done.7
  11.4 0.1 fusion.table_ref
  11.5 0.0 copy-done.1
  11.5 0.0 copy-done.2
  11.5 0.0 copy-done.3
  11.5 0.0 copy-done.4
  11.5 0.0 copy-done.5
  11.5 0.0 copy-done.6
  11.5 1.9 %first_half.1 = (f32[256,128]{1,0:T(8,128)S(1)}, f32[64,128]{1,0:T(8,128)S(1)}, f32[256,128]{1,0:T(8,128)S(1)}) custom-call(f32[40,128]{1,0:T(8,128)S(1)} %fusion.table_ref, f32[128,128]{1,0:T(8,128)S(1)} %bitcast.25, f32[128,128]{1,0:T(8,128)S(1)} %collective-permute-done.v1, f32[128,128]{1,0:T(8,128)S(1)} %collective-permute-done.1.v2, ...), custom_call_target="tpu_custom_call" | custom-call | tf_op jit(solution)/shard_map/first_half/pallas_call | solution.py:257
  13.4 0.3 collective-permute-done.3.halo_ref
  13.7 1.3 %second_half.1 = (f32[128,128]{1,0:T(8,128)S(1)}, f32[128,128]{1,0:T(8,128)S(1)}, f32[128,128]{1,0:T(8,128)S(1)}, f32[128,128]{1,0:T(8,128)S(1)}, f32[64,128]{1,0:T(8,128)S(1)}) custom-call(f32[40,128]{1,0:T(8,128)S(1)} %fusion.table_ref, f32[256,128]{1,0:T(8,128)S(1)} %get-tuple-element.16.upper_ref, f32[256,128]{1,0:T(8,128)S(1)} %collective-permute-done.3.halo_ref, ...), custom_call_target="tpu_custom_call" | custom-call | bytes 30000000 | tf_op jit(solution)/shard_map/second_half/pallas_call | solution.py:257
  15.0 1.2 %collective-permute-start.4 = (f32[128,128]{1,0:T(8,128)S(1)}, f32[128,128]{1,0:T(8,128)S(1)}, u32[]{:S(2)}, u32[]{:S(2)}) collective-permute-start(f32[128,128]{1,0:T(8,128)S(1)} %get-tuple-element.19), channel_id=1, source_target_pairs={{0,192},{64,0},{128,64},{192,128},{1,193},{65,1},{129,65},{193,129... | collective-permute-start | bytes 196616 | tf_op jit(solution)/shard_map/mass_over_liq/ppermute | solution.py:274
  16.2 1.5 %collective-permute-start.5 = (f32[128,128]{1,0:T(8,128)S(1)}, f32[128,128]{1,0:T(8,128)S(1)}, u32[]{:S(2)}, u32[]{:S(2)}) collective-permute-start(f32[128,128]{1,0:T(8,128)S(1)} %get-tuple-element.20), channel_id=1, source_target_pairs={{0,128},{64,192},{128,0},{192,64},{1,129},{65,193},{129,1},{193,65... | collective-permute-start | bytes 196616 | tf_op jit(solution)/shard_map/mass_over_liq/ppermute | solution.py:274
  17.7 0.5 %collective-permute-start.6 = (f32[128,128]{1,0:T(8,128)S(1)}, f32[128,128]{1,0:T(8,128)S(1)}, u32[]{:S(2)}, u32[]{:S(2)}) collective-permute-start(f32[128,128]{1,0:T(8,128)S(1)} %get-tuple-element.21), channel_id=1, source_target_pairs={{0,64},{64,128},{128,192},{192,0},{1,65},{65,129},{129,193},{193,1... | collective-permute-start | bytes 196616 | tf_op jit(solution)/shard_map/mass_over_liq/ppermute | solution.py:274
  18.3 2.2 %collective-permute-start.7 = (f32[64,128]{1,0:T(8,128)S(1)}, f32[64,128]{1,0:T(8,128)S(1)}, u32[]{:S(2)}, u32[]{:S(2)}) collective-permute-start(f32[64,128]{1,0:T(8,128)S(1)} %get-tuple-element.22.lower_ref), channel_id=1, source_target_pairs={{0,56},{8,0},{16,8},{24,16},{32,24},{40,32},{48,40},{56,48},{1,57}... | collective-permute-start | bytes 98312 | tf_op jit(solution)/shard_map/expected_over_ill/ppermute | solution.py:279
  20.5 1.6 %collective-permute-done.7.halo_ref = f32[64,128]{1,0:T(8,128)S(1)} collective-permute-done((f32[64,128]{1,0:T(8,128)S(1)}, f32[64,128]{1,0:T(8,128)S(1)}, u32[]{:S(2)}, u32[]{:S(2)}) %collective-permute-start.7) | collective-permute-done | bytes 32800 | tf_op jit(solution)/shard_map/expected_over_ill/ppermute | solution.py:279
  22.1 0.0 collective-permute-done.4.p1
  22.1 0.0 collective-permute-done.5.p2
  22.1 1.2 %collective-permute-done.6.p3 = f32[128,128]{1,0:T(8,128)S(1)} collective-permute-done((f32[128,128]{1,0:T(8,128)S(1)}, f32[128,128]{1,0:T(8,128)S(1)}, u32[]{:S(2)}, u32[]{:S(2)}) %collective-permute-start.6) | collective-permute-done | bytes 65568 | tf_op jit(solution)/shard_map/mass_over_liq/ppermute | solution.py:274
  23.3 0.1 collective-permute-start.11
  23.4 0.3 collective-permute-start.10
  23.8 0.9 %collective-permute-done.11.core_ref = f32[136,128]{1,0:T(8,128)S(1)} collective-permute-done((f32[136,128]{1,0:T(8,128)S(1)}, f32[136,128]{1,0:T(8,128)S(1)}, u32[]{:S(2)}, u32[]{:S(2)}) %collective-permute-start.11) | collective-permute-done | bytes 69664 | tf_op jit(solution)/shard_map/mass_over_core/ppermute | solution.py:337
  24.7 2.0 %collective-permute-start.12 = (f32[144,128]{1,0:T(8,128)S(1)}, f32[144,128]{1,0:T(8,128)S(1)}, u32[]{:S(2)}, u32[]{:S(2)}) collective-permute-start(f32[144,128]{1,0:T(8,128)S(1)} %leave.1), channel_id=1, source_target_pairs={{1,0},{2,1},{3,2},{4,3},{5,4},{6,5},{7,6},{9,8},{10,9},{11,10},{12... | collective-permute-start | bytes 221192 | tf_op jit(solution)/shard_map/mass_over_dur/ppermute | solution.py:341
  26.7 2.1 %collective-permute-start.8 = (f32[192,128]{1,0:T(8,128)S(1)}, f32[192,128]{1,0:T(8,128)S(1)}, u32[]{:S(2)}, u32[]{:S(2)}) collective-permute-start(f32[192,128]{1,0:T(8,128)S(1)} %get-tuple-element.24.e0), channel_id=1, source_target_pairs={{0,192},{64,0},{128,64},{192,128},{1,193},{65,1},{129,65},{193,129... | collective-permute-start | bytes 294920 | tf_op jit(solution)/shard_map/expected_over_liq/ppermute | solution.py:274
  28.8 0.6 %collective-permute-start.9 = (f32[192,128]{1,0:T(8,128)S(1)}, f32[192,128]{1,0:T(8,128)S(1)}, u32[]{:S(2)}, u32[]{:S(2)}) collective-permute-start(f32[192,128]{1,0:T(8,128)S(1)} %get-tuple-element.24.e0), channel_id=1, source_target_pairs={{0,128},{64,192},{128,0},{192,64},{1,129},{65,193},{129,1},{193,65... | collective-permute-start | bytes 294920 | tf_op jit(solution)/shard_map/expected_over_liq/ppermute | solution.py:274
  29.4 2.9 %collective-permute-done.12.dur_ref = f32[144,128]{1,0:T(8,128)S(1)} collective-permute-done((f32[144,128]{1,0:T(8,128)S(1)}, f32[144,128]{1,0:T(8,128)S(1)}, u32[]{:S(2)}, u32[]{:S(2)}) %collective-permute-start.12) | collective-permute-done | bytes 73760 | tf_op jit(solution)/shard_map/mass_over_dur/ppermute | solution.py:341
  32.3 0.3 settle.1
  32.6 0.7 %collective-permute-start.13 = (f32[128,128]{1,0:T(8,128)S(1)}, f32[128,128]{1,0:T(8,128)S(1)}, u32[]{:S(2)}, u32[]{:S(2)}) collective-permute-start(f32[128,128]{1,0:T(8,128)S(1)} %get-tuple-element.27), channel_id=1, source_target_pairs={{0,16},{8,24},{16,32},{24,40},{32,48},{40,56},{48,0},{56,8},{1,17}... | collective-permute-start | bytes 196616 | tf_op jit(solution)/shard_map/mass_over_ill/ppermute | solution.py:347
  33.3 3.0 %collective-permute-start.14 = (f32[128,128]{1,0:T(8,128)S(1)}, f32[128,128]{1,0:T(8,128)S(1)}, u32[]{:S(2)}, u32[]{:S(2)}) collective-permute-start(f32[128,128]{1,0:T(8,128)S(1)} %get-tuple-element.28), channel_id=1, source_target_pairs={{0,32},{8,40},{16,48},{24,56},{32,0},{40,8},{48,16},{56,24},{1,33}... | collective-permute-start | bytes 196616 | tf_op jit(solution)/shard_map/mass_over_ill/ppermute | solution.py:347
  36.3 0.0 collective-permute-done.10.e3
  36.3 1.4 %collective-permute-start.15 = (f32[128,128]{1,0:T(8,128)S(1)}, f32[128,128]{1,0:T(8,128)S(1)}, u32[]{:S(2)}, u32[]{:S(2)}) collective-permute-start(f32[128,128]{1,0:T(8,128)S(1)} %get-tuple-element.29), channel_id=1, source_target_pairs={{0,48},{8,56},{16,0},{24,8},{32,16},{40,24},{48,32},{56,40},{1,49}... | collective-permute-start | bytes 196616 | tf_op jit(solution)/shard_map/mass_over_ill/ppermute | solution.py:347
  37.7 0.0 collective-permute-done.8.e1
  37.7 0.0 collective-permute-done.9.e2
  37.7 1.1 %consume.1 = f32[128,128]{1,0:T(8,128)} custom-call(f32[40,128]{1,0:T(8,128)S(1)} %fusion.table_ref, f32[192,128]{1,0:T(8,128)S(1)} %get-tuple-element.24.e0, f32[192,128]{1,0:T(8,128)S(1)} %collective-permute-done.8.e1, f32[192,128]{1,0:T(8,128)S(1)} %collective-permute-done.9.e2, f32[192,128]{1,0:T(8,128)S(1)} %collective-permute-done.10.e3, ...), custom_call_target="tpu_custom_call" | custom-call | tf_op jit(solution)/shard_map/consume/pallas_call | solution.py:257
  38.8 0.0 collective-permute-done.13.s1
  38.8 0.5 %collective-permute-done.14.s2 = f32[128,128]{1,0:T(8,128)S(1)} collective-permute-done((f32[128,128]{1,0:T(8,128)S(1)}, f32[128,128]{1,0:T(8,128)S(1)}, u32[]{:S(2)}, u32[]{:S(2)}) %collective-permute-start.14) | collective-permute-done | bytes 65568 | tf_op jit(solution)/shard_map/mass_over_ill/ppermute | solution.py:347
  39.3 1.3 %collective-permute-done.15.s3 = f32[128,128]{1,0:T(8,128)S(1)} collective-permute-done((f32[128,128]{1,0:T(8,128)S(1)}, f32[128,128]{1,0:T(8,128)S(1)}, u32[]{:S(2)}, u32[]{:S(2)}) %collective-permute-start.15) | collective-permute-done | bytes 65568 | tf_op jit(solution)/shard_map/mass_over_ill/ppermute | solution.py:347
  40.6 0.9 %population.1 = f32[128,128]{1,0:T(8,128)} custom-call(f32[40,128]{1,0:T(8,128)S(1)} %fusion.table_ref, f32[128,128]{1,0:T(8,128)S(1)} %get-tuple-element.26.s0, f32[128,128]{1,0:T(8,128)S(1)} %collective-permute-done.13.s1, f32[128,128]{1,0:T(8,128)S(1)} %collective-permute-done.14.s2, f32[128,128]{1,0:T(8,128)S(1)} %collective-permute-done.15.s3), custom_call_target="tpu_custom_call" | custom-call | tf_op jit(solution)/shard_map/population/pallas_call | solution.py:257
  (9 shorter events, 0.1 us)
Async XLA Ops:
  0.6 7.7 %collective-permute-start = (f32[128,128]{1,0:T(8,128)}, f32[128,128]{1,0:T(8,128)S(1)}, u32[]{:S(2)}, u32[]{:S(2)}) collective-permute-start(f32[128,128]{1,0:T(8,128)} %bitcast.33), channel_id=1, source_target_pairs={{0,192},{64,0},{128,64},{192,128},{1,193},{65,1},{129,65},{193,129... | collective-permute-start | bytes 196616 | tf_op jit(solution)/shard_map/value_over_liq/ppermute | solution.py:274
  3.5 6.0 %collective-permute-start.1 = (f32[128,128]{1,0:T(8,128)}, f32[128,128]{1,0:T(8,128)S(1)}, u32[]{:S(2)}, u32[]{:S(2)}) collective-permute-start(f32[128,128]{1,0:T(8,128)} %bitcast.34), channel_id=1, source_target_pairs={{0,128},{64,192},{128,0},{192,64},{1,129},{65,193},{129,1},{193,65... | collective-permute-start | bytes 196616 | tf_op jit(solution)/shard_map/value_over_liq/ppermute | solution.py:274
  4.3 5.9 %collective-permute-start.2 = (f32[128,128]{1,0:T(8,128)}, f32[128,128]{1,0:T(8,128)S(1)}, u32[]{:S(2)}, u32[]{:S(2)}) collective-permute-start(f32[128,128]{1,0:T(8,128)} %bitcast.35), channel_id=1, source_target_pairs={{0,64},{64,128},{128,192},{192,0},{1,65},{65,129},{129,193},{193,1... | collective-permute-start | bytes 196616 | tf_op jit(solution)/shard_map/value_over_liq/ppermute | solution.py:274
  6.0 0.8 %copy-start = (s32[32,2,2,128]{3,2,1,0:T(2,128)S(1)}, s32[32,2,2,128]{3,2,1,0:T(2,128)}, u32[]{:S(2)}) copy-start(s32[32,2,2,128]{3,2,1,0:T(2,128)} %param.21) | copy-start | bytes 196612
  6.9 4.3 %copy-start.10 = (f32[2]{0:T(128)S(1)}, f32[2]{0:T(128)}, u32[]{:S(2)}) copy-start(f32[2]{0:T(128)} %param.16) | copy-start | bytes 28
  6.9 4.3 %copy-start.11 = (f32[2]{0:T(128)S(1)}, f32[2]{0:T(128)}, u32[]{:S(2)}) copy-start(f32[2]{0:T(128)} %param.15) | copy-start | bytes 28
  6.9 4.4 %copy-start.9 = (f32[32]{0:T(128)S(1)}, f32[32]{0:T(128)}, u32[]{:S(2)}) copy-start(f32[32]{0:T(128)} %param.14) | copy-start | bytes 388
  6.9 4.5 %copy-start.8 = (s32[32,2,2]{0,2,1:T(2,128)S(1)}, s32[32,2,2]{0,2,1:T(2,128)}, u32[]{:S(2)}) copy-start(s32[32,2,2]{0,2,1:T(2,128)} %param.22) | copy-start | bytes 1540
  6.9 4.5 %copy-start.7 = (f32[32,32]{1,0:T(8,128)S(1)}, f32[32,32]{1,0:T(8,128)}, u32[]{:S(2)}) copy-start(f32[32,32]{1,0:T(8,128)} %param.13) | copy-start | bytes 12292
  6.9 4.6 %copy-start.1 = (s32[32,2,2,128]{3,2,1,0:T(2,128)S(1)}, s32[32,2,2,128]{3,2,1,0:T(2,128)}, u32[]{:S(2)}) copy-start(s32[32,2,2,128]{3,2,1,0:T(2,128)} %param.21) | copy-start | bytes 196612
  6.9 4.6 %copy-start.2 = (s32[32,2,2,128]{3,2,1,0:T(2,128)S(1)}, s32[32,2,2,128]{3,2,1,0:T(2,128)}, u32[]{:S(2)}) copy-start(s32[32,2,2,128]{3,2,1,0:T(2,128)} %param.17) | copy-start | bytes 196612
  6.9 4.6 %copy-start.3 = (f32[32,2,2,128]{3,2,1,0:T(2,128)S(1)}, f32[32,2,2,128]{3,2,1,0:T(2,128)}, u32[]{:S(2)}) copy-start(f32[32,2,2,128]{3,2,1,0:T(2,128)} %param.18) | copy-start | bytes 196612
  6.9 4.6 %copy-start.4 = (f32[32,2,2,128]{3,2,1,0:T(2,128)S(1)}, f32[32,2,2,128]{3,2,1,0:T(2,128)}, u32[]{:S(2)}) copy-start(f32[32,2,2,128]{3,2,1,0:T(2,128)} %param.19) | copy-start | bytes 196612
  6.9 4.6 %copy-start.5 = (f32[32,2,2,128]{3,2,1,0:T(2,128)S(1)}, f32[32,2,2,128]{3,2,1,0:T(2,128)}, u32[]{:S(2)}) copy-start(f32[32,2,2,128]{3,2,1,0:T(2,128)} %param.20) | copy-start | bytes 196612
  7.0 4.6 %copy-start.6 = (f32[32,2,2,128]{3,2,1,0:T(2,128)S(1)}, f32[32,2,2,128]{3,2,1,0:T(2,128)}, u32[]{:S(2)}) copy-start(f32[32,2,2,128]{3,2,1,0:T(2,128)} %param.23) | copy-start | bytes 196612
  10.2 3.6 %collective-permute-start.3 = (f32[256,128]{1,0:T(8,128)S(1)}, f32[256,128]{1,0:T(8,128)S(1)}, u32[]{:S(2)}, u32[]{:S(2)}) collective-permute-start(f32[256,128]{1,0:T(8,128)S(1)} %value_over_ill.1), channel_id=1, source_target_pairs={{0,56},{8,0},{16,8},{24,16},{32,24},{40,32},{48,40},{56,48},{1,57}... | collective-permute-start | bytes 393224 | tf_op jit(solution)/shard_map/value_over_ill/ppermute | solution.py:279
  15.0 7.1 %collective-permute-start.4 = (f32[128,128]{1,0:T(8,128)S(1)}, f32[128,128]{1,0:T(8,128)S(1)}, u32[]{:S(2)}, u32[]{:S(2)}) collective-permute-start(f32[128,128]{1,0:T(8,128)S(1)} %get-tuple-element.19), channel_id=1, source_target_pairs={{0,192},{64,0},{128,64},{192,128},{1,193},{65,1},{129,65},{193,129... | collective-permute-start | bytes 196616 | tf_op jit(solution)/shard_map/mass_over_liq/ppermute | solution.py:274
  16.2 5.9 %collective-permute-start.5 = (f32[128,128]{1,0:T(8,128)S(1)}, f32[128,128]{1,0:T(8,128)S(1)}, u32[]{:S(2)}, u32[]{:S(2)}) collective-permute-start(f32[128,128]{1,0:T(8,128)S(1)} %get-tuple-element.20), channel_id=1, source_target_pairs={{0,128},{64,192},{128,0},{192,64},{1,129},{65,193},{129,1},{193,65... | collective-permute-start | bytes 196616 | tf_op jit(solution)/shard_map/mass_over_liq/ppermute | solution.py:274
  17.7 5.6 %collective-permute-start.6 = (f32[128,128]{1,0:T(8,128)S(1)}, f32[128,128]{1,0:T(8,128)S(1)}, u32[]{:S(2)}, u32[]{:S(2)}) collective-permute-start(f32[128,128]{1,0:T(8,128)S(1)} %get-tuple-element.21), channel_id=1, source_target_pairs={{0,64},{64,128},{128,192},{192,0},{1,65},{65,129},{129,193},{193,1... | collective-permute-start | bytes 196616 | tf_op jit(solution)/shard_map/mass_over_liq/ppermute | solution.py:274
  18.3 3.8 %collective-permute-start.7 = (f32[64,128]{1,0:T(8,128)S(1)}, f32[64,128]{1,0:T(8,128)S(1)}, u32[]{:S(2)}, u32[]{:S(2)}) collective-permute-start(f32[64,128]{1,0:T(8,128)S(1)} %get-tuple-element.22.lower_ref), channel_id=1, source_target_pairs={{0,56},{8,0},{16,8},{24,16},{32,24},{40,32},{48,40},{56,48},{1,57}... | collective-permute-start | bytes 98312 | tf_op jit(solution)/shard_map/expected_over_ill/ppermute | solution.py:279
  23.3 1.3 %collective-permute-start.11 = (f32[136,128]{1,0:T(8,128)S(1)}, f32[136,128]{1,0:T(8,128)S(1)}, u32[]{:S(2)}, u32[]{:S(2)}) collective-permute-start(f32[136,128]{1,0:T(8,128)S(1)} %get-tuple-element.25.own_ref), channel_id=1, source_target_pairs={{0,8},{8,0},{16,24},{24,16},{32,40},{40,32},{48,56},{56,48},{1,9},... | collective-permute-start | bytes 208904 | tf_op jit(solution)/shard_map/mass_over_core/ppermute | solution.py:337
  23.4 12.9 %collective-permute-start.10 = (f32[192,128]{1,0:T(8,128)S(1)}, f32[192,128]{1,0:T(8,128)S(1)}, u32[]{:S(2)}, u32[]{:S(2)}) collective-permute-start(f32[192,128]{1,0:T(8,128)S(1)} %get-tuple-element.24.e0), channel_id=1, source_target_pairs={{0,64},{64,128},{128,192},{192,0},{1,65},{65,129},{129,193},{193,1... | collective-permute-start | bytes 294920 | tf_op jit(solution)/shard_map/expected_over_liq/ppermute | solution.py:274
  24.7 7.6 %collective-permute-start.12 = (f32[144,128]{1,0:T(8,128)S(1)}, f32[144,128]{1,0:T(8,128)S(1)}, u32[]{:S(2)}, u32[]{:S(2)}) collective-permute-start(f32[144,128]{1,0:T(8,128)S(1)} %leave.1), channel_id=1, source_target_pairs={{1,0},{2,1},{3,2},{4,3},{5,4},{6,5},{7,6},{9,8},{10,9},{11,10},{12... | collective-permute-start | bytes 221192 | tf_op jit(solution)/shard_map/mass_over_dur/ppermute | solution.py:341
  26.7 11.0 %collective-permute-start.8 = (f32[192,128]{1,0:T(8,128)S(1)}, f32[192,128]{1,0:T(8,128)S(1)}, u32[]{:S(2)}, u32[]{:S(2)}) collective-permute-start(f32[192,128]{1,0:T(8,128)S(1)} %get-tuple-element.24.e0), channel_id=1, source_target_pairs={{0,192},{64,0},{128,64},{192,128},{1,193},{65,1},{129,65},{193,129... | collective-permute-start | bytes 294920 | tf_op jit(solution)/shard_map/expected_over_liq/ppermute | solution.py:274
  28.8 8.9 %collective-permute-start.9 = (f32[192,128]{1,0:T(8,128)S(1)}, f32[192,128]{1,0:T(8,128)S(1)}, u32[]{:S(2)}, u32[]{:S(2)}) collective-permute-start(f32[192,128]{1,0:T(8,128)S(1)} %get-tuple-element.24.e0), channel_id=1, source_target_pairs={{0,128},{64,192},{128,0},{192,64},{1,129},{65,193},{129,1},{193,65... | collective-permute-start | bytes 294920 | tf_op jit(solution)/shard_map/expected_over_liq/ppermute | solution.py:274
  32.6 6.2 %collective-permute-start.13 = (f32[128,128]{1,0:T(8,128)S(1)}, f32[128,128]{1,0:T(8,128)S(1)}, u32[]{:S(2)}, u32[]{:S(2)}) collective-permute-start(f32[128,128]{1,0:T(8,128)S(1)} %get-tuple-element.27), channel_id=1, source_target_pairs={{0,16},{8,24},{16,32},{24,40},{32,48},{40,56},{48,0},{56,8},{1,17}... | collective-permute-start | bytes 196616 | tf_op jit(solution)/shard_map/mass_over_ill/ppermute | solution.py:347
  33.3 5.9 %collective-permute-start.14 = (f32[128,128]{1,0:T(8,128)S(1)}, f32[128,128]{1,0:T(8,128)S(1)}, u32[]{:S(2)}, u32[]{:S(2)}) collective-permute-start(f32[128,128]{1,0:T(8,128)S(1)} %get-tuple-element.28), channel_id=1, source_target_pairs={{0,32},{8,40},{16,48},{24,56},{32,0},{40,8},{48,16},{56,24},{1,33}... | collective-permute-start | bytes 196616 | tf_op jit(solution)/shard_map/mass_over_ill/ppermute | solution.py:347
  36.3 4.3 %collective-permute-start.15 = (f32[128,128]{1,0:T(8,128)S(1)}, f32[128,128]{1,0:T(8,128)S(1)}, u32[]{:S(2)}, u32[]{:S(2)}) collective-permute-start(f32[128,128]{1,0:T(8,128)S(1)} %get-tuple-element.29), channel_id=1, source_target_pairs={{0,48},{8,56},{16,0},{24,8},{32,16},{40,24},{48,32},{56,40},{1,49}... | collective-permute-start | bytes 196616 | tf_op jit(solution)/shard_map/mass_over_ill/ppermute | solution.py:347

commit v4 on v3

--- a/solution.py
+++ b/solution.py
@@ -78,8 +78,6 @@
         rows = slice(d * Z, (d + 1) * Z)
         mass_scr[0, rows, :] = population * share
         mass_scr[1, rows, :] = population * (1.0 - share)
-    scaled = table_ref[8:, :Z] * (DISCOUNT * GROSS_RATE)
-    expected = split_lanes(dot_full(scaled, jnp.concatenate(values, axis=1)), 2)
 
     sub8 = lax.broadcasted_iota(jnp.int32, (8, LANES), 0)
     is_low = sub8 < 4
@@ -101,6 +99,8 @@
             both = jnp.concatenate([mass, rest], axis=0).astype(jnp.bfloat16)
             out = lax.dot_general(both, hot, (((1,), (hot_lanes,)), ((), ())), preferred_element_type=jnp.float32)
             row_scr[row * 8 : row * 8 + 8, :] = out[:8] + out[8:]
+    scaled = table_ref[8:, :Z] * (DISCOUNT * GROSS_RATE)
+    expected = split_lanes(dot_full(scaled, jnp.concatenate(values, axis=1)), 2)
     lane = lax.broadcasted_iota(jnp.int32, (HALF_ROWS, LANES), 1)
     low = [row_scr[pl.ds(q, HALF_ROWS, stride=8), :] for q in range(4)]
     high = [pltpu.roll(row_scr[pl.ds(4 + q, HALF_ROWS, stride=8), :], 1, 1) for q in range(4)]

time: 41.7 us -> 41.5 us (level)
  no operation moved by 1% of the time
where the time goes in v4:
time: 41.5 us; the launch traced here: 41.3 us
  starting transfers between devices  21.3 us (51%)
  waiting for transfers between devices  10.7 us (26%)
  Pallas kernels  6.54 us (16%)
  local copies, waits for them, and re-layouts  1.86 us (4%)
  between operations  0.82 us (2%)
    ppermute x9, starting transfers between devices, from_other_liq(): lax.ppermute(pieces[k], 'liq', turned('liq', k))  10.8 us
    pallas_call x9, Pallas kernels, call(): pl.pallas_call(kernel, out_shape=shapes[0] if single else shapes, in_spec...  6.54 us
    ppermute x3, starting transfers between devices, body(): lax.ppermute(parts[k], 'ill', turned('ill', 2 * k))  5.08 us
    ppermute x2, starting transfers between devices, from_above_ill(): return lax.ppermute(x, 'ill', turned('ill', -1))  3.28 us
    ppermute x9, waiting for transfers between devices, from_other_liq(): lax.ppermute(pieces[k], 'liq', turned('liq', k))  2.99 us
    ppermute x1, waiting for transfers between devices, body(): from_dur = lax.ppermute(to_dur, 'dur', below_dur)  2.89 us
    ppermute x2, waiting for transfers between devices, from_above_ill(): return lax.ppermute(x, 'ill', turned('ill', -1))  2.04 us
    ppermute x1, starting transfers between devices, body(): from_dur = lax.ppermute(to_dur, 'dur', below_dur)  2.02 us
  transfers between devices with their start and end apart: 16, of which 9 were waited for; matrix products, arithmetic and copies ran while one was open for 3% of the time, Pallas kernels for 11%

profile of v4, /device:TPU:96, one launch (start us, length us, event | category | flops | bytes accessed | tf_op | source)
XLA Modules:
  0.0 41.3 jit_solution(16061276916112990511)
XLA Ops:
  0.6 2.8 %collective-permute-start = (f32[128,128]{1,0:T(8,128)}, f32[128,128]{1,0:T(8,128)S(1)}, u32[]{:S(2)}, u32[]{:S(2)}) collective-permute-start(f32[128,128]{1,0:T(8,128)} %bitcast.33), channel_id=1, source_target_pairs={{0,192},{64,0},{128,64},{192,128},{1,193},{65,1},{129,65},{193,129... | collective-permute-start | bytes 196616 | tf_op jit(solution)/shard_map/value_over_liq/ppermute | solution.py:274
  3.5 0.8 %collective-permute-start.1 = (f32[128,128]{1,0:T(8,128)}, f32[128,128]{1,0:T(8,128)S(1)}, u32[]{:S(2)}, u32[]{:S(2)}) collective-permute-start(f32[128,128]{1,0:T(8,128)} %bitcast.34), channel_id=1, source_target_pairs={{0,128},{64,192},{128,0},{192,64},{1,129},{65,193},{129,1},{193,65... | collective-permute-start | bytes 196616 | tf_op jit(solution)/shard_map/value_over_liq/ppermute | solution.py:274
  4.3 0.9 %collective-permute-start.2 = (f32[128,128]{1,0:T(8,128)}, f32[128,128]{1,0:T(8,128)S(1)}, u32[]{:S(2)}, u32[]{:S(2)}) collective-permute-start(f32[128,128]{1,0:T(8,128)} %bitcast.35), channel_id=1, source_target_pairs={{0,64},{64,128},{128,192},{192,0},{1,65},{65,129},{129,193},{193,1... | collective-permute-start | bytes 196616 | tf_op jit(solution)/shard_map/value_over_liq/ppermute | solution.py:274
  5.2 0.9 %copy.15 = f32[2,2,32,128]{3,2,1,0:T(8,128)S(1)} copy(f32[2,2,32,128]{3,0,1,2:T(2,128)} %bitcast.36) | data formatting | bytes 131072 | tf_op jit(solution)/shard_map/value_over_liq/transpose | solution.py:296
  6.0 0.0 copy-start
  6.0 0.8 %copy-done = s32[32,2,2,128]{3,2,1,0:T(2,128)S(1)} copy-done((s32[32,2,2,128]{3,2,1,0:T(2,128)S(1)}, s32[32,2,2,128]{3,2,1,0:T(2,128)}, u32[]{:S(2)}) %copy-start) | copy-done | bytes 65560
  6.9 0.0 copy-start.10
  6.9 0.0 copy-start.11
  6.9 0.0 copy-start.7
  6.9 0.0 copy-start.1
  6.9 0.0 copy-start.2
  6.9 0.0 copy-start.3
  6.9 0.0 copy-start.4
  6.9 0.0 copy-start.5
  7.0 0.0 copy-start.6
  7.0 1.4 %hot.1.hot_ref = bf16[8192,128]{1,0:T(8,128)(2,1)S(1)} custom-call(s32[128,128]{1,0:T(8,128)S(1)} %bitcast.15), custom_call_target="tpu_custom_call" | custom-call | tf_op jit(solution)/shard_map/hot/pallas_call | solution.py:257
  8.3 0.0 collective-permute-done.v1
  8.4 1.1 %collective-permute-done.1.v2 = f32[128,128]{1,0:T(8,128)S(1)} collective-permute-done((f32[128,128]{1,0:T(8,128)}, f32[128,128]{1,0:T(8,128)S(1)}, u32[]{:S(2)}, u32[]{:S(2)}) %collective-permute-start.1) | collective-permute-done | bytes 65568 | tf_op jit(solution)/shard_map/value_over_liq/ppermute | solution.py:274
  9.5 0.7 %collective-permute-done.2.v3 = f32[128,128]{1,0:T(8,128)S(1)} collective-permute-done((f32[128,128]{1,0:T(8,128)}, f32[128,128]{1,0:T(8,128)S(1)}, u32[]{:S(2)}, u32[]{:S(2)}) %collective-permute-start.2) | collective-permute-done | bytes 65568 | tf_op jit(solution)/shard_map/value_over_liq/ppermute | solution.py:274
  10.2 1.0 %collective-permute-start.3 = (f32[256,128]{1,0:T(8,128)S(1)}, f32[256,128]{1,0:T(8,128)S(1)}, u32[]{:S(2)}, u32[]{:S(2)}) collective-permute-start(f32[256,128]{1,0:T(8,128)S(1)} %value_over_ill.1), channel_id=1, source_target_pairs={{0,56},{8,0},{16,8},{24,16},{32,24},{40,32},{48,40},{56,48},{1,57}... | collective-permute-start | bytes 393224 | tf_op jit(solution)/shard_map/value_over_ill/ppermute | solution.py:279
  11.2 0.0 copy-done.10
  11.2 0.0 copy-done.11
  11.2 0.1 broadcast_select_fusion
  11.3 0.0 copy-done.9
  11.3 0.1 copy.14
  11.4 0.0 copy-done.8
  11.4 0.0 copy-done.7
  11.4 0.1 fusion.table_ref
  11.5 0.0 copy-done.1
  11.5 0.0 copy-done.2
  11.5 0.0 copy-done.3
  11.5 0.0 copy-done.4
  11.5 0.0 copy-done.5
  11.5 0.0 copy-done.6
  11.5 1.8 %first_half.1 = (f32[256,128]{1,0:T(8,128)S(1)}, f32[64,128]{1,0:T(8,128)S(1)}, f32[256,128]{1,0:T(8,128)S(1)}) custom-call(f32[40,128]{1,0:T(8,128)S(1)} %fusion.table_ref, f32[128,128]{1,0:T(8,128)S(1)} %bitcast.25, f32[128,128]{1,0:T(8,128)S(1)} %collective-permute-done.v1, f32[128,128]{1,0:T(8,128)S(1)} %collective-permute-done.1.v2, ...), custom_call_target="tpu_custom_call" | custom-call | tf_op jit(solution)/shard_map/first_half/pallas_call | solution.py:257
  13.3 0.4 %collective-permute-done.3.halo_ref = f32[256,128]{1,0:T(8,128)S(1)} collective-permute-done((f32[256,128]{1,0:T(8,128)S(1)}, f32[256,128]{1,0:T(8,128)S(1)}, u32[]{:S(2)}, u32[]{:S(2)}) %collective-permute-start.3) | collective-permute-done | bytes 131104 | tf_op jit(solution)/shard_map/value_over_ill/ppermute | solution.py:279
  13.7 1.1 %second_half.1 = (f32[128,128]{1,0:T(8,128)S(1)}, f32[128,128]{1,0:T(8,128)S(1)}, f32[128,128]{1,0:T(8,128)S(1)}, f32[128,128]{1,0:T(8,128)S(1)}, f32[64,128]{1,0:T(8,128)S(1)}) custom-call(f32[40,128]{1,0:T(8,128)S(1)} %fusion.table_ref, f32[256,128]{1,0:T(8,128)S(1)} %get-tuple-element.16.upper_ref, f32[256,128]{1,0:T(8,128)S(1)} %collective-permute-done.3.halo_ref, ...), custom_call_target="tpu_custom_call" | custom-call | bytes 30000000 | tf_op jit(solution)/shard_map/second_half/pallas_call | solution.py:257
  14.8 1.2 %collective-permute-start.4 = (f32[128,128]{1,0:T(8,128)S(1)}, f32[128,128]{1,0:T(8,128)S(1)}, u32[]{:S(2)}, u32[]{:S(2)}) collective-permute-start(f32[128,128]{1,0:T(8,128)S(1)} %get-tuple-element.19), channel_id=1, source_target_pairs={{0,192},{64,0},{128,64},{192,128},{1,193},{65,1},{129,65},{193,129... | collective-permute-start | bytes 196616 | tf_op jit(solution)/shard_map/mass_over_liq/ppermute | solution.py:274
  16.0 1.5 %collective-permute-start.5 = (f32[128,128]{1,0:T(8,128)S(1)}, f32[128,128]{1,0:T(8,128)S(1)}, u32[]{:S(2)}, u32[]{:S(2)}) collective-permute-start(f32[128,128]{1,0:T(8,128)S(1)} %get-tuple-element.20), channel_id=1, source_target_pairs={{0,128},{64,192},{128,0},{192,64},{1,129},{65,193},{129,1},{193,65... | collective-permute-start | bytes 196616 | tf_op jit(solution)/shard_map/mass_over_liq/ppermute | solution.py:274
  17.6 0.5 %collective-permute-start.6 = (f32[128,128]{1,0:T(8,128)S(1)}, f32[128,128]{1,0:T(8,128)S(1)}, u32[]{:S(2)}, u32[]{:S(2)}) collective-permute-start(f32[128,128]{1,0:T(8,128)S(1)} %get-tuple-element.21), channel_id=1, source_target_pairs={{0,64},{64,128},{128,192},{192,0},{1,65},{65,129},{129,193},{193,1... | collective-permute-start | bytes 196616 | tf_op jit(solution)/shard_map/mass_over_liq/ppermute | solution.py:274
  18.1 2.2 %collective-permute-start.7 = (f32[64,128]{1,0:T(8,128)S(1)}, f32[64,128]{1,0:T(8,128)S(1)}, u32[]{:S(2)}, u32[]{:S(2)}) collective-permute-start(f32[64,128]{1,0:T(8,128)S(1)} %get-tuple-element.22.lower_ref), channel_id=1, source_target_pairs={{0,56},{8,0},{16,8},{24,16},{32,24},{40,32},{48,40},{56,48},{1,57}... | collective-permute-start | bytes 98312 | tf_op jit(solution)/shard_map/expected_over_ill/ppermute | solution.py:279
  20.3 1.6 %collective-permute-done.7.halo_ref = f32[64,128]{1,0:T(8,128)S(1)} collective-permute-done((f32[64,128]{1,0:T(8,128)S(1)}, f32[64,128]{1,0:T(8,128)S(1)}, u32[]{:S(2)}, u32[]{:S(2)}) %collective-permute-start.7) | collective-permute-done | bytes 32800 | tf_op jit(solution)/shard_map/expected_over_ill/ppermute | solution.py:279
  21.9 0.0 collective-permute-done.4.p1
  21.9 0.0 collective-permute-done.5.p2
  21.9 1.2 %collective-permute-done.6.p3 = f32[128,128]{1,0:T(8,128)S(1)} collective-permute-done((f32[128,128]{1,0:T(8,128)S(1)}, f32[128,128]{1,0:T(8,128)S(1)}, u32[]{:S(2)}, u32[]{:S(2)}) %collective-permute-start.6) | collective-permute-done | bytes 65568 | tf_op jit(solution)/shard_map/mass_over_liq/ppermute | solution.py:274
  23.2 0.1 collective-permute-start.11
  23.3 0.3 collective-permute-start.10
  23.6 0.9 %collective-permute-done.11.core_ref = f32[136,128]{1,0:T(8,128)S(1)} collective-permute-done((f32[136,128]{1,0:T(8,128)S(1)}, f32[136,128]{1,0:T(8,128)S(1)}, u32[]{:S(2)}, u32[]{:S(2)}) %collective-permute-start.11) | collective-permute-done | bytes 69664 | tf_op jit(solution)/shard_map/mass_over_core/ppermute | solution.py:337
  24.5 2.0 %collective-permute-start.12 = (f32[144,128]{1,0:T(8,128)S(1)}, f32[144,128]{1,0:T(8,128)S(1)}, u32[]{:S(2)}, u32[]{:S(2)}) collective-permute-start(f32[144,128]{1,0:T(8,128)S(1)} %leave.1), channel_id=1, source_target_pairs={{1,0},{2,1},{3,2},{4,3},{5,4},{6,5},{7,6},{9,8},{10,9},{11,10},{12... | collective-permute-start | bytes 221192 | tf_op jit(solution)/shard_map/mass_over_dur/ppermute | solution.py:341
  26.5 2.1 %collective-permute-start.8 = (f32[192,128]{1,0:T(8,128)S(1)}, f32[192,128]{1,0:T(8,128)S(1)}, u32[]{:S(2)}, u32[]{:S(2)}) collective-permute-start(f32[192,128]{1,0:T(8,128)S(1)} %get-tuple-element.24.e0), channel_id=1, source_target_pairs={{0,192},{64,0},{128,64},{192,128},{1,193},{65,1},{129,65},{193,129... | collective-permute-start | bytes 294920 | tf_op jit(solution)/shard_map/expected_over_liq/ppermute | solution.py:274
  28.7 0.6 %collective-permute-start.9 = (f32[192,128]{1,0:T(8,128)S(1)}, f32[192,128]{1,0:T(8,128)S(1)}, u32[]{:S(2)}, u32[]{:S(2)}) collective-permute-start(f32[192,128]{1,0:T(8,128)S(1)} %get-tuple-element.24.e0), channel_id=1, source_target_pairs={{0,128},{64,192},{128,0},{192,64},{1,129},{65,193},{129,1},{193,65... | collective-permute-start | bytes 294920 | tf_op jit(solution)/shard_map/expected_over_liq/ppermute | solution.py:274
  29.2 2.9 %collective-permute-done.12.dur_ref = f32[144,128]{1,0:T(8,128)S(1)} collective-permute-done((f32[144,128]{1,0:T(8,128)S(1)}, f32[144,128]{1,0:T(8,128)S(1)}, u32[]{:S(2)}, u32[]{:S(2)}) %collective-permute-start.12) | collective-permute-done | bytes 73760 | tf_op jit(solution)/shard_map/mass_over_dur/ppermute | solution.py:341
  32.1 0.3 settle.1
  32.4 0.7 %collective-permute-start.13 = (f32[128,128]{1,0:T(8,128)S(1)}, f32[128,128]{1,0:T(8,128)S(1)}, u32[]{:S(2)}, u32[]{:S(2)}) collective-permute-start(f32[128,128]{1,0:T(8,128)S(1)} %get-tuple-element.27), channel_id=1, source_target_pairs={{0,16},{8,24},{16,32},{24,40},{32,48},{40,56},{48,0},{56,8},{1,17}... | collective-permute-start | bytes 196616 | tf_op jit(solution)/shard_map/mass_over_ill/ppermute | solution.py:347
  33.2 3.0 %collective-permute-start.14 = (f32[128,128]{1,0:T(8,128)S(1)}, f32[128,128]{1,0:T(8,128)S(1)}, u32[]{:S(2)}, u32[]{:S(2)}) collective-permute-start(f32[128,128]{1,0:T(8,128)S(1)} %get-tuple-element.28), channel_id=1, source_target_pairs={{0,32},{8,40},{16,48},{24,56},{32,0},{40,8},{48,16},{56,24},{1,33}... | collective-permute-start | bytes 196616 | tf_op jit(solution)/shard_map/mass_over_ill/ppermute | solution.py:347
  36.2 0.0 collective-permute-done.10.e3
  36.2 1.4 %collective-permute-start.15 = (f32[128,128]{1,0:T(8,128)S(1)}, f32[128,128]{1,0:T(8,128)S(1)}, u32[]{:S(2)}, u32[]{:S(2)}) collective-permute-start(f32[128,128]{1,0:T(8,128)S(1)} %get-tuple-element.29), channel_id=1, source_target_pairs={{0,48},{8,56},{16,0},{24,8},{32,16},{40,24},{48,32},{56,40},{1,49}... | collective-permute-start | bytes 196616 | tf_op jit(solution)/shard_map/mass_over_ill/ppermute | solution.py:347
  37.5 0.0 collective-permute-done.8.e1
  37.5 0.0 collective-permute-done.9.e2
  37.5 1.1 %consume.1 = f32[128,128]{1,0:T(8,128)} custom-call(f32[40,128]{1,0:T(8,128)S(1)} %fusion.table_ref, f32[192,128]{1,0:T(8,128)S(1)} %get-tuple-element.24.e0, f32[192,128]{1,0:T(8,128)S(1)} %collective-permute-done.8.e1, f32[192,128]{1,0:T(8,128)S(1)} %collective-permute-done.9.e2, f32[192,128]{1,0:T(8,128)S(1)} %collective-permute-done.10.e3, ...), custom_call_target="tpu_custom_call" | custom-call | tf_op jit(solution)/shard_map/consume/pallas_call | solution.py:257
  38.6 0.0 collective-permute-done.13.s1
  38.6 0.5 %collective-permute-done.14.s2 = f32[128,128]{1,0:T(8,128)S(1)} collective-permute-done((f32[128,128]{1,0:T(8,128)S(1)}, f32[128,128]{1,0:T(8,128)S(1)}, u32[]{:S(2)}, u32[]{:S(2)}) %collective-permute-start.14) | collective-permute-done | bytes 65568 | tf_op jit(solution)/shard_map/mass_over_ill/ppermute | solution.py:347
  39.1 1.3 %collective-permute-done.15.s3 = f32[128,128]{1,0:T(8,128)S(1)} collective-permute-done((f32[128,128]{1,0:T(8,128)S(1)}, f32[128,128]{1,0:T(8,128)S(1)}, u32[]{:S(2)}, u32[]{:S(2)}) %collective-permute-start.15) | collective-permute-done | bytes 65568 | tf_op jit(solution)/shard_map/mass_over_ill/ppermute | solution.py:347
  40.4 0.9 %population.1 = f32[128,128]{1,0:T(8,128)} custom-call(f32[40,128]{1,0:T(8,128)S(1)} %fusion.table_ref, f32[128,128]{1,0:T(8,128)S(1)} %get-tuple-element.26.s0, f32[128,128]{1,0:T(8,128)S(1)} %collective-permute-done.13.s1, f32[128,128]{1,0:T(8,128)S(1)} %collective-permute-done.14.s2, f32[128,128]{1,0:T(8,128)S(1)} %collective-permute-done.15.s3), custom_call_target="tpu_custom_call" | custom-call | tf_op jit(solution)/shard_map/population/pallas_call | solution.py:257
  (9 shorter events, 0.1 us)
Async XLA Ops:
  0.6 7.7 %collective-permute-start = (f32[128,128]{1,0:T(8,128)}, f32[128,128]{1,0:T(8,128)S(1)}, u32[]{:S(2)}, u32[]{:S(2)}) collective-permute-start(f32[128,128]{1,0:T(8,128)} %bitcast.33), channel_id=1, source_target_pairs={{0,192},{64,0},{128,64},{192,128},{1,193},{65,1},{129,65},{193,129... | collective-permute-start | bytes 196616 | tf_op jit(solution)/shard_map/value_over_liq/ppermute | solution.py:274
  3.5 6.0 %collective-permute-start.1 = (f32[128,128]{1,0:T(8,128)}, f32[128,128]{1,0:T(8,128)S(1)}, u32[]{:S(2)}, u32[]{:S(2)}) collective-permute-start(f32[128,128]{1,0:T(8,128)} %bitcast.34), channel_id=1, source_target_pairs={{0,128},{64,192},{128,0},{192,64},{1,129},{65,193},{129,1},{193,65... | collective-permute-start | bytes 196616 | tf_op jit(solution)/shard_map/value_over_liq/ppermute | solution.py:274
  4.3 5.9 %collective-permute-start.2 = (f32[128,128]{1,0:T(8,128)}, f32[128,128]{1,0:T(8,128)S(1)}, u32[]{:S(2)}, u32[]{:S(2)}) collective-permute-start(f32[128,128]{1,0:T(8,128)} %bitcast.35), channel_id=1, source_target_pairs={{0,64},{64,128},{128,192},{192,0},{1,65},{65,129},{129,193},{193,1... | collective-permute-start | bytes 196616 | tf_op jit(solution)/shard_map/value_over_liq/ppermute | solution.py:274
  6.0 0.8 %copy-start = (s32[32,2,2,128]{3,2,1,0:T(2,128)S(1)}, s32[32,2,2,128]{3,2,1,0:T(2,128)}, u32[]{:S(2)}) copy-start(s32[32,2,2,128]{3,2,1,0:T(2,128)} %param.21) | copy-start | bytes 196612
  6.9 4.3 %copy-start.10 = (f32[2]{0:T(128)S(1)}, f32[2]{0:T(128)}, u32[]{:S(2)}) copy-start(f32[2]{0:T(128)} %param.16) | copy-start | bytes 28
  6.9 4.3 %copy-start.11 = (f32[2]{0:T(128)S(1)}, f32[2]{0:T(128)}, u32[]{:S(2)}) copy-start(f32[2]{0:T(128)} %param.15) | copy-start | bytes 28
  6.9 4.4 %copy-start.9 = (f32[32]{0:T(128)S(1)}, f32[32]{0:T(128)}, u32[]{:S(2)}) copy-start(f32[32]{0:T(128)} %param.14) | copy-start | bytes 388
  6.9 4.5 %copy-start.8 = (s32[32,2,2]{0,2,1:T(2,128)S(1)}, s32[32,2,2]{0,2,1:T(2,128)}, u32[]{:S(2)}) copy-start(s32[32,2,2]{0,2,1:T(2,128)} %param.22) | copy-start | bytes 1540
  6.9 4.5 %copy-start.7 = (f32[32,32]{1,0:T(8,128)S(1)}, f32[32,32]{1,0:T(8,128)}, u32[]{:S(2)}) copy-start(f32[32,32]{1,0:T(8,128)} %param.13) | copy-start | bytes 12292
  6.9 4.6 %copy-start.1 = (s32[32,2,2,128]{3,2,1,0:T(2,128)S(1)}, s32[32,2,2,128]{3,2,1,0:T(2,128)}, u32[]{:S(2)}) copy-start(s32[32,2,2,128]{3,2,1,0:T(2,128)} %param.21) | copy-start | bytes 196612
  6.9 4.6 %copy-start.2 = (s32[32,2,2,128]{3,2,1,0:T(2,128)S(1)}, s32[32,2,2,128]{3,2,1,0:T(2,128)}, u32[]{:S(2)}) copy-start(s32[32,2,2,128]{3,2,1,0:T(2,128)} %param.17) | copy-start | bytes 196612
  6.9 4.6 %copy-start.3 = (f32[32,2,2,128]{3,2,1,0:T(2,128)S(1)}, f32[32,2,2,128]{3,2,1,0:T(2,128)}, u32[]{:S(2)}) copy-start(f32[32,2,2,128]{3,2,1,0:T(2,128)} %param.18) | copy-start | bytes 196612
  6.9 4.6 %copy-start.4 = (f32[32,2,2,128]{3,2,1,0:T(2,128)S(1)}, f32[32,2,2,128]{3,2,1,0:T(2,128)}, u32[]{:S(2)}) copy-start(f32[32,2,2,128]{3,2,1,0:T(2,128)} %param.19) | copy-start | bytes 196612
  6.9 4.6 %copy-start.5 = (f32[32,2,2,128]{3,2,1,0:T(2,128)S(1)}, f32[32,2,2,128]{3,2,1,0:T(2,128)}, u32[]{:S(2)}) copy-start(f32[32,2,2,128]{3,2,1,0:T(2,128)} %param.20) | copy-start | bytes 196612
  7.0 4.6 %copy-start.6 = (f32[32,2,2,128]{3,2,1,0:T(2,128)S(1)}, f32[32,2,2,128]{3,2,1,0:T(2,128)}, u32[]{:S(2)}) copy-start(f32[32,2,2,128]{3,2,1,0:T(2,128)} %param.23) | copy-start | bytes 196612
  10.2 3.6 %collective-permute-start.3 = (f32[256,128]{1,0:T(8,128)S(1)}, f32[256,128]{1,0:T(8,128)S(1)}, u32[]{:S(2)}, u32[]{:S(2)}) collective-permute-start(f32[256,128]{1,0:T(8,128)S(1)} %value_over_ill.1), channel_id=1, source_target_pairs={{0,56},{8,0},{16,8},{24,16},{32,24},{40,32},{48,40},{56,48},{1,57}... | collective-permute-start | bytes 393224 | tf_op jit(solution)/shard_map/value_over_ill/ppermute | solution.py:279
  14.8 7.1 %collective-permute-start.4 = (f32[128,128]{1,0:T(8,128)S(1)}, f32[128,128]{1,0:T(8,128)S(1)}, u32[]{:S(2)}, u32[]{:S(2)}) collective-permute-start(f32[128,128]{1,0:T(8,128)S(1)} %get-tuple-element.19), channel_id=1, source_target_pairs={{0,192},{64,0},{128,64},{192,128},{1,193},{65,1},{129,65},{193,129... | collective-permute-start | bytes 196616 | tf_op jit(solution)/shard_map/mass_over_liq/ppermute | solution.py:274
  16.0 5.9 %collective-permute-start.5 = (f32[128,128]{1,0:T(8,128)S(1)}, f32[128,128]{1,0:T(8,128)S(1)}, u32[]{:S(2)}, u32[]{:S(2)}) collective-permute-start(f32[128,128]{1,0:T(8,128)S(1)} %get-tuple-element.20), channel_id=1, source_target_pairs={{0,128},{64,192},{128,0},{192,64},{1,129},{65,193},{129,1},{193,65... | collective-permute-start | bytes 196616 | tf_op jit(solution)/shard_map/mass_over_liq/ppermute | solution.py:274
  17.6 5.6 %collective-permute-start.6 = (f32[128,128]{1,0:T(8,128)S(1)}, f32[128,128]{1,0:T(8,128)S(1)}, u32[]{:S(2)}, u32[]{:S(2)}) collective-permute-start(f32[128,128]{1,0:T(8,128)S(1)} %get-tuple-element.21), channel_id=1, source_target_pairs={{0,64},{64,128},{128,192},{192,0},{1,65},{65,129},{129,193},{193,1... | collective-permute-start | bytes 196616 | tf_op jit(solution)/shard_map/mass_over_liq/ppermute | solution.py:274
  18.1 3.8 %collective-permute-start.7 = (f32[64,128]{1,0:T(8,128)S(1)}, f32[64,128]{1,0:T(8,128)S(1)}, u32[]{:S(2)}, u32[]{:S(2)}) collective-permute-start(f32[64,128]{1,0:T(8,128)S(1)} %get-tuple-element.22.lower_ref), channel_id=1, source_target_pairs={{0,56},{8,0},{16,8},{24,16},{32,24},{40,32},{48,40},{56,48},{1,57}... | collective-permute-start | bytes 98312 | tf_op jit(solution)/shard_map/expected_over_ill/ppermute | solution.py:279
  23.2 1.3 %collective-permute-start.11 = (f32[136,128]{1,0:T(8,128)S(1)}, f32[136,128]{1,0:T(8,128)S(1)}, u32[]{:S(2)}, u32[]{:S(2)}) collective-permute-start(f32[136,128]{1,0:T(8,128)S(1)} %get-tuple-element.25.own_ref), channel_id=1, source_target_pairs={{0,8},{8,0},{16,24},{24,16},{32,40},{40,32},{48,56},{56,48},{1,9},... | collective-permute-start | bytes 208904 | tf_op jit(solution)/shard_map/mass_over_core/ppermute | solution.py:337
  23.3 12.9 %collective-permute-start.10 = (f32[192,128]{1,0:T(8,128)S(1)}, f32[192,128]{1,0:T(8,128)S(1)}, u32[]{:S(2)}, u32[]{:S(2)}) collective-permute-start(f32[192,128]{1,0:T(8,128)S(1)} %get-tuple-element.24.e0), channel_id=1, source_target_pairs={{0,64},{64,128},{128,192},{192,0},{1,65},{65,129},{129,193},{193,1... | collective-permute-start | bytes 294920 | tf_op jit(solution)/shard_map/expected_over_liq/ppermute | solution.py:274
  24.5 7.6 %collective-permute-start.12 = (f32[144,128]{1,0:T(8,128)S(1)}, f32[144,128]{1,0:T(8,128)S(1)}, u32[]{:S(2)}, u32[]{:S(2)}) collective-permute-start(f32[144,128]{1,0:T(8,128)S(1)} %leave.1), channel_id=1, source_target_pairs={{1,0},{2,1},{3,2},{4,3},{5,4},{6,5},{7,6},{9,8},{10,9},{11,10},{12... | collective-permute-start | bytes 221192 | tf_op jit(solution)/shard_map/mass_over_dur/ppermute | solution.py:341
  26.5 11.0 %collective-permute-start.8 = (f32[192,128]{1,0:T(8,128)S(1)}, f32[192,128]{1,0:T(8,128)S(1)}, u32[]{:S(2)}, u32[]{:S(2)}) collective-permute-start(f32[192,128]{1,0:T(8,128)S(1)} %get-tuple-element.24.e0), channel_id=1, source_target_pairs={{0,192},{64,0},{128,64},{192,128},{1,193},{65,1},{129,65},{193,129... | collective-permute-start | bytes 294920 | tf_op jit(solution)/shard_map/expected_over_liq/ppermute | solution.py:274
  28.7 8.9 %collective-permute-start.9 = (f32[192,128]{1,0:T(8,128)S(1)}, f32[192,128]{1,0:T(8,128)S(1)}, u32[]{:S(2)}, u32[]{:S(2)}) collective-permute-start(f32[192,128]{1,0:T(8,128)S(1)} %get-tuple-element.24.e0), channel_id=1, source_target_pairs={{0,128},{64,192},{128,0},{192,64},{1,129},{65,193},{129,1},{193,65... | collective-permute-start | bytes 294920 | tf_op jit(solution)/shard_map/expected_over_liq/ppermute | solution.py:274
  32.4 6.2 %collective-permute-start.13 = (f32[128,128]{1,0:T(8,128)S(1)}, f32[128,128]{1,0:T(8,128)S(1)}, u32[]{:S(2)}, u32[]{:S(2)}) collective-permute-start(f32[128,128]{1,0:T(8,128)S(1)} %get-tuple-element.27), channel_id=1, source_target_pairs={{0,16},{8,24},{16,32},{24,40},{32,48},{40,56},{48,0},{56,8},{1,17}... | collective-permute-start | bytes 196616 | tf_op jit(solution)/shard_map/mass_over_ill/ppermute | solution.py:347
  33.2 5.9 %collective-permute-start.14 = (f32[128,128]{1,0:T(8,128)S(1)}, f32[128,128]{1,0:T(8,128)S(1)}, u32[]{:S(2)}, u32[]{:S(2)}) collective-permute-start(f32[128,128]{1,0:T(8,128)S(1)} %get-tuple-element.28), channel_id=1, source_target_pairs={{0,32},{8,40},{16,48},{24,56},{32,0},{40,8},{48,16},{56,24},{1,33}... | collective-permute-start | bytes 196616 | tf_op jit(solution)/shard_map/mass_over_ill/ppermute | solution.py:347
  36.2 4.3 %collective-permute-start.15 = (f32[128,128]{1,0:T(8,128)S(1)}, f32[128,128]{1,0:T(8,128)S(1)}, u32[]{:S(2)}, u32[]{:S(2)}) collective-permute-start(f32[128,128]{1,0:T(8,128)S(1)} %get-tuple-element.29), channel_id=1, source_target_pairs={{0,48},{8,56},{16,0},{24,8},{32,16},{40,24},{48,32},{56,40},{1,49}... | collective-permute-start | bytes 196616 | tf_op jit(solution)/shard_map/mass_over_ill/ppermute | solution.py:347

commit v5 on v4

--- a/solution.py
+++ b/solution.py
@@ -174,7 +174,7 @@
         expected_ref[d * Z : (d + 1) * Z, :] = expected[d]
 
 
-def consume_kernel(table_ref, e0, e1, e2, e3, index_ref, weight_ref, out_ref):
+def consume_kernel(table_ref, e0, e2, e1, e3, index_ref, weight_ref, out_ref):
     pieces = (e0, e1, e2, e3)
     for a in range(2):
         for d in range(2):
@@ -346,7 +346,7 @@
     with jax.named_scope("mass_over_ill"):
         arrived = [lax.ppermute(parts[k], "ill", turned("ill", 2 * k)) for k in range(1, 4)]
     with jax.named_scope("consume"):
-        consumption = call(consume_kernel, [PLANE_ROWS], [table, *expected_pieces, index, weight])
+        consumption = call(consume_kernel, [PLANE_ROWS], [table, *(expected_pieces[q] for q in (0, 2, 1, 3)), index, weight])
     with jax.named_scope("population"):
         population_next = call(population_kernel, [PLANE_ROWS], [table, parts[0], *arrived])
     shape = population.shape

time: 41.5 us -> 41.5 us (level)
  waiting for transfers between devices: 10.7 us -> 10 us
  starting transfers between devices: 21.3 us -> 21.9 us
    ppermute x9, starting transfers between devices: 10.8 us -> 11.4 us  [from_other_liq(): lax.ppermute(pieces[k], 'liq', turned('liq', k))]
    ppermute x1, waiting for transfers between devices: 2.89 us -> 2.28 us  [body(): from_dur = lax.ppermute(to_dur, 'dur', below_dur)]
where the time goes in v5:
time: 41.5 us; the launch traced here: 41.3 us
  starting transfers between devices  21.9 us (53%)
  waiting for transfers between devices  10 us (24%)
  Pallas kernels  6.54 us (16%)
  local copies, waits for them, and re-layouts  1.86 us (4%)
  between operations  0.82 us (2%)
    ppermute x9, starting transfers between devices, from_other_liq(): lax.ppermute(pieces[k], 'liq', turned('liq', k))  11.4 us
    pallas_call x9, Pallas kernels, call(): pl.pallas_call(kernel, out_shape=shapes[0] if single else shapes, in_spec...  6.54 us
    ppermute x3, starting transfers between devices, body(): lax.ppermute(parts[k], 'ill', turned('ill', 2 * k))  5.08 us
    ppermute x2, starting transfers between devices, from_above_ill(): return lax.ppermute(x, 'ill', turned('ill', -1))  3.28 us
    ppermute x9, waiting for transfers between devices, from_other_liq(): lax.ppermute(pieces[k], 'liq', turned('liq', k))  2.99 us
    ppermute x1, waiting for transfers between devices, body(): from_dur = lax.ppermute(to_dur, 'dur', below_dur)  2.28 us
    ppermute x2, waiting for transfers between devices, from_above_ill(): return lax.ppermute(x, 'ill', turned('ill', -1))  2.04 us
    ppermute x1, starting transfers between devices, body(): from_dur = lax.ppermute(to_dur, 'dur', below_dur)  2.02 us
  transfers between devices with their start and end apart: 16, of which 9 were waited for; matrix products, arithmetic and copies ran while one was open for 3% of the time, Pallas kernels for 11%

profile of v5, /device:TPU:96, one launch (start us, length us, event | category | flops | bytes accessed | tf_op | source)
XLA Modules:
  0.0 41.3 jit_solution(1588377095961717930)
XLA Ops:
  0.6 2.8 %collective-permute-start = (f32[128,128]{1,0:T(8,128)}, f32[128,128]{1,0:T(8,128)S(1)}, u32[]{:S(2)}, u32[]{:S(2)}) collective-permute-start(f32[128,128]{1,0:T(8,128)} %bitcast.33), channel_id=1, source_target_pairs={{0,192},{64,0},{128,64},{192,128},{1,193},{65,1},{129,65},{193,129... | collective-permute-start | bytes 196616 | tf_op jit(solution)/shard_map/value_over_liq/ppermute | solution.py:274
  3.5 0.8 %collective-permute-start.1 = (f32[128,128]{1,0:T(8,128)}, f32[128,128]{1,0:T(8,128)S(1)}, u32[]{:S(2)}, u32[]{:S(2)}) collective-permute-start(f32[128,128]{1,0:T(8,128)} %bitcast.34), channel_id=1, source_target_pairs={{0,128},{64,192},{128,0},{192,64},{1,129},{65,193},{129,1},{193,65... | collective-permute-start | bytes 196616 | tf_op jit(solution)/shard_map/value_over_liq/ppermute | solution.py:274
  4.3 0.9 %collective-permute-start.2 = (f32[128,128]{1,0:T(8,128)}, f32[128,128]{1,0:T(8,128)S(1)}, u32[]{:S(2)}, u32[]{:S(2)}) collective-permute-start(f32[128,128]{1,0:T(8,128)} %bitcast.35), channel_id=1, source_target_pairs={{0,64},{64,128},{128,192},{192,0},{1,65},{65,129},{129,193},{193,1... | collective-permute-start | bytes 196616 | tf_op jit(solution)/shard_map/value_over_liq/ppermute | solution.py:274
  5.2 0.9 %copy.15 = f32[2,2,32,128]{3,2,1,0:T(8,128)S(1)} copy(f32[2,2,32,128]{3,0,1,2:T(2,128)} %bitcast.36) | data formatting | bytes 131072 | tf_op jit(solution)/shard_map/value_over_liq/transpose | solution.py:296
  6.0 0.0 copy-start
  6.0 0.8 %copy-done = s32[32,2,2,128]{3,2,1,0:T(2,128)S(1)} copy-done((s32[32,2,2,128]{3,2,1,0:T(2,128)S(1)}, s32[32,2,2,128]{3,2,1,0:T(2,128)}, u32[]{:S(2)}) %copy-start) | copy-done | bytes 65560
  6.9 0.0 copy-start.10
  6.9 0.0 copy-start.11
  6.9 0.0 copy-start.7
  6.9 0.0 copy-start.1
  6.9 0.0 copy-start.2
  6.9 0.0 copy-start.3
  6.9 0.0 copy-start.4
  6.9 0.0 copy-start.5
  7.0 0.0 copy-start.6
  7.0 1.4 %hot.1.hot_ref = bf16[8192,128]{1,0:T(8,128)(2,1)S(1)} custom-call(s32[128,128]{1,0:T(8,128)S(1)} %bitcast.15), custom_call_target="tpu_custom_call" | custom-call | tf_op jit(solution)/shard_map/hot/pallas_call | solution.py:257
  8.3 0.0 collective-permute-done.v1
  8.4 1.1 %collective-permute-done.1.v2 = f32[128,128]{1,0:T(8,128)S(1)} collective-permute-done((f32[128,128]{1,0:T(8,128)}, f32[128,128]{1,0:T(8,128)S(1)}, u32[]{:S(2)}, u32[]{:S(2)}) %collective-permute-start.1) | collective-permute-done | bytes 65568 | tf_op jit(solution)/shard_map/value_over_liq/ppermute | solution.py:274
  9.5 0.7 %collective-permute-done.2.v3 = f32[128,128]{1,0:T(8,128)S(1)} collective-permute-done((f32[128,128]{1,0:T(8,128)}, f32[128,128]{1,0:T(8,128)S(1)}, u32[]{:S(2)}, u32[]{:S(2)}) %collective-permute-start.2) | collective-permute-done | bytes 65568 | tf_op jit(solution)/shard_map/value_over_liq/ppermute | solution.py:274
  10.2 1.0 %collective-permute-start.3 = (f32[256,128]{1,0:T(8,128)S(1)}, f32[256,128]{1,0:T(8,128)S(1)}, u32[]{:S(2)}, u32[]{:S(2)}) collective-permute-start(f32[256,128]{1,0:T(8,128)S(1)} %value_over_ill.1), channel_id=1, source_target_pairs={{0,56},{8,0},{16,8},{24,16},{32,24},{40,32},{48,40},{56,48},{1,57}... | collective-permute-start | bytes 393224 | tf_op jit(solution)/shard_map/value_over_ill/ppermute | solution.py:279
  11.2 0.0 copy-done.10
  11.2 0.0 copy-done.11
  11.2 0.1 broadcast_select_fusion
  11.3 0.0 copy-done.9
  11.3 0.1 copy.14
  11.4 0.0 copy-done.8
  11.4 0.0 copy-done.7
  11.4 0.1 fusion.table_ref
  11.5 0.0 copy-done.1
  11.5 0.0 copy-done.2
  11.5 0.0 copy-done.3
  11.5 0.0 copy-done.4
  11.5 0.0 copy-done.5
  11.5 0.0 copy-done.6
  11.5 1.8 %first_half.1 = (f32[256,128]{1,0:T(8,128)S(1)}, f32[64,128]{1,0:T(8,128)S(1)}, f32[256,128]{1,0:T(8,128)S(1)}) custom-call(f32[40,128]{1,0:T(8,128)S(1)} %fusion.table_ref, f32[128,128]{1,0:T(8,128)S(1)} %bitcast.25, f32[128,128]{1,0:T(8,128)S(1)} %collective-permute-done.v1, f32[128,128]{1,0:T(8,128)S(1)} %collective-permute-done.1.v2, ...), custom_call_target="tpu_custom_call" | custom-call | tf_op jit(solution)/shard_map/first_half/pallas_call | solution.py:257
  13.3 0.4 %collective-permute-done.3.halo_ref = f32[256,128]{1,0:T(8,128)S(1)} collective-permute-done((f32[256,128]{1,0:T(8,128)S(1)}, f32[256,128]{1,0:T(8,128)S(1)}, u32[]{:S(2)}, u32[]{:S(2)}) %collective-permute-start.3) | collective-permute-done | bytes 131104 | tf_op jit(solution)/shard_map/value_over_ill/ppermute | solution.py:279
  13.7 1.1 %second_half.1 = (f32[128,128]{1,0:T(8,128)S(1)}, f32[128,128]{1,0:T(8,128)S(1)}, f32[128,128]{1,0:T(8,128)S(1)}, f32[128,128]{1,0:T(8,128)S(1)}, f32[64,128]{1,0:T(8,128)S(1)}) custom-call(f32[40,128]{1,0:T(8,128)S(1)} %fusion.table_ref, f32[256,128]{1,0:T(8,128)S(1)} %get-tuple-element.16.upper_ref, f32[256,128]{1,0:T(8,128)S(1)} %collective-permute-done.3.halo_ref, ...), custom_call_target="tpu_custom_call" | custom-call | bytes 30000000 | tf_op jit(solution)/shard_map/second_half/pallas_call | solution.py:257
  14.8 1.2 %collective-permute-start.4 = (f32[128,128]{1,0:T(8,128)S(1)}, f32[128,128]{1,0:T(8,128)S(1)}, u32[]{:S(2)}, u32[]{:S(2)}) collective-permute-start(f32[128,128]{1,0:T(8,128)S(1)} %get-tuple-element.19), channel_id=1, source_target_pairs={{0,192},{64,0},{128,64},{192,128},{1,193},{65,1},{129,65},{193,129... | collective-permute-start | bytes 196616 | tf_op jit(solution)/shard_map/mass_over_liq/ppermute | solution.py:274
  16.0 1.5 %collective-permute-start.5 = (f32[128,128]{1,0:T(8,128)S(1)}, f32[128,128]{1,0:T(8,128)S(1)}, u32[]{:S(2)}, u32[]{:S(2)}) collective-permute-start(f32[128,128]{1,0:T(8,128)S(1)} %get-tuple-element.20), channel_id=1, source_target_pairs={{0,128},{64,192},{128,0},{192,64},{1,129},{65,193},{129,1},{193,65... | collective-permute-start | bytes 196616 | tf_op jit(solution)/shard_map/mass_over_liq/ppermute | solution.py:274
  17.6 0.5 %collective-permute-start.6 = (f32[128,128]{1,0:T(8,128)S(1)}, f32[128,128]{1,0:T(8,128)S(1)}, u32[]{:S(2)}, u32[]{:S(2)}) collective-permute-start(f32[128,128]{1,0:T(8,128)S(1)} %get-tuple-element.21), channel_id=1, source_target_pairs={{0,64},{64,128},{128,192},{192,0},{1,65},{65,129},{129,193},{193,1... | collective-permute-start | bytes 196616 | tf_op jit(solution)/shard_map/mass_over_liq/ppermute | solution.py:274
  18.1 2.2 %collective-permute-start.7 = (f32[64,128]{1,0:T(8,128)S(1)}, f32[64,128]{1,0:T(8,128)S(1)}, u32[]{:S(2)}, u32[]{:S(2)}) collective-permute-start(f32[64,128]{1,0:T(8,128)S(1)} %get-tuple-element.22.lower_ref), channel_id=1, source_target_pairs={{0,56},{8,0},{16,8},{24,16},{32,24},{40,32},{48,40},{56,48},{1,57}... | collective-permute-start | bytes 98312 | tf_op jit(solution)/shard_map/expected_over_ill/ppermute | solution.py:279
  20.3 1.6 %collective-permute-done.7.halo_ref = f32[64,128]{1,0:T(8,128)S(1)} collective-permute-done((f32[64,128]{1,0:T(8,128)S(1)}, f32[64,128]{1,0:T(8,128)S(1)}, u32[]{:S(2)}, u32[]{:S(2)}) %collective-permute-start.7) | collective-permute-done | bytes 32800 | tf_op jit(solution)/shard_map/expected_over_ill/ppermute | solution.py:279
  21.9 0.0 collective-permute-done.4.p1
  21.9 0.0 collective-permute-done.5.p2
  21.9 1.2 %collective-permute-done.6.p3 = f32[128,128]{1,0:T(8,128)S(1)} collective-permute-done((f32[128,128]{1,0:T(8,128)S(1)}, f32[128,128]{1,0:T(8,128)S(1)}, u32[]{:S(2)}, u32[]{:S(2)}) %collective-permute-start.6) | collective-permute-done | bytes 65568 | tf_op jit(solution)/shard_map/mass_over_liq/ppermute | solution.py:274
  23.2 0.1 collective-permute-start.11
  23.3 0.3 collective-permute-start.10
  23.6 0.9 %collective-permute-done.11.core_ref = f32[136,128]{1,0:T(8,128)S(1)} collective-permute-done((f32[136,128]{1,0:T(8,128)S(1)}, f32[136,128]{1,0:T(8,128)S(1)}, u32[]{:S(2)}, u32[]{:S(2)}) %collective-permute-start.11) | collective-permute-done | bytes 69664 | tf_op jit(solution)/shard_map/mass_over_core/ppermute | solution.py:337
  24.5 2.0 %collective-permute-start.12 = (f32[144,128]{1,0:T(8,128)S(1)}, f32[144,128]{1,0:T(8,128)S(1)}, u32[]{:S(2)}, u32[]{:S(2)}) collective-permute-start(f32[144,128]{1,0:T(8,128)S(1)} %leave.1), channel_id=1, source_target_pairs={{1,0},{2,1},{3,2},{4,3},{5,4},{6,5},{7,6},{9,8},{10,9},{11,10},{12... | collective-permute-start | bytes 221192 | tf_op jit(solution)/shard_map/mass_over_dur/ppermute | solution.py:341
  26.5 1.9 %collective-permute-start.8 = (f32[192,128]{1,0:T(8,128)S(1)}, f32[192,128]{1,0:T(8,128)S(1)}, u32[]{:S(2)}, u32[]{:S(2)}) collective-permute-start(f32[192,128]{1,0:T(8,128)S(1)} %get-tuple-element.24.e0), channel_id=1, source_target_pairs={{0,128},{64,192},{128,0},{192,64},{1,129},{65,193},{129,1},{193,65... | collective-permute-start | bytes 294920 | tf_op jit(solution)/shard_map/expected_over_liq/ppermute | solution.py:274
  28.5 1.4 %collective-permute-start.9 = (f32[192,128]{1,0:T(8,128)S(1)}, f32[192,128]{1,0:T(8,128)S(1)}, u32[]{:S(2)}, u32[]{:S(2)}) collective-permute-start(f32[192,128]{1,0:T(8,128)S(1)} %get-tuple-element.24.e0), channel_id=1, source_target_pairs={{0,192},{64,0},{128,64},{192,128},{1,193},{65,1},{129,65},{193,129... | collective-permute-start | bytes 294920 | tf_op jit(solution)/shard_map/expected_over_liq/ppermute | solution.py:274
  29.9 2.3 %collective-permute-done.12.dur_ref = f32[144,128]{1,0:T(8,128)S(1)} collective-permute-done((f32[144,128]{1,0:T(8,128)S(1)}, f32[144,128]{1,0:T(8,128)S(1)}, u32[]{:S(2)}, u32[]{:S(2)}) %collective-permute-start.12) | collective-permute-done | bytes 73760 | tf_op jit(solution)/shard_map/mass_over_dur/ppermute | solution.py:341
  32.1 0.3 settle.1
  32.4 0.7 %collective-permute-start.13 = (f32[128,128]{1,0:T(8,128)S(1)}, f32[128,128]{1,0:T(8,128)S(1)}, u32[]{:S(2)}, u32[]{:S(2)}) collective-permute-start(f32[128,128]{1,0:T(8,128)S(1)} %get-tuple-element.27), channel_id=1, source_target_pairs={{0,16},{8,24},{16,32},{24,40},{32,48},{40,56},{48,0},{56,8},{1,17}... | collective-permute-start | bytes 196616 | tf_op jit(solution)/shard_map/mass_over_ill/ppermute | solution.py:347
  33.2 3.0 %collective-permute-start.14 = (f32[128,128]{1,0:T(8,128)S(1)}, f32[128,128]{1,0:T(8,128)S(1)}, u32[]{:S(2)}, u32[]{:S(2)}) collective-permute-start(f32[128,128]{1,0:T(8,128)S(1)} %get-tuple-element.28), channel_id=1, source_target_pairs={{0,32},{8,40},{16,48},{24,56},{32,0},{40,8},{48,16},{56,24},{1,33}... | collective-permute-start | bytes 196616 | tf_op jit(solution)/shard_map/mass_over_ill/ppermute | solution.py:347
  36.2 0.0 collective-permute-done.10.e3
  36.2 1.4 %collective-permute-start.15 = (f32[128,128]{1,0:T(8,128)S(1)}, f32[128,128]{1,0:T(8,128)S(1)}, u32[]{:S(2)}, u32[]{:S(2)}) collective-permute-start(f32[128,128]{1,0:T(8,128)S(1)} %get-tuple-element.29), channel_id=1, source_target_pairs={{0,48},{8,56},{16,0},{24,8},{32,16},{40,24},{48,32},{56,40},{1,49}... | collective-permute-start | bytes 196616 | tf_op jit(solution)/shard_map/mass_over_ill/ppermute | solution.py:347
  37.5 0.0 collective-permute-done.8.e2
  37.5 0.0 collective-permute-done.9.e1
  37.5 1.1 %consume.1 = f32[128,128]{1,0:T(8,128)} custom-call(f32[40,128]{1,0:T(8,128)S(1)} %fusion.table_ref, f32[192,128]{1,0:T(8,128)S(1)} %get-tuple-element.24.e0, f32[192,128]{1,0:T(8,128)S(1)} %collective-permute-done.8.e2, f32[192,128]{1,0:T(8,128)S(1)} %collective-permute-done.9.e1, f32[192,128]{1,0:T(8,128)S(1)} %collective-permute-done.10.e3, ...), custom_call_target="tpu_custom_call" | custom-call | tf_op jit(solution)/shard_map/consume/pallas_call | solution.py:257
  38.6 0.0 collective-permute-done.13.s1
  38.6 0.5 %collective-permute-done.14.s2 = f32[128,128]{1,0:T(8,128)S(1)} collective-permute-done((f32[128,128]{1,0:T(8,128)S(1)}, f32[128,128]{1,0:T(8,128)S(1)}, u32[]{:S(2)}, u32[]{:S(2)}) %collective-permute-start.14) | collective-permute-done | bytes 65568 | tf_op jit(solution)/shard_map/mass_over_ill/ppermute | solution.py:347
  39.1 1.3 %collective-permute-done.15.s3 = f32[128,128]{1,0:T(8,128)S(1)} collective-permute-done((f32[128,128]{1,0:T(8,128)S(1)}, f32[128,128]{1,0:T(8,128)S(1)}, u32[]{:S(2)}, u32[]{:S(2)}) %collective-permute-start.15) | collective-permute-done | bytes 65568 | tf_op jit(solution)/shard_map/mass_over_ill/ppermute | solution.py:347
  40.4 0.9 %population.1 = f32[128,128]{1,0:T(8,128)} custom-call(f32[40,128]{1,0:T(8,128)S(1)} %fusion.table_ref, f32[128,128]{1,0:T(8,128)S(1)} %get-tuple-element.26.s0, f32[128,128]{1,0:T(8,128)S(1)} %collective-permute-done.13.s1, f32[128,128]{1,0:T(8,128)S(1)} %collective-permute-done.14.s2, f32[128,128]{1,0:T(8,128)S(1)} %collective-permute-done.15.s3), custom_call_target="tpu_custom_call" | custom-call | tf_op jit(solution)/shard_map/population/pallas_call | solution.py:257
  (9 shorter events, 0.1 us)
Async XLA Ops:
  0.6 7.7 %collective-permute-start = (f32[128,128]{1,0:T(8,128)}, f32[128,128]{1,0:T(8,128)S(1)}, u32[]{:S(2)}, u32[]{:S(2)}) collective-permute-start(f32[128,128]{1,0:T(8,128)} %bitcast.33), channel_id=1, source_target_pairs={{0,192},{64,0},{128,64},{192,128},{1,193},{65,1},{129,65},{193,129... | collective-permute-start | bytes 196616 | tf_op jit(solution)/shard_map/value_over_liq/ppermute | solution.py:274
  3.5 6.0 %collective-permute-start.1 = (f32[128,128]{1,0:T(8,128)}, f32[128,128]{1,0:T(8,128)S(1)}, u32[]{:S(2)}, u32[]{:S(2)}) collective-permute-start(f32[128,128]{1,0:T(8,128)} %bitcast.34), channel_id=1, source_target_pairs={{0,128},{64,192},{128,0},{192,64},{1,129},{65,193},{129,1},{193,65... | collective-permute-start | bytes 196616 | tf_op jit(solution)/shard_map/value_over_liq/ppermute | solution.py:274
  4.3 5.9 %collective-permute-start.2 = (f32[128,128]{1,0:T(8,128)}, f32[128,128]{1,0:T(8,128)S(1)}, u32[]{:S(2)}, u32[]{:S(2)}) collective-permute-start(f32[128,128]{1,0:T(8,128)} %bitcast.35), channel_id=1, source_target_pairs={{0,64},{64,128},{128,192},{192,0},{1,65},{65,129},{129,193},{193,1... | collective-permute-start | bytes 196616 | tf_op jit(solution)/shard_map/value_over_liq/ppermute | solution.py:274
  6.0 0.8 %copy-start = (s32[32,2,2,128]{3,2,1,0:T(2,128)S(1)}, s32[32,2,2,128]{3,2,1,0:T(2,128)}, u32[]{:S(2)}) copy-start(s32[32,2,2,128]{3,2,1,0:T(2,128)} %param.21) | copy-start | bytes 196612
  6.9 4.3 %copy-start.10 = (f32[2]{0:T(128)S(1)}, f32[2]{0:T(128)}, u32[]{:S(2)}) copy-start(f32[2]{0:T(128)} %param.16) | copy-start | bytes 28
  6.9 4.3 %copy-start.11 = (f32[2]{0:T(128)S(1)}, f32[2]{0:T(128)}, u32[]{:S(2)}) copy-start(f32[2]{0:T(128)} %param.15) | copy-start | bytes 28
  6.9 4.4 %copy-start.9 = (f32[32]{0:T(128)S(1)}, f32[32]{0:T(128)}, u32[]{:S(2)}) copy-start(f32[32]{0:T(128)} %param.14) | copy-start | bytes 388
  6.9 4.5 %copy-start.8 = (s32[32,2,2]{0,2,1:T(2,128)S(1)}, s32[32,2,2]{0,2,1:T(2,128)}, u32[]{:S(2)}) copy-start(s32[32,2,2]{0,2,1:T(2,128)} %param.22) | copy-start | bytes 1540
  6.9 4.5 %copy-start.7 = (f32[32,32]{1,0:T(8,128)S(1)}, f32[32,32]{1,0:T(8,128)}, u32[]{:S(2)}) copy-start(f32[32,32]{1,0:T(8,128)} %param.13) | copy-start | bytes 12292
  6.9 4.6 %copy-start.1 = (s32[32,2,2,128]{3,2,1,0:T(2,128)S(1)}, s32[32,2,2,128]{3,2,1,0:T(2,128)}, u32[]{:S(2)}) copy-start(s32[32,2,2,128]{3,2,1,0:T(2,128)} %param.21) | copy-start | bytes 196612
  6.9 4.6 %copy-start.2 = (s32[32,2,2,128]{3,2,1,0:T(2,128)S(1)}, s32[32,2,2,128]{3,2,1,0:T(2,128)}, u32[]{:S(2)}) copy-start(s32[32,2,2,128]{3,2,1,0:T(2,128)} %param.17) | copy-start | bytes 196612
  6.9 4.6 %copy-start.3 = (f32[32,2,2,128]{3,2,1,0:T(2,128)S(1)}, f32[32,2,2,128]{3,2,1,0:T(2,128)}, u32[]{:S(2)}) copy-start(f32[32,2,2,128]{3,2,1,0:T(2,128)} %param.18) | copy-start | bytes 196612
  6.9 4.6 %copy-start.4 = (f32[32,2,2,128]{3,2,1,0:T(2,128)S(1)}, f32[32,2,2,128]{3,2,1,0:T(2,128)}, u32[]{:S(2)}) copy-start(f32[32,2,2,128]{3,2,1,0:T(2,128)} %param.19) | copy-start | bytes 196612
  6.9 4.6 %copy-start.5 = (f32[32,2,2,128]{3,2,1,0:T(2,128)S(1)}, f32[32,2,2,128]{3,2,1,0:T(2,128)}, u32[]{:S(2)}) copy-start(f32[32,2,2,128]{3,2,1,0:T(2,128)} %param.20) | copy-start | bytes 196612
  7.0 4.6 %copy-start.6 = (f32[32,2,2,128]{3,2,1,0:T(2,128)S(1)}, f32[32,2,2,128]{3,2,1,0:T(2,128)}, u32[]{:S(2)}) copy-start(f32[32,2,2,128]{3,2,1,0:T(2,128)} %param.23) | copy-start | bytes 196612
  10.2 3.6 %collective-permute-start.3 = (f32[256,128]{1,0:T(8,128)S(1)}, f32[256,128]{1,0:T(8,128)S(1)}, u32[]{:S(2)}, u32[]{:S(2)}) collective-permute-start(f32[256,128]{1,0:T(8,128)S(1)} %value_over_ill.1), channel_id=1, source_target_pairs={{0,56},{8,0},{16,8},{24,16},{32,24},{40,32},{48,40},{56,48},{1,57}... | collective-permute-start | bytes 393224 | tf_op jit(solution)/shard_map/value_over_ill/ppermute | solution.py:279
  14.8 7.1 %collective-permute-start.4 = (f32[128,128]{1,0:T(8,128)S(1)}, f32[128,128]{1,0:T(8,128)S(1)}, u32[]{:S(2)}, u32[]{:S(2)}) collective-permute-start(f32[128,128]{1,0:T(8,128)S(1)} %get-tuple-element.19), channel_id=1, source_target_pairs={{0,192},{64,0},{128,64},{192,128},{1,193},{65,1},{129,65},{193,129... | collective-permute-start | bytes 196616 | tf_op jit(solution)/shard_map/mass_over_liq/ppermute | solution.py:274
  16.0 5.9 %collective-permute-start.5 = (f32[128,128]{1,0:T(8,128)S(1)}, f32[128,128]{1,0:T(8,128)S(1)}, u32[]{:S(2)}, u32[]{:S(2)}) collective-permute-start(f32[128,128]{1,0:T(8,128)S(1)} %get-tuple-element.20), channel_id=1, source_target_pairs={{0,128},{64,192},{128,0},{192,64},{1,129},{65,193},{129,1},{193,65... | collective-permute-start | bytes 196616 | tf_op jit(solution)/shard_map/mass_over_liq/ppermute | solution.py:274
  17.6 5.6 %collective-permute-start.6 = (f32[128,128]{1,0:T(8,128)S(1)}, f32[128,128]{1,0:T(8,128)S(1)}, u32[]{:S(2)}, u32[]{:S(2)}) collective-permute-start(f32[128,128]{1,0:T(8,128)S(1)} %get-tuple-element.21), channel_id=1, source_target_pairs={{0,64},{64,128},{128,192},{192,0},{1,65},{65,129},{129,193},{193,1... | collective-permute-start | bytes 196616 | tf_op jit(solution)/shard_map/mass_over_liq/ppermute | solution.py:274
  18.1 3.8 %collective-permute-start.7 = (f32[64,128]{1,0:T(8,128)S(1)}, f32[64,128]{1,0:T(8,128)S(1)}, u32[]{:S(2)}, u32[]{:S(2)}) collective-permute-start(f32[64,128]{1,0:T(8,128)S(1)} %get-tuple-element.22.lower_ref), channel_id=1, source_target_pairs={{0,56},{8,0},{16,8},{24,16},{32,24},{40,32},{48,40},{56,48},{1,57}... | collective-permute-start | bytes 98312 | tf_op jit(solution)/shard_map/expected_over_ill/ppermute | solution.py:279
  23.2 1.3 %collective-permute-start.11 = (f32[136,128]{1,0:T(8,128)S(1)}, f32[136,128]{1,0:T(8,128)S(1)}, u32[]{:S(2)}, u32[]{:S(2)}) collective-permute-start(f32[136,128]{1,0:T(8,128)S(1)} %get-tuple-element.25.own_ref), channel_id=1, source_target_pairs={{0,8},{8,0},{16,24},{24,16},{32,40},{40,32},{48,56},{56,48},{1,9},... | collective-permute-start | bytes 208904 | tf_op jit(solution)/shard_map/mass_over_core/ppermute | solution.py:337
  23.3 12.9 %collective-permute-start.10 = (f32[192,128]{1,0:T(8,128)S(1)}, f32[192,128]{1,0:T(8,128)S(1)}, u32[]{:S(2)}, u32[]{:S(2)}) collective-permute-start(f32[192,128]{1,0:T(8,128)S(1)} %get-tuple-element.24.e0), channel_id=1, source_target_pairs={{0,64},{64,128},{128,192},{192,0},{1,65},{65,129},{129,193},{193,1... | collective-permute-start | bytes 294920 | tf_op jit(solution)/shard_map/expected_over_liq/ppermute | solution.py:274
  24.5 7.6 %collective-permute-start.12 = (f32[144,128]{1,0:T(8,128)S(1)}, f32[144,128]{1,0:T(8,128)S(1)}, u32[]{:S(2)}, u32[]{:S(2)}) collective-permute-start(f32[144,128]{1,0:T(8,128)S(1)} %leave.1), channel_id=1, source_target_pairs={{1,0},{2,1},{3,2},{4,3},{5,4},{6,5},{7,6},{9,8},{10,9},{11,10},{12... | collective-permute-start | bytes 221192 | tf_op jit(solution)/shard_map/mass_over_dur/ppermute | solution.py:341
  26.5 11.0 %collective-permute-start.8 = (f32[192,128]{1,0:T(8,128)S(1)}, f32[192,128]{1,0:T(8,128)S(1)}, u32[]{:S(2)}, u32[]{:S(2)}) collective-permute-start(f32[192,128]{1,0:T(8,128)S(1)} %get-tuple-element.24.e0), channel_id=1, source_target_pairs={{0,128},{64,192},{128,0},{192,64},{1,129},{65,193},{129,1},{193,65... | collective-permute-start | bytes 294920 | tf_op jit(solution)/shard_map/expected_over_liq/ppermute | solution.py:274
  28.5 9.1 %collective-permute-start.9 = (f32[192,128]{1,0:T(8,128)S(1)}, f32[192,128]{1,0:T(8,128)S(1)}, u32[]{:S(2)}, u32[]{:S(2)}) collective-permute-start(f32[192,128]{1,0:T(8,128)S(1)} %get-tuple-element.24.e0), channel_id=1, source_target_pairs={{0,192},{64,0},{128,64},{192,128},{1,193},{65,1},{129,65},{193,129... | collective-permute-start | bytes 294920 | tf_op jit(solution)/shard_map/expected_over_liq/ppermute | solution.py:274
  32.4 6.2 %collective-permute-start.13 = (f32[128,128]{1,0:T(8,128)S(1)}, f32[128,128]{1,0:T(8,128)S(1)}, u32[]{:S(2)}, u32[]{:S(2)}) collective-permute-start(f32[128,128]{1,0:T(8,128)S(1)} %get-tuple-element.27), channel_id=1, source_target_pairs={{0,16},{8,24},{16,32},{24,40},{32,48},{40,56},{48,0},{56,8},{1,17}... | collective-permute-start | bytes 196616 | tf_op jit(solution)/shard_map/mass_over_ill/ppermute | solution.py:347
  33.2 5.9 %collective-permute-start.14 = (f32[128,128]{1,0:T(8,128)S(1)}, f32[128,128]{1,0:T(8,128)S(1)}, u32[]{:S(2)}, u32[]{:S(2)}) collective-permute-start(f32[128,128]{1,0:T(8,128)S(1)} %get-tuple-element.28), channel_id=1, source_target_pairs={{0,32},{8,40},{16,48},{24,56},{32,0},{40,8},{48,16},{56,24},{1,33}... | collective-permute-start | bytes 196616 | tf_op jit(solution)/shard_map/mass_over_ill/ppermute | solution.py:347
  36.2 4.3 %collective-permute-start.15 = (f32[128,128]{1,0:T(8,128)S(1)}, f32[128,128]{1,0:T(8,128)S(1)}, u32[]{:S(2)}, u32[]{:S(2)}) collective-permute-start(f32[128,128]{1,0:T(8,128)S(1)} %get-tuple-element.29), channel_id=1, source_target_pairs={{0,48},{8,56},{16,0},{24,8},{32,16},{40,24},{48,32},{56,40},{1,49}... | collective-permute-start | bytes 196616 | tf_op jit(solution)/shard_map/mass_over_ill/ppermute | solution.py:347
